TPU v7x, 32 devices: a whole 2x2x4 slice. The times are simulated.
32 devices in a mesh: ctx: 8 (over z, y), ws: 4 (over x, core).
Axes of the slice: x: 2, y: 2, z: 4, core: 2. Of those that a mesh axis runs over, the one named last changes fastest.
Arguments:
- inputs: bfloat16 [2, 4096, 1152], P(None, ('ctx', 'ws')), may hold values from -6 to 6
- attn_gain: bfloat16 [1152], P(('ctx', 'ws')), may hold values from 0.25 to 1.75
- query_weight: bfloat16 [1152, 1152], P(('ctx', 'ws')), may hold values from -0.1875 to 0.1875
- key_matrix: bfloat16 [1152, 384], P(('ctx', 'ws')), may hold values from -0.1875 to 0.1875
- value_matrix: bfloat16 [1152, 384], P(('ctx', 'ws')), may hold values from -0.1875 to 0.1875
- out_weight: bfloat16 [1152, 1152], P(('ctx', 'ws')), may hold values from -3.5 to 3.5
- ffn_gain: bfloat16 [1152], P(('ctx', 'ws')), may hold values from 0.25 to 1.75
- gate_weight: bfloat16 [1152, 3072], P(('ctx', 'ws')), may hold values from -0.1875 to 0.1875
- up_weight: bfloat16 [1152, 3072], P(('ctx', 'ws')), may hold values from -0.1875 to 0.1875
- down_weight: bfloat16 [3072, 1152], P(('ctx', 'ws')), may hold values from -0.109375 to 0.109375
- cotangent: bfloat16 [2, 4096, 1152], P(None, ('ctx', 'ws')), may hold values from -6 to 6
Outputs:
- layer_out: bfloat16 [2, 4096, 1152], P(None, ('ctx', 'ws'))
- input_grad: bfloat16 [2, 4096, 1152], P(None, ('ctx', 'ws'))
- attn_gain_grad: float32 [1152], P(('ctx', 'ws'))
- query_grad: float32 [1152, 1152], P(('ctx', 'ws'))
- key_grad: float32 [1152, 384], P(('ctx', 'ws'))
- value_grad: float32 [1152, 384], P(('ctx', 'ws'))
- out_grad: float32 [1152, 1152], P(('ctx', 'ws'))
- ffn_gain_grad: float32 [1152], P(('ctx', 'ws'))
- gate_grad: float32 [1152, 3072], P(('ctx', 'ws'))
- up_grad: float32 [1152, 3072], P(('ctx', 'ws'))
- down_grad: float32 [3072, 1152], P(('ctx', 'ws'))
All inputs are finite; a program needn't handle non-finite values.
Results may differ from a plain program's by a relative error of at most 0.02.
Values may be sent and summed in bfloat16 or wider, within the bound.
A program may use at most 256 MiB of HBM per device.

v0:
```python
import jax
import jax.numpy as jnp
from jax import lax
from jax.sharding import PartitionSpec as P

QUERY_HEADS = 18
KEY_VALUE_HEADS = 6
HEAD_SIZE = 64


EPSILON = 1e-05
MASKED_SCORE = -1e30


def shifted(block, axis, distance):
    devices = range(lax.axis_size(axis))
    route = [((i - distance) % len(devices), i) for i in devices]
    return lax.ppermute(block, axis, route)


def as_sent(x):

    def short(part):
        return part.astype(jnp.bfloat16) if part.dtype == jnp.float32 else part

    return jax.tree.map(short, x)


def matrix_multiply(left, right):
    return jnp.dot(left, right, preferred_element_type=jnp.float32)


def outer_sum(left, right):
    return jnp.einsum("ri,rj->ij", left, right, preferred_element_type=jnp.float32)


def back_product(gradient, weight):
    return jnp.einsum("rj,ij->ri", gradient, weight, preferred_element_type=jnp.float32)


def normalize(layer_rows, gain_vector):
    inverse = lax.rsqrt(jnp.mean(layer_rows * layer_rows, axis=-1, keepdims=True) + EPSILON)
    return (layer_rows * inverse * gain_vector, inverse)


def normalize_back(layer_rows, inverse, gain_vector, gradient):
    weighted = gradient * gain_vector
    inner_mean = jnp.mean(weighted * layer_rows, axis=-1, keepdims=True)
    row_grad = inverse * weighted - layer_rows * (inverse * inverse * inverse) * inner_mean
    gain_grad = jnp.sum(gradient * layer_rows * inverse, axis=0)
    return (row_grad, gain_grad)


def rotary_tables(token_positions):
    quarter = HEAD_SIZE // 2
    frequency = 10000.0 ** (-2.0 * jnp.arange(quarter, dtype=jnp.float32) / HEAD_SIZE)
    angles = token_positions.astype(jnp.float32)[:, None] * frequency[None, :]
    return (jnp.cos(angles)[:, None, :], jnp.sin(angles)[:, None, :])


def rotate(heads, cosine_table, sine_table):
    quarter = HEAD_SIZE // 2
    first_half = heads[..., :quarter]
    second_half = heads[..., quarter:]
    return jnp.concatenate(
        [
            first_half * cosine_table - second_half * sine_table,
            second_half * cosine_table + first_half * sine_table,
        ],
        axis=-1,
    )


def rotate_back(heads, cosine_table, sine_table):
    quarter = HEAD_SIZE // 2
    first_half = heads[..., :quarter]
    second_half = heads[..., quarter:]
    return jnp.concatenate(
        [
            first_half * cosine_table + second_half * sine_table,
            second_half * cosine_table - first_half * sine_table,
        ],
        axis=-1,
    )


def query_places(own_ctx, own_member, count_of_rows, ctx_count, device_count):
    rows_per_half = count_of_rows // 2
    local_index = jnp.arange(count_of_rows, dtype=jnp.int32)
    span_index = jnp.where(local_index < rows_per_half, own_ctx, 2 * ctx_count - 1 - own_ctx)
    return (
        span_index * (device_count * rows_per_half)
        + own_member * rows_per_half
        + local_index % rows_per_half
    )


def block_places(source_ctx, count_of_rows, ctx_count, device_count):
    rows_per_half = count_of_rows // 2
    member_index = jnp.arange(device_count, dtype=jnp.int32)[:, None, None]
    half_index = jnp.arange(2, dtype=jnp.int32)[None, :, None]
    inner_index = jnp.arange(rows_per_half, dtype=jnp.int32)[None, None, :]
    span_index = jnp.where(half_index == 0, source_ctx, 2 * ctx_count - 1 - source_ctx)
    return (
        span_index * (device_count * rows_per_half) + member_index * rows_per_half + inner_index
    ).reshape(-1)


def split_block(block_of_keys):
    hidden_width = KEY_VALUE_HEADS * HEAD_SIZE
    device_count, _, rows_per_half, _ = block_of_keys.shape
    rows_of_keys = block_of_keys[..., :hidden_width].reshape(
        device_count, 2, rows_per_half, KEY_VALUE_HEADS, HEAD_SIZE
    )
    rows_of_values = block_of_keys[..., hidden_width:].reshape(
        device_count, 2, rows_per_half, KEY_VALUE_HEADS, HEAD_SIZE
    )
    return (rows_of_keys, rows_of_values)


def attend(query_rows, rows_of_keys, rows_of_values, causal_visible):
    scores = jnp.einsum(
        "rgjd,kgd->grjk", query_rows, rows_of_keys, preferred_element_type=jnp.float32
    ) * HEAD_SIZE ** (-0.5)
    if causal_visible is not None:
        scores = jnp.where(causal_visible[None, :, None, :], scores, MASKED_SCORE)
    row_max = jnp.max(scores, axis=-1)
    exponentials = jnp.exp(scores - row_max[..., None])
    row_total = jnp.sum(exponentials, axis=-1)
    mixture = jnp.einsum(
        "grjk,kgd->rgjd",
        exponentials.astype(jnp.bfloat16),
        rows_of_values,
        preferred_element_type=jnp.float32,
    )
    return (jnp.transpose(row_max, (1, 0, 2)), jnp.transpose(row_total, (1, 0, 2)), mixture)


def empty_part(count_of_rows):
    queries_per_group = QUERY_HEADS // KEY_VALUE_HEADS
    return (
        jnp.full((count_of_rows, KEY_VALUE_HEADS, queries_per_group), MASKED_SCORE, jnp.float32),
        jnp.zeros((count_of_rows, KEY_VALUE_HEADS, queries_per_group), jnp.float32),
        jnp.zeros((count_of_rows, KEY_VALUE_HEADS, queries_per_group, HEAD_SIZE), jnp.float32),
    )


def combine(carried, incoming):
    carried_max, carried_total, carried_mix = carried
    incoming_max, incoming_total, incoming_mix = incoming
    new_max = jnp.maximum(carried_max, incoming_max)
    carried_scale = jnp.exp(carried_max - new_max)
    incoming_scale = jnp.exp(incoming_max - new_max)
    return (
        new_max,
        carried_total * carried_scale + incoming_total * incoming_scale,
        carried_mix * carried_scale[..., None] + incoming_mix * incoming_scale[..., None],
    )


def forward_block(carried, block_of_keys, source_ctx, own_ctx, query_rows, own_places, ctx_count):
    rows_of_keys, rows_of_values = split_block(block_of_keys)
    device_count, _, rows_per_half, _ = block_of_keys.shape

    def forward_earlier():
        return attend(
            query_rows,
            rows_of_keys[:, 0].reshape(-1, KEY_VALUE_HEADS, HEAD_SIZE),
            rows_of_values[:, 0].reshape(-1, KEY_VALUE_HEADS, HEAD_SIZE),
            None,
        )

    def forward_later():
        late_part = attend(
            query_rows[rows_per_half:],
            rows_of_keys.reshape(-1, KEY_VALUE_HEADS, HEAD_SIZE),
            rows_of_values.reshape(-1, KEY_VALUE_HEADS, HEAD_SIZE),
            None,
        )
        early_part = empty_part(rows_per_half)
        return tuple(
            (
                jnp.concatenate([early_piece, late_piece], axis=0)
                for early_piece, late_piece in zip(early_part, late_part)
            )
        )

    def forward_diagonal():
        key_places = block_places(source_ctx, 2 * rows_per_half, ctx_count, device_count)
        causal_visible = own_places[:, None] >= key_places[None, :]
        return attend(
            query_rows,
            rows_of_keys.reshape(-1, KEY_VALUE_HEADS, HEAD_SIZE),
            rows_of_values.reshape(-1, KEY_VALUE_HEADS, HEAD_SIZE),
            causal_visible,
        )

    branch_index = jnp.where(source_ctx == own_ctx, 2, jnp.where(source_ctx > own_ctx, 1, 0))
    return combine(
        carried, lax.switch(branch_index, [forward_earlier, forward_later, forward_diagonal])
    )


def attend_back(
    query_rows, attended_grad, log_total, delta_rows, rows_of_keys, rows_of_values, causal_visible
):
    scores = jnp.einsum(
        "rgjd,kgd->grjk", query_rows, rows_of_keys, preferred_element_type=jnp.float32
    ) * HEAD_SIZE ** (-0.5)
    if causal_visible is not None:
        scores = jnp.where(causal_visible[None, :, None, :], scores, MASKED_SCORE)
    probabilities = jnp.exp(scores - jnp.transpose(log_total, (1, 0, 2))[..., None])
    prob_grad = jnp.einsum(
        "rgjd,kgd->grjk", attended_grad, rows_of_values, preferred_element_type=jnp.float32
    )
    score_grad = (
        probabilities * (prob_grad - jnp.transpose(delta_rows, (1, 0, 2))[..., None])
    ).astype(jnp.bfloat16)
    query_part = jnp.einsum(
        "grjk,kgd->rgjd", score_grad, rows_of_keys, preferred_element_type=jnp.float32
    ) * HEAD_SIZE ** (-0.5)
    key_part = jnp.einsum(
        "grjk,rgjd->kgd", score_grad, query_rows, preferred_element_type=jnp.float32
    ) * HEAD_SIZE ** (-0.5)
    value_part = jnp.einsum(
        "grjk,rgjd->kgd",
        probabilities.astype(jnp.bfloat16),
        attended_grad,
        preferred_element_type=jnp.float32,
    )
    return (query_part, key_part, value_part)


def backward_block(
    block_of_keys,
    source_ctx,
    own_ctx,
    query_rows,
    attended_grad,
    log_total,
    delta_rows,
    own_places,
    ctx_count,
):
    rows_of_keys, rows_of_values = split_block(block_of_keys)
    device_count, _, rows_per_half, _ = block_of_keys.shape
    hidden_width = KEY_VALUE_HEADS * HEAD_SIZE

    def backward_earlier():
        query_part, key_part, value_part = attend_back(
            query_rows,
            attended_grad,
            log_total,
            delta_rows,
            rows_of_keys[:, 0].reshape(-1, KEY_VALUE_HEADS, HEAD_SIZE),
            rows_of_values[:, 0].reshape(-1, KEY_VALUE_HEADS, HEAD_SIZE),
            None,
        )
        early_grad = jnp.concatenate(
            [
                key_part.reshape(device_count, 1, rows_per_half, hidden_width),
                value_part.reshape(device_count, 1, rows_per_half, hidden_width),
            ],
            axis=-1,
        )
        return (query_part, jnp.concatenate([early_grad, jnp.zeros_like(early_grad)], axis=1))

    def backward_later():
        query_part, key_part, value_part = attend_back(
            query_rows[rows_per_half:],
            attended_grad[rows_per_half:],
            log_total[rows_per_half:],
            delta_rows[rows_per_half:],
            rows_of_keys.reshape(-1, KEY_VALUE_HEADS, HEAD_SIZE),
            rows_of_values.reshape(-1, KEY_VALUE_HEADS, HEAD_SIZE),
            None,
        )
        query_part = jnp.concatenate([jnp.zeros_like(query_part), query_part], axis=0)
        return (
            query_part,
            jnp.concatenate(
                [
                    key_part.reshape(device_count, 2, rows_per_half, hidden_width),
                    value_part.reshape(device_count, 2, rows_per_half, hidden_width),
                ],
                axis=-1,
            ),
        )

    def backward_diagonal():
        key_places = block_places(source_ctx, 2 * rows_per_half, ctx_count, device_count)
        causal_visible = own_places[:, None] >= key_places[None, :]
        query_part, key_part, value_part = attend_back(
            query_rows,
            attended_grad,
            log_total,
            delta_rows,
            rows_of_keys.reshape(-1, KEY_VALUE_HEADS, HEAD_SIZE),
            rows_of_values.reshape(-1, KEY_VALUE_HEADS, HEAD_SIZE),
            causal_visible,
        )
        return (
            query_part,
            jnp.concatenate(
                [
                    key_part.reshape(device_count, 2, rows_per_half, hidden_width),
                    value_part.reshape(device_count, 2, rows_per_half, hidden_width),
                ],
                axis=-1,
            ),
        )

    branch_index = jnp.where(source_ctx == own_ctx, 2, jnp.where(source_ctx > own_ctx, 1, 0))
    return lax.switch(branch_index, [backward_earlier, backward_later, backward_diagonal])


def per_device(
    inputs,
    attn_gain,
    query_weight,
    key_matrix,
    value_matrix,
    out_weight,
    ffn_gain,
    gate_weight,
    up_weight,
    down_weight,
    cotangent,
):
    ctx_count = lax.axis_size("ctx")
    device_count = lax.axis_size("ws")
    own_ctx = lax.axis_index("ctx")
    own_member = lax.axis_index("ws")
    micro_count, count_of_rows, _ = inputs.shape
    rows_per_half = count_of_rows // 2
    queries_per_group = QUERY_HEADS // KEY_VALUE_HEADS
    hidden_width = KEY_VALUE_HEADS * HEAD_SIZE
    own_places = query_places(own_ctx, own_member, count_of_rows, ctx_count, device_count)
    cosine_table, sine_table = rotary_tables(own_places)
    grad_sums = None
    layer_outs = []
    input_grads = []
    for micro_batch in range(micro_count):
        gathered = (
            lax.all_gather(attn_gain, ("ctx", "ws"), axis=0, tiled=True),
            lax.all_gather(query_weight, ("ctx", "ws"), axis=0, tiled=True),
            lax.all_gather(key_matrix, ("ctx", "ws"), axis=0, tiled=True),
            lax.all_gather(value_matrix, ("ctx", "ws"), axis=0, tiled=True),
            lax.all_gather(out_weight, ("ctx", "ws"), axis=0, tiled=True),
            lax.all_gather(ffn_gain, ("ctx", "ws"), axis=0, tiled=True),
            lax.all_gather(gate_weight, ("ctx", "ws"), axis=0, tiled=True),
            lax.all_gather(up_weight, ("ctx", "ws"), axis=0, tiled=True),
            lax.all_gather(down_weight, ("ctx", "ws"), axis=0, tiled=True),
        )
        (
            full_attn_gain,
            full_query,
            complete_key,
            full_value,
            full_out,
            full_ffn_gain,
            full_gate,
            full_up,
            full_down,
        ) = gathered
        first_gain = full_attn_gain.astype(jnp.float32)
        second_gain = full_ffn_gain.astype(jnp.float32)
        layer_rows = inputs[micro_batch].astype(jnp.float32)
        normalized_rows, first_inverse = normalize(layer_rows, first_gain)
        normalized_reduced = normalized_rows.astype(jnp.bfloat16)
        query_rows = rotate(
            matrix_multiply(normalized_reduced, full_query).reshape(
                count_of_rows, QUERY_HEADS, HEAD_SIZE
            ),
            cosine_table,
            sine_table,
        )
        query_rows = query_rows.astype(jnp.bfloat16).reshape(
            count_of_rows, KEY_VALUE_HEADS, queries_per_group, HEAD_SIZE
        )
        rows_of_keys = rotate(
            matrix_multiply(normalized_reduced, complete_key).reshape(
                count_of_rows, KEY_VALUE_HEADS, HEAD_SIZE
            ),
            cosine_table,
            sine_table,
        ).astype(jnp.bfloat16)
        rows_of_values = matrix_multiply(normalized_reduced, full_value).astype(jnp.bfloat16)
        local_block = jnp.concatenate(
            [rows_of_keys.reshape(count_of_rows, hidden_width), rows_of_values], axis=-1
        )
        group_block = lax.all_gather(local_block, "ws", axis=0, tiled=True).reshape(
            device_count, 2, rows_per_half, 2 * hidden_width
        )

        def fold_step(carried, shard_piece):

            def visit_block(state_now, block_entry):
                block_of_keys, source_ctx = block_entry
                return (
                    forward_block(
                        state_now,
                        block_of_keys,
                        source_ctx,
                        own_ctx,
                        query_rows,
                        own_places,
                        ctx_count,
                    ),
                    None,
                )

            source_list = jnp.arange(shard_piece.shape[0], dtype=jnp.int32)
            result_state, _ = lax.scan(visit_block, carried, (shard_piece, source_list))
            return result_state

        row_max, row_total, mixture = fold_step(
            empty_part(count_of_rows), lax.all_gather(group_block[None], "ctx", axis=0, tiled=True)
        )
        attended = mixture / row_total[..., None]
        log_total = row_max + jnp.log(row_total)
        attended_low = attended.astype(jnp.bfloat16).reshape(count_of_rows, QUERY_HEADS * HEAD_SIZE)
        middle = layer_rows + matrix_multiply(attended_low, full_out)
        hidden, second_inverse = normalize(middle, second_gain)
        hidden_low = hidden.astype(jnp.bfloat16)
        gate_rows = matrix_multiply(hidden_low, full_gate)
        up_rows = matrix_multiply(hidden_low, full_up)
        sigmoid_gate = jax.nn.sigmoid(gate_rows)
        silu_gate = gate_rows * sigmoid_gate
        activated = (silu_gate * up_rows).astype(jnp.bfloat16)
        layer_outs.append((middle + matrix_multiply(activated, full_down)).astype(jnp.bfloat16))
        upstream_low = cotangent[micro_batch]
        upstream = upstream_low.astype(jnp.float32)
        down_sum = outer_sum(activated, upstream_low)
        act_grad = back_product(upstream_low, full_down)
        gate_low = (
            act_grad * up_rows * sigmoid_gate * (1.0 + gate_rows * (1.0 - sigmoid_gate))
        ).astype(jnp.bfloat16)
        up_low = (act_grad * silu_gate).astype(jnp.bfloat16)
        gate_sum = outer_sum(hidden_low, gate_low)
        up_sum = outer_sum(hidden_low, up_low)
        hidden_grad = back_product(gate_low, full_gate) + back_product(up_low, full_up)
        middle_part, ffn_gain_sum = normalize_back(middle, second_inverse, second_gain, hidden_grad)
        middle_grad = middle_part + upstream
        branch_low = middle_grad.astype(jnp.bfloat16)
        out_sum = outer_sum(attended_low, branch_low)
        attended_grad = (
            back_product(branch_low, full_out)
            .reshape(count_of_rows, KEY_VALUE_HEADS, queries_per_group, HEAD_SIZE)
            .astype(jnp.bfloat16)
        )
        delta_rows = jnp.sum(attended_grad.astype(jnp.float32) * attended, axis=-1)

        def cycle_step(turn_index, carried):
            block_of_keys, block_grad, query_total = carried
            source_ctx = (own_ctx - turn_index) % ctx_count
            query_part, block_part = backward_block(
                block_of_keys,
                source_ctx,
                own_ctx,
                query_rows,
                attended_grad,
                log_total,
                delta_rows,
                own_places,
                ctx_count,
            )
            block_grad = block_grad + block_part
            next_block = shifted(block_of_keys, "ctx", 1)
            next_grad = shifted(as_sent(block_grad), "ctx", 1).astype(block_grad.dtype)
            return (next_block, next_grad, query_total + query_part)

        cycle_start = (
            group_block,
            jnp.zeros(group_block.shape, jnp.float32),
            jnp.zeros((count_of_rows, KEY_VALUE_HEADS, queries_per_group, HEAD_SIZE), jnp.float32),
        )
        _, block_grad, query_total = lax.fori_loop(0, ctx_count, cycle_step, cycle_start)
        local_gradient = (
            lax.psum_scatter(block_grad.astype(jnp.bfloat16), "ws", scatter_dimension=0, tiled=True)
            .astype(jnp.float32)
            .reshape(count_of_rows, 2 * hidden_width)
        )
        key_low = rotate_back(
            local_gradient[:, :hidden_width].reshape(count_of_rows, KEY_VALUE_HEADS, HEAD_SIZE),
            cosine_table,
            sine_table,
        )
        key_low = key_low.astype(jnp.bfloat16).reshape(count_of_rows, hidden_width)
        value_low = local_gradient[:, hidden_width:].astype(jnp.bfloat16)
        query_low = rotate_back(
            query_total.reshape(count_of_rows, QUERY_HEADS, HEAD_SIZE), cosine_table, sine_table
        )
        query_low = query_low.astype(jnp.bfloat16).reshape(count_of_rows, QUERY_HEADS * HEAD_SIZE)
        query_sum = outer_sum(normalized_reduced, query_low)
        key_sum = outer_sum(normalized_reduced, key_low)
        value_sum = outer_sum(normalized_reduced, value_low)
        normed_grad = (
            back_product(query_low, full_query)
            + back_product(key_low, complete_key)
            + back_product(value_low, full_value)
        )
        input_part, attn_gain_sum = normalize_back(
            layer_rows, first_inverse, first_gain, normed_grad
        )
        input_grads.append((middle_grad + input_part).astype(jnp.bfloat16))
        batch_terms = (
            attn_gain_sum,
            query_sum,
            key_sum,
            value_sum,
            out_sum,
            ffn_gain_sum,
            gate_sum,
            up_sum,
            down_sum,
        )
        if grad_sums is None:
            grad_sums = batch_terms
        else:
            grad_sums = tuple(
                (
                    earlier_sum + batch_term
                    for earlier_sum, batch_term in zip(grad_sums, batch_terms)
                )
            )
    owned_grads = (
        lax.psum_scatter(grad_sums[0], ("ctx", "ws"), scatter_dimension=0, tiled=True),
        lax.psum_scatter(grad_sums[1], ("ctx", "ws"), scatter_dimension=0, tiled=True),
        lax.psum_scatter(grad_sums[2], ("ctx", "ws"), scatter_dimension=0, tiled=True),
        lax.psum_scatter(grad_sums[3], ("ctx", "ws"), scatter_dimension=0, tiled=True),
        lax.psum_scatter(grad_sums[4], ("ctx", "ws"), scatter_dimension=0, tiled=True),
        lax.psum_scatter(grad_sums[5], ("ctx", "ws"), scatter_dimension=0, tiled=True),
        lax.psum_scatter(grad_sums[6], ("ctx", "ws"), scatter_dimension=0, tiled=True),
        lax.psum_scatter(grad_sums[7], ("ctx", "ws"), scatter_dimension=0, tiled=True),
        lax.psum_scatter(grad_sums[8], ("ctx", "ws"), scatter_dimension=0, tiled=True),
    )
    return (
        jnp.stack(layer_outs),
        jnp.stack(input_grads),
        owned_grads[0],
        owned_grads[1],
        owned_grads[2],
        owned_grads[3],
        owned_grads[4],
        owned_grads[5],
        owned_grads[6],
        owned_grads[7],
        owned_grads[8],
    )


def solution(mesh):
    in_specs = (
        P(None, ("ctx", "ws"), None),
        P(("ctx", "ws")),
        P(("ctx", "ws"), None),
        P(("ctx", "ws"), None),
        P(("ctx", "ws"), None),
        P(("ctx", "ws"), None),
        P(("ctx", "ws")),
        P(("ctx", "ws"), None),
        P(("ctx", "ws"), None),
        P(("ctx", "ws"), None),
        P(None, ("ctx", "ws"), None),
    )
    out_specs = (
        P(None, ("ctx", "ws"), None),
        P(None, ("ctx", "ws"), None),
        P(("ctx", "ws")),
        P(("ctx", "ws"), None),
        P(("ctx", "ws"), None),
        P(("ctx", "ws"), None),
        P(("ctx", "ws"), None),
        P(("ctx", "ws")),
        P(("ctx", "ws"), None),
        P(("ctx", "ws"), None),
        P(("ctx", "ws"), None),
    )
    return jax.shard_map(
        per_device, mesh=mesh, in_specs=in_specs, out_specs=out_specs, check_vma=False
    )
```

profile of v0, /device:TPU:0, one launch (start us, length us, event | category | flops | bytes accessed | tf_op | source)
XLA Modules:
  0.0 2636.0 jit_solution(17148787788336654309)
XLA Ops:
  8.7 47.6 %all-gather.1 = bf16[32,36,384]{2,1,0:T(8,128)(2,1)S(1)} all-gather(bf16[1,36,384]{2,1,0:T(8,128)(2,1)} %bitcast.680), channel_id=1, replica_groups=mesh['ctx'=8,'ws'=4] {'ctx','ws'}, dimensions={0}, use_global_device_ids=true | all-gather | bytes 912384 | tf_op jit(solution)/shard_map/all_gather | solution.py:348
  58.0 37.1 %all-reduce.27 = (bf16[1152]{0:T(1024)(128)(2,1)S(1)}, bf16[1152]{0:T(1024)(128)(2,1)S(1)}) all-reduce(bf16[1152]{0:T(1024)(128)(2,1)S(1)} %dynamic-update-slice, bf16[1152]{0:T(1024)(128)(2,1)S(1)} %dynamic-update-slice.1), channel_id=1, replica_groups=mesh['ctx'=8,'ws'=4] {'ctx','ws'}, use_global_device_ids=true, to_apply=%add.10 | all-reduce | flops 2304 | bytes 9216
  95.0 44.1 %all-gather = bf16[32,36,384]{2,1,0:T(8,128)(2,1)S(1)} all-gather(bf16[1,36,384]{2,1,0:T(8,128)(2,1)S(1)} %bitcast.681), channel_id=1, replica_groups=mesh['ctx'=8,'ws'=4] {'ctx','ws'}, dimensions={0}, use_global_device_ids=true | all-gather | bytes 912384 | tf_op jit(solution)/shard_map/all_gather | solution.py:347
  181.1 66.3 %all-gather.14.cloned.1.call-done = bf16[8,4,2,64,768]{4,3,2,1,0:T(8,128)(2,1)} async-done(((bf16[1,4,2,64,768]{4,3,2,1,0:T(8,128)(2,1)}), bf16[8,4,2,64,768]{4,3,2,1,0:T(8,128)(2,1)}) %all-gather.14.cloned.1.call-update) | async-done | bytes 6291472 | tf_op jit(solution)/shard_map/all_gather | solution.py:418
  248.0 179.9 %while.78 = (s32[]{:T(128)}, f32[128,6,3]{0,2,1:T(4,128)}, f32[128,6,3]{0,2,1:T(4,128)}, f32[128,6,3,64]{0,3,2,1:T(8,128)}, s32[8]{0:T(128)}, /*index=5*/s32[]{:...) while((s32[]{:T(128)}, f32[128,6,3]{0,2,1:T(4,128)}, ...), condition=%wide.region_11.12_spmd.clone.clone.clone, body=%wide.region_1.11_spmd.clone.clone.clone.sunk | while | flops 315637120 | bytes 44741736 | solution.py:414
  256.9 12.7 conditional.20
  434.1 183.7 %while.79 = (s32[]{:T(128)}, f32[128,6,3]{0,2,1:T(4,128)}, f32[128,6,3]{0,2,1:T(4,128)}, f32[128,6,3,64]{0,3,2,1:T(8,128)}, s32[8]{0:T(128)}, /*index=5*/s32[]{:...) while((s32[]{:T(128)}, f32[128,6,3]{0,2,1:T(4,128)}, ...), condition=%wide.region_24.25_spmd.clone.clone.clone, body=%wide.region_14.0_spmd.clone.clone.clone.sunk | while | flops 315637120 | bytes 44741736 | solution.py:414
  443.5 12.9 conditional.21
  697.9 549.9 %while.80 = (s32[]{:T(128)}, bf16[4,2,64,768]{3,2,1,0:T(8,128)(2,1)}, f32[4,2,64,768]{3,2,1,0:T(8,128)}, f32[128,6,3,64]{0,3,2,1:T(8,128)}, s32[]{:T(128)}, /*in...) while((s32[]{:T(128)}, ...), condition=%wide.region_32.33_spmd.clone.clone.clone, body=%wide.region_28.32_spmd.clone.clone.clone.sunk | while | flops 769443712 | bytes 90286584 | solution.py:478
  702.5 26.4 %conditional.22 = (f32[128,6,3,64]{0,3,2,1:T(8,128)}, f32[4,2,64,768]{3,2,1,0:T(8,128)}) conditional(s32[]{:T(128)} %clamp.44, (bf16[4,2,64,384]{2,1,0,3:T(2,128)(2,1)S(1)}, bf16[128,6,3,64]{0,3,2,1:T(8,128)(2,1)S(1)}, f32[128,6,3]{0,2,1:T(4,128)S(1)}, bf16[4,2,64,384]{2,1,0,3:T(2,128)(2,1)S(1)}, ...), branch_computations={%region_29.29_spmd, %region_30.30_spmd, %region_31.31_spmd.clone} | conditional | flops 767575808 | bytes 57056984 | solution.py:314
  732.1 21.9 collective-permute-done.1
  774.2 26.2 conditional.22
  804.0 21.9 collective-permute-done.1
  845.3 26.2 conditional.22
  875.1 21.9 collective-permute-done.1
  915.4 26.2 conditional.22
  945.2 21.9 collective-permute-done.1
  984.6 26.2 conditional.22
  1014.4 21.9 collective-permute-done.1
  1052.8 26.2 conditional.22
  1082.7 21.9 collective-permute-done.1
  1120.2 26.2 conditional.22
  1150.0 21.9 collective-permute-done.1
  1186.6 26.2 conditional.22
  1216.5 21.9 collective-permute-done.1
  1250.3 494.4 %while.81 = (s32[]{:T(128)}, bf16[4,2,64,768]{3,2,1,0:T(8,128)(2,1)S(1)}, f32[4,2,64,768]{3,2,1,0:T(8,128)}, f32[128,6,3,64]{0,3,2,1:T(8,128)}, s32[]{:T(128)}, ...) while((s32[]{:T(128)}, ...), condition=%wide.region_41.42_spmd.clone.clone.clone, body=%wide.region_37.41_spmd.clone.clone.clone.sunk | while | flops 769443712 | bytes 87140840 | solution.py:478
  1269.7 26.4 %conditional.23 = (f32[128,6,3,64]{0,3,2,1:T(8,128)}, f32[4,2,64,768]{3,2,1,0:T(8,128)}) conditional(s32[]{:T(128)} %clamp.45, (bf16[4,2,64,384]{2,1,0,3:T(2,128)(2,1)S(1)}, bf16[128,6,3,64]{0,3,2,1:T(8,128)(2,1)S(1)}, f32[128,6,3]{0,2,1:T(4,128)S(1)}, bf16[4,2,64,384]{2,1,0,3:T(2,128)(2,1)S(1)}, ...), branch_computations={%region_38.38_spmd, %region_39.39_spmd, %region_40.40_spmd.clone} | conditional | flops 767575808 | bytes 57056984 | solution.py:314
  1299.2 21.2 collective-permute-done.3
  1332.1 26.2 conditional.23
  1361.9 20.4 collective-permute-done.3
  1393.9 26.2 conditional.23
  1423.7 19.5 collective-permute-done.3
  1454.9 26.2 conditional.23
  1484.7 18.7 collective-permute-done.3
  1515.1 26.2 conditional.23
  1544.9 17.9 collective-permute-done.3
  1574.4 26.2 conditional.23
  1604.2 17.1 collective-permute-done.3
  1633.0 26.2 conditional.23
  1662.8 16.3 collective-permute-done.3
  1690.7 26.2 conditional.23
  1720.5 15.5 collective-permute-done.3
  1786.6 13.8 convolution_add_fusion.2
  1815.0 532.9 %fusion.281 = (f32[48,1152]{1,0:T(8,128)}, f32[48,384]{1,0:T(8,128)}, f32[48,384]{1,0:T(8,128)S(1)}, f32[48,1152]{1,0:T(8,128)S(1)}, f32[40,3072]{1,0:T(8,128)}, /*index=5*/f32[40,3072]{1,0:T(8,128)}) fusion(f32[1152,1152]{1,0:T(8,128)} %convolution_add_fusion.4, f32[1152,384]{1,0:T(8,128)} %convolution_add_fusion.6, ...), kind=kCustom, calls=%all-reduce-scatter.6 | all-reduce-scatter fusion | flops 12582914 | bytes 44040192
  2347.8 31.3 %collective-permute-start.18 = (f32[48,384]{1,0:T(8,128)}, f32[48,384]{1,0:T(8,128)S(1)}, u32[]{:S(2)}, u32[]{:S(2)}) collective-permute-start(f32[48,384]{1,0:T(8,128)} %get-tuple-element.1744), channel_id=1, source_target_pairs={{0,7},{1,8},{2,9},{3,10},{4,11},{5,12},{6,13},{7,14},{8,15},{9,16}... | collective-permute-start | bytes 221192
  2491.8 53.8 %all-reduce.26 = (f32[1152]{0:T(1024)S(1)}, f32[1152]{0:T(1024)S(1)}) all-reduce(f32[1152]{0:T(1024)S(1)} %add.531, f32[1152]{0:T(1024)S(1)} %add.536), channel_id=4, replica_groups=mesh['ctx'=8,'ws'=4] {'ctx','ws'}, use_global_device_ids=true, to_apply=%region_46.47.clone | all-reduce | flops 2304 | bytes 18432
  2583.1 15.0 concatenate.111
  2612.8 13.4 concatenate.113
  (1579 shorter events, 1542.8 us)
Async XLA Ops:
  7.2 157.3 %all-gather.20.cloned.1.call-start = ((), (), s32[]{:S(2)}) async-start(), calls=%async_computation.9 | async-start | bytes 3041280 | tf_op jit(solution)/shard_map/all_gather | solution.py:346
  7.9 168.0 %all-gather.22.cloned.1.call-start = ((), (), s32[]{:S(2)}) async-start(), calls=%async_computation.10 | async-start | bytes 3041280 | tf_op jit(solution)/shard_map/all_gather | solution.py:349
  8.7 238.7 %all-gather.14.cloned.1.call-start = ((), (), s32[]{:S(2)}) async-start(), calls=%async_computation.3 | async-start | bytes 7077888 | tf_op jit(solution)/shard_map/all_gather | solution.py:418
  152.0 281.6 %all-gather.18.cloned.1.call-start = ((), (), s32[]{:S(2)}) async-start(), calls=%async_computation.5 | async-start | bytes 7077888 | tf_op jit(solution)/shard_map/all_gather | solution.py:418
  161.8 460.9 %all-gather.24.cloned.1.call-start = ((), (), s32[]{:S(2)}) async-start(), calls=%async_computation.11 | async-start | bytes 8110080 | tf_op jit(solution)/shard_map/all_gather | solution.py:351
  162.4 469.3 %all-gather.26.cloned.1.call-start = ((), (), s32[]{:S(2)}) async-start(), calls=%async_computation.12 | async-start | bytes 8110080 | tf_op jit(solution)/shard_map/all_gather | solution.py:352
  163.0 485.4 %all-gather.16.cloned.1.call-start = ((), (), s32[]{:S(2)}) async-start(), calls=%async_computation.4 | async-start | bytes 7299072 | tf_op jit(solution)/shard_map/all_gather | solution.py:353
  163.8 1644.4 %reduce-scatter.16.cloned.1.call-start = ((), (), s32[]{:S(2)}) async-start(), calls=%async_computation.6 | async-start | bytes 983040 | tf_op jit(solution)/shard_map/reduce_scatter | solution.py:480
  730.6 23.3 collective-permute-start.1
  730.7 38.2 %collective-permute-start = (bf16[4,2,64,768]{3,2,1,0:T(8,128)(2,1)S(1)}, bf16[4,2,64,768]{3,2,1,0:T(8,128)(2,1)S(1)}, u32[]{:S(2)}, u32[]{:S(2)}) collective-permute-start(bf16[4,2,64,768]{3,2,1,0:T(8,128)(2,1)S(1)} %copy-done.26), channel_id=1, source_target_pairs={{28,0},{0,4},{4,8},{8,12},{12,16},{16,20},{20,24},{24,28},{29,1},{... | collective-permute-start | bytes 2359304 | tf_op jit(solution)/shard_map/while/body/eval_jaxpr/ppermute | solution.py:18
  802.6 23.3 collective-permute-start.1
  802.7 37.2 %collective-permute-start = (bf16[4,2,64,768]{3,2,1,0:T(8,128)(2,1)S(1)}, bf16[4,2,64,768]{3,2,1,0:T(8,128)(2,1)S(1)}, u32[]{:S(2)}, u32[]{:S(2)}) collective-permute-start(bf16[4,2,64,768]{3,2,1,0:T(8,128)(2,1)S(1)} %copy-done.26), channel_id=1, source_target_pairs={{28,0},{0,4},{4,8},{8,12},{12,16},{16,20},{20,24},{24,28},{29,1},{... | collective-permute-start | bytes 2359304 | tf_op jit(solution)/shard_map/while/body/eval_jaxpr/ppermute | solution.py:18
  873.6 23.3 collective-permute-start.1
  873.7 36.3 %collective-permute-start = (bf16[4,2,64,768]{3,2,1,0:T(8,128)(2,1)S(1)}, bf16[4,2,64,768]{3,2,1,0:T(8,128)(2,1)S(1)}, u32[]{:S(2)}, u32[]{:S(2)}) collective-permute-start(bf16[4,2,64,768]{3,2,1,0:T(8,128)(2,1)S(1)} %copy-done.26), channel_id=1, source_target_pairs={{28,0},{0,4},{4,8},{8,12},{12,16},{16,20},{20,24},{24,28},{29,1},{... | collective-permute-start | bytes 2359304 | tf_op jit(solution)/shard_map/while/body/eval_jaxpr/ppermute | solution.py:18
  943.8 23.3 collective-permute-start.1
  943.8 35.4 %collective-permute-start = (bf16[4,2,64,768]{3,2,1,0:T(8,128)(2,1)S(1)}, bf16[4,2,64,768]{3,2,1,0:T(8,128)(2,1)S(1)}, u32[]{:S(2)}, u32[]{:S(2)}) collective-permute-start(bf16[4,2,64,768]{3,2,1,0:T(8,128)(2,1)S(1)} %copy-done.26), channel_id=1, source_target_pairs={{28,0},{0,4},{4,8},{8,12},{12,16},{16,20},{20,24},{24,28},{29,1},{... | collective-permute-start | bytes 2359304 | tf_op jit(solution)/shard_map/while/body/eval_jaxpr/ppermute | solution.py:18
  1013.0 23.3 collective-permute-start.1
  1013.0 34.5 %collective-permute-start = (bf16[4,2,64,768]{3,2,1,0:T(8,128)(2,1)S(1)}, bf16[4,2,64,768]{3,2,1,0:T(8,128)(2,1)S(1)}, u32[]{:S(2)}, u32[]{:S(2)}) collective-permute-start(bf16[4,2,64,768]{3,2,1,0:T(8,128)(2,1)S(1)} %copy-done.26), channel_id=1, source_target_pairs={{28,0},{0,4},{4,8},{8,12},{12,16},{16,20},{20,24},{24,28},{29,1},{... | collective-permute-start | bytes 2359304 | tf_op jit(solution)/shard_map/while/body/eval_jaxpr/ppermute | solution.py:18
  1081.2 23.3 collective-permute-start.1
  1081.3 33.5 %collective-permute-start = (bf16[4,2,64,768]{3,2,1,0:T(8,128)(2,1)S(1)}, bf16[4,2,64,768]{3,2,1,0:T(8,128)(2,1)S(1)}, u32[]{:S(2)}, u32[]{:S(2)}) collective-permute-start(bf16[4,2,64,768]{3,2,1,0:T(8,128)(2,1)S(1)} %copy-done.26), channel_id=1, source_target_pairs={{28,0},{0,4},{4,8},{8,12},{12,16},{16,20},{20,24},{24,28},{29,1},{... | collective-permute-start | bytes 2359304 | tf_op jit(solution)/shard_map/while/body/eval_jaxpr/ppermute | solution.py:18
  1148.6 23.3 collective-permute-start.1
  1148.7 32.6 %collective-permute-start = (bf16[4,2,64,768]{3,2,1,0:T(8,128)(2,1)S(1)}, bf16[4,2,64,768]{3,2,1,0:T(8,128)(2,1)S(1)}, u32[]{:S(2)}, u32[]{:S(2)}) collective-permute-start(bf16[4,2,64,768]{3,2,1,0:T(8,128)(2,1)S(1)} %copy-done.26), channel_id=1, source_target_pairs={{28,0},{0,4},{4,8},{8,12},{12,16},{16,20},{20,24},{24,28},{29,1},{... | collective-permute-start | bytes 2359304 | tf_op jit(solution)/shard_map/while/body/eval_jaxpr/ppermute | solution.py:18
  1215.0 23.3 collective-permute-start.1
  1215.1 31.7 %collective-permute-start = (bf16[4,2,64,768]{3,2,1,0:T(8,128)(2,1)S(1)}, bf16[4,2,64,768]{3,2,1,0:T(8,128)(2,1)S(1)}, u32[]{:S(2)}, u32[]{:S(2)}) collective-permute-start(bf16[4,2,64,768]{3,2,1,0:T(8,128)(2,1)S(1)} %copy-done.26), channel_id=1, source_target_pairs={{28,0},{0,4},{4,8},{8,12},{12,16},{16,20},{20,24},{24,28},{29,1},{... | collective-permute-start | bytes 2359304 | tf_op jit(solution)/shard_map/while/body/eval_jaxpr/ppermute | solution.py:18
  1250.2 559.1 %reduce-scatter.18.cloned.1.call-start = ((), (), s32[]{:S(2)}) async-start(), calls=%async_computation.7 | async-start | bytes 983040 | tf_op jit(solution)/shard_map/reduce_scatter | solution.py:480
  1297.8 22.6 collective-permute-start.3
  1297.9 30.9 %collective-permute-start.2 = (bf16[4,2,64,768]{3,2,1,0:T(8,128)(2,1)S(1)}, bf16[4,2,64,768]{3,2,1,0:T(8,128)(2,1)S(1)}, u32[]{:S(2)}, u32[]{:S(2)}) collective-permute-start(bf16[4,2,64,768]{3,2,1,0:T(8,128)(2,1)S(1)} %copy-done.28), channel_id=1, source_target_pairs={{28,0},{0,4},{4,8},{8,12},{12,16},{16,20},{20,24},{24,28},{29,1},{... | collective-permute-start | bytes 2359304 | tf_op jit(solution)/shard_map/while/body/eval_jaxpr/ppermute | solution.py:18
  1360.5 30.0 %collective-permute-start.2 = (bf16[4,2,64,768]{3,2,1,0:T(8,128)(2,1)S(1)}, bf16[4,2,64,768]{3,2,1,0:T(8,128)(2,1)S(1)}, u32[]{:S(2)}, u32[]{:S(2)}) collective-permute-start(bf16[4,2,64,768]{3,2,1,0:T(8,128)(2,1)S(1)} %copy-done.28), channel_id=1, source_target_pairs={{28,0},{0,4},{4,8},{8,12},{12,16},{16,20},{20,24},{24,28},{29,1},{... | collective-permute-start | bytes 2359304 | tf_op jit(solution)/shard_map/while/body/eval_jaxpr/ppermute | solution.py:18
  1422.3 29.2 %collective-permute-start.2 = (bf16[4,2,64,768]{3,2,1,0:T(8,128)(2,1)S(1)}, bf16[4,2,64,768]{3,2,1,0:T(8,128)(2,1)S(1)}, u32[]{:S(2)}, u32[]{:S(2)}) collective-permute-start(bf16[4,2,64,768]{3,2,1,0:T(8,128)(2,1)S(1)} %copy-done.28), channel_id=1, source_target_pairs={{28,0},{0,4},{4,8},{8,12},{12,16},{16,20},{20,24},{24,28},{29,1},{... | collective-permute-start | bytes 2359304 | tf_op jit(solution)/shard_map/while/body/eval_jaxpr/ppermute | solution.py:18
  1483.3 28.4 %collective-permute-start.2 = (bf16[4,2,64,768]{3,2,1,0:T(8,128)(2,1)S(1)}, bf16[4,2,64,768]{3,2,1,0:T(8,128)(2,1)S(1)}, u32[]{:S(2)}, u32[]{:S(2)}) collective-permute-start(bf16[4,2,64,768]{3,2,1,0:T(8,128)(2,1)S(1)} %copy-done.28), channel_id=1, source_target_pairs={{28,0},{0,4},{4,8},{8,12},{12,16},{16,20},{20,24},{24,28},{29,1},{... | collective-permute-start | bytes 2359304 | tf_op jit(solution)/shard_map/while/body/eval_jaxpr/ppermute | solution.py:18
  1543.5 27.6 %collective-permute-start.2 = (bf16[4,2,64,768]{3,2,1,0:T(8,128)(2,1)S(1)}, bf16[4,2,64,768]{3,2,1,0:T(8,128)(2,1)S(1)}, u32[]{:S(2)}, u32[]{:S(2)}) collective-permute-start(bf16[4,2,64,768]{3,2,1,0:T(8,128)(2,1)S(1)} %copy-done.28), channel_id=1, source_target_pairs={{28,0},{0,4},{4,8},{8,12},{12,16},{16,20},{20,24},{24,28},{29,1},{... | collective-permute-start | bytes 2359304 | tf_op jit(solution)/shard_map/while/body/eval_jaxpr/ppermute | solution.py:18
  1602.9 26.8 %collective-permute-start.2 = (bf16[4,2,64,768]{3,2,1,0:T(8,128)(2,1)S(1)}, bf16[4,2,64,768]{3,2,1,0:T(8,128)(2,1)S(1)}, u32[]{:S(2)}, u32[]{:S(2)}) collective-permute-start(bf16[4,2,64,768]{3,2,1,0:T(8,128)(2,1)S(1)} %copy-done.28), channel_id=1, source_target_pairs={{28,0},{0,4},{4,8},{8,12},{12,16},{16,20},{20,24},{24,28},{29,1},{... | collective-permute-start | bytes 2359304 | tf_op jit(solution)/shard_map/while/body/eval_jaxpr/ppermute | solution.py:18
  1661.4 25.9 collective-permute-start.2
  1719.2 25.1 collective-permute-start.2
  1747.2 881.7 %reduce-scatter.20.cloned.1.call-start = ((), (), s32[]{:S(2)}) async-start(), calls=%async_computation.8 | async-start | bytes 14598144 | tf_op jit(solution)/shard_map/reduce_scatter | solution.py:536
  2347.8 56.4 %collective-permute-start.18 = (f32[48,384]{1,0:T(8,128)}, f32[48,384]{1,0:T(8,128)S(1)}, u32[]{:S(2)}, u32[]{:S(2)}) collective-permute-start(f32[48,384]{1,0:T(8,128)} %get-tuple-element.1744), channel_id=1, source_target_pairs={{0,7},{1,8},{2,9},{3,10},{4,11},{5,12},{6,13},{7,14},{8,15},{9,16}... | collective-permute-start | bytes 221192
  2379.1 27.7 %collective-permute-start.17 = (f32[48,384]{1,0:T(8,128)}, f32[48,384]{1,0:T(8,128)S(1)}, u32[]{:S(2)}, u32[]{:S(2)}) collective-permute-start(f32[48,384]{1,0:T(8,128)} %get-tuple-element.1744), channel_id=1, source_target_pairs={{0,6},{1,7},{2,8},{3,9},{4,10},{5,11},{6,12},{7,13},{8,14},{9,15},... | collective-permute-start | bytes 221192
  2386.8 23.9 collective-permute-start.16
  2431.7 22.6 collective-permute-start.9
  2472.5 101.2 %collective-permute-start.38 = (f32[40,3072]{1,0:T(8,128)}, f32[40,3072]{1,0:T(8,128)}, u32[]{:S(2)}, u32[]{:S(2)}) collective-permute-start(f32[40,3072]{1,0:T(8,128)} %get-tuple-element.1747), channel_id=1, source_target_pairs={{0,3},{1,4},{2,5},{3,6},{4,7},{5,8},{6,9},{7,10},{8,11},{9,12},{10... | collective-permute-start | bytes 1474568
  2478.6 83.9 %collective-permute-start.30 = (f32[48,1152]{1,0:T(8,128)S(1)}, f32[48,1152]{1,0:T(8,128)S(1)}, u32[]{:S(2)}, u32[]{:S(2)}) collective-permute-start(f32[48,1152]{1,0:T(8,128)S(1)} %get-tuple-element.1746), channel_id=1, source_target_pairs={{0,3},{1,4},{2,5},{3,6},{4,7},{5,8},{6,9},{7,10},{8,11},{9,12},{10... | collective-permute-start | bytes 663560
  2480.1 84.4 %collective-permute-start.29 = (f32[48,1152]{1,0:T(8,128)S(1)}, f32[48,1152]{1,0:T(8,128)S(1)}, u32[]{:S(2)}, u32[]{:S(2)}) collective-permute-start(f32[48,1152]{1,0:T(8,128)S(1)} %get-tuple-element.1746), channel_id=1, source_target_pairs={{0,2},{1,3},{2,4},{3,5},{4,6},{5,7},{6,8},{7,9},{8,10},{9,11},{10,... | collective-permute-start | bytes 663560
  2486.1 84.4 %collective-permute-start.28 = (f32[48,1152]{1,0:T(8,128)S(1)}, f32[48,1152]{1,0:T(8,128)}, u32[]{:S(2)}, u32[]{:S(2)}) collective-permute-start(f32[48,1152]{1,0:T(8,128)S(1)} %get-tuple-element.1746), channel_id=1, source_target_pairs={{0,1},{1,2},{2,3},{3,4},{4,5},{5,6},{6,7},{7,8},{8,9},{9,10},{10,1... | collective-permute-start | bytes 663560
  2488.1 110.7 %collective-permute-start.37 = (f32[40,3072]{1,0:T(8,128)}, f32[40,3072]{1,0:T(8,128)}, u32[]{:S(2)}, u32[]{:S(2)}) collective-permute-start(f32[40,3072]{1,0:T(8,128)} %get-tuple-element.1747), channel_id=1, source_target_pairs={{0,2},{1,3},{2,4},{3,5},{4,6},{5,7},{6,8},{7,9},{8,10},{9,11},{10,... | collective-permute-start | bytes 1474568
  2562.4 41.4 %collective-permute-start.36 = (f32[40,3072]{1,0:T(8,128)}, f32[40,3072]{1,0:T(8,128)}, u32[]{:S(2)}, u32[]{:S(2)}) collective-permute-start(f32[40,3072]{1,0:T(8,128)} %get-tuple-element.1747), channel_id=1, source_target_pairs={{0,1},{1,2},{2,3},{3,4},{4,5},{5,6},{6,7},{7,8},{8,9},{9,10},{10,1... | collective-permute-start | bytes 1474568
  2564.5 48.2 %collective-permute-start.42 = (f32[40,3072]{1,0:T(8,128)S(1)}, f32[40,3072]{1,0:T(8,128)}, u32[]{:S(2)}, u32[]{:S(2)}) collective-permute-start(f32[40,3072]{1,0:T(8,128)S(1)} %copy-done.82), channel_id=1, source_target_pairs={{0,3},{1,4},{2,5},{3,6},{4,7},{5,8},{6,9},{7,10},{8,11},{9,12},{10... | collective-permute-start | bytes 1474568
  2570.5 42.2 %collective-permute-start.41 = (f32[40,3072]{1,0:T(8,128)S(1)}, f32[40,3072]{1,0:T(8,128)}, u32[]{:S(2)}, u32[]{:S(2)}) collective-permute-start(f32[40,3072]{1,0:T(8,128)S(1)} %copy-done.82), channel_id=1, source_target_pairs={{0,2},{1,3},{2,4},{3,5},{4,6},{5,7},{6,8},{7,9},{8,10},{9,11},{10,... | collective-permute-start | bytes 1474568
  2573.6 39.1 %collective-permute-start.40 = (f32[40,3072]{1,0:T(8,128)S(1)}, f32[40,3072]{1,0:T(8,128)}, u32[]{:S(2)}, u32[]{:S(2)}) collective-permute-start(f32[40,3072]{1,0:T(8,128)S(1)} %copy-done.82), channel_id=1, source_target_pairs={{0,1},{1,2},{2,3},{3,4},{4,5},{5,6},{6,7},{7,8},{8,9},{9,10},{10,1... | collective-permute-start | bytes 1474568
  (311 other events, 4006.6 us)
Sparse Core Ops, SparseCore 0:
  11.0 61.9 all-gather.19
  75.8 59.5 all-gather.21
  152.2 95.2 all-gather.13
  249.5 97.1 all-gather.17
  349.4 73.7 all-gather.23
  426.0 73.8 all-gather.25
  502.7 71.0 all-gather.15
  1250.3 20.4 reduce-scatter.15
  1747.3 20.4 reduce-scatter.17
  1774.2 234.7 reduce-scatter.19
where the time goes:
time: 2660 us; the launch traced here: 2640 us
  blocking collectives  734 us (28%)
  local copies, waits for them, and re-layouts  670 us (25%)
  waiting for transfers between devices  513 us (19%)
  matrix products  267 us (10%)
  other arithmetic  239 us (9%)
  starting transfers between devices  154 us (6%)
  loops' own time  42.9 us (2%)
    unnamed x3, blocking collectives  624 us
    ppermute x32, waiting for transfers between devices, shifted(): return lax.ppermute(block, axis, route)  443 us
    unnamed x40, starting transfers between devices  152 us
    unnamed x284, local copies, waits for them, and re-layouts  104 us
    all_gather x2, waiting for transfers between devices, per_device(): lax.all_gather(group_block[None], 'ctx', axis=0, tiled=True)  66.3 us
    another operation x42, local copies, waits for them, and re-layouts  59.6 us
    dynamic_slice x48, local copies, waits for them, and re-layouts, fold_step(): result_state, _ = lax.scan(visit_block, carried, (shard_piece, source_list))  59.2 us
    slice x32, local copies, waits for them, and re-layouts, split_block(): block_of_keys[..., hidden_width:]  53.4 us
  transfers between devices with their start and end apart: 82, of which 34 were waited for; matrix products, arithmetic and copies ran while one was open for 52% of the time, Pallas kernels for 0%

commit v1 on v0

--- a/solution.py
+++ b/solution.py
@@ -1,7 +1,10 @@
 import jax
 import jax.numpy as jnp
 from jax import lax
+from jax.experimental import pallas as pl
+from jax.experimental.pallas import tpu as pltpu
 from jax.sharding import PartitionSpec as P
+import functools
 
 QUERY_HEADS = 18
 KEY_VALUE_HEADS = 6
@@ -550,6 +553,702 @@
     )
 
 
+MESH = pl.DeviceIdType.MESH
+NEG = -1e30
+WIDE = 128
+VMEM_LIMIT = 60 * 1024 * 1024
+
+
+def fits_fast(mesh):
+    return mesh.shape["ctx"] == 8 and mesh.shape["ws"] == 4
+
+
+def place():
+    c = lax.axis_index("ctx")
+    w = lax.axis_index("ws")
+    return c // 2, lax.rem(c, 2), w // 2, lax.rem(w, 2)
+
+
+def device(z, y, x, k):
+    return (z * 2 + y, x * 2 + k)
+
+
+def greet(zn):
+    z, y, x, k = place()
+    others = [device(lax.rem(z + j, zn), y, x, k) for j in range(1, zn)]
+    others += [device(z, y, 1 - x, k), device(z, 1 - y, x, k), device(z, y, x, 1 - k)]
+    barrier = pltpu.get_barrier_semaphore()
+    for other in others:
+        pl.semaphore_signal(barrier, inc=1, device_id=other, device_id_type=MESH)
+    pl.semaphore_wait(barrier, len(others))
+
+
+def remote(src, dst, send, recv, where):
+    return pltpu.make_async_remote_copy(
+        src_ref=src, dst_ref=dst, send_sem=send, recv_sem=recv, device_id=where, device_id_type=MESH
+    )
+
+
+class Gather:
+    SEMS = 12
+
+    def __init__(self, src, dst, send, recv, zn):
+        z, y, x, k = place()
+        own = dst.at[z, y, x, k]
+        hz = zn // 2
+        xn, yn, sib = device(z, y, 1 - x, k), device(z, 1 - y, x, k), device(z, y, x, 1 - k)
+
+        def push(i, ref, where):
+            return remote(ref, ref, send.at[i], recv.at[i], where)
+
+        def col(yy, xx, lo=0, n=zn):
+            return dst.at[pl.ds(lo, n), yy, xx, k]
+
+        self.local = pltpu.make_async_copy(src, own, send.at[0])
+        self.along = [
+            remote(src, own, send.at[j], recv.at[j], device(lax.rem(z + j, zn), y, x, k))
+            for j in range(1, zn)
+        ]
+        self.cols = [push(4, col(y, x), xn), push(5, col(y, x), yn)]
+        self.corner = [push(7, col(1 - y, x, 0, hz), xn), push(8, col(y, 1 - x, hz, hz), yn)]
+        self.twin_own = push(6, col(y, x), sib)
+        self.twin_cols = [push(9, col(y, 1 - x), sib), push(10, col(1 - y, x), sib)]
+        self.twin_corner = push(11, col(1 - y, 1 - x), sib)
+
+    def stage(self, n):
+        if n == 0:
+            self.local.start()
+            for c in self.along:
+                c.start()
+        elif n == 1:
+            self.local.wait()
+            for c in self.along:
+                c.wait_recv()
+            for c in self.cols:
+                c.start()
+            self.twin_own.start()
+        elif n == 2:
+            for c in self.cols:
+                c.wait_recv()
+            for c in self.corner:
+                c.start()
+            for c in self.twin_cols:
+                c.start()
+        elif n == 3:
+            for c in self.corner:
+                c.wait_recv()
+            self.twin_corner.start()
+        elif n == 4:
+            for c in [self.twin_own] + self.twin_cols + [self.twin_corner]:
+                c.wait_recv()
+            for c in (
+                self.along
+                + self.cols
+                + self.corner
+                + [self.twin_own]
+                + self.twin_cols
+                + [self.twin_corner]
+            ):
+                c.wait_send()
+
+
+def run_stages(items, stages):
+    for t in range(len(items) + stages - 1):
+        for n in range(stages):
+            if 0 <= t - n < len(items):
+                items[t - n].stage(n)
+
+
+def pieces_of(rows, cols, nrow, ncol):
+    return [
+        (i * (rows // nrow), rows // nrow, j * (cols // ncol), cols // ncol)
+        for i in range(nrow)
+        for j in range(ncol)
+    ]
+
+
+def gather_all(arrays, rows_used, cuts, collective_id):
+    zn = lax.axis_size("ctx") // 2
+    n = len(arrays)
+    work = [
+        (a, piece)
+        for a in range(n)
+        for piece in pieces_of(rows_used[a], arrays[a].shape[1], *cuts[a])
+    ]
+
+    def kernel(*refs):
+        ins, outs, (send, recv) = refs[:n], refs[n : 2 * n], refs[2 * n :]
+        greet(zn)
+        items = []
+        for i, (a, (r0, nr, c0, nc)) in enumerate(work):
+            src = ins[a].at[pl.ds(r0, nr), pl.ds(c0, nc)]
+            dst = outs[a].at[:, :, :, :, pl.ds(r0, nr), pl.ds(c0, nc)]
+            items.append(Gather(src, dst, send.at[i], recv.at[i], zn))
+        run_stages(items, 5)
+
+    return pl.pallas_call(
+        kernel,
+        out_shape=[
+            jax.ShapeDtypeStruct((zn, 2, 2, 2, rows_used[a], arrays[a].shape[1]), arrays[a].dtype)
+            for a in range(n)
+        ],
+        in_specs=[pl.BlockSpec(memory_space=pl.ANY)] * n,
+        out_specs=[pl.BlockSpec(memory_space=pl.ANY)] * n,
+        scratch_shapes=[
+            pltpu.SemaphoreType.DMA((len(work), Gather.SEMS)),
+            pltpu.SemaphoreType.DMA((len(work), Gather.SEMS)),
+        ],
+        compiler_params=pltpu.CompilerParams(
+            collective_id=collective_id, has_side_effects=True, vmem_limit_bytes=VMEM_LIMIT
+        ),
+    )(*arrays)
+
+
+class Scatter:
+    SEMS = 10
+
+    @staticmethod
+    def scratch(zn, nr, nc):
+        b = jnp.bfloat16
+        return [
+            pltpu.VMEM((zn, 2, 2, nr, nc), b),
+            pltpu.VMEM((zn, 2, 2, nr, nc), b),
+            pltpu.VMEM((2, zn // 2, nr, nc), b),
+            pltpu.VMEM((2, zn, nr, nc), b),
+            pltpu.VMEM((zn - 1, nr, nc), b),
+        ]
+
+    def __init__(self, part, out, bufs, send, recv, zn):
+        z, y, x, k = self.at = place()
+        self.zn = zn
+        hz = zn // 2
+        xn, yn, sib = device(z, y, 1 - x, k), device(z, 1 - y, x, k), device(z, y, x, 1 - k)
+        self.held, self.twin, self.corners, self.colsums, self.ends = held, twin, corners, colsums, ends = bufs
+        self.out = out
+        self.load = pltpu.make_async_copy(part.at[:, :, :, k], held, send.at[0])
+        self.to_twin = remote(part.at[:, :, :, 1 - k], twin, send.at[1], recv.at[1], sib)
+        self.to_corner = [
+            remote(held.at[pl.ds(0, hz), 1 - y, 1 - x], corners.at[0], send.at[2], recv.at[2], yn),
+            remote(held.at[pl.ds(hz, hz), 1 - y, 1 - x], corners.at[1], send.at[3], recv.at[3], xn),
+        ]
+        self.to_col = [
+            remote(held.at[:, y, 1 - x], colsums.at[0], send.at[4], recv.at[4], xn),
+            remote(held.at[:, 1 - y, x], colsums.at[1], send.at[5], recv.at[5], yn),
+        ]
+        self.along = []
+        for j in range(1, zn):
+            zz = lax.rem(z + j, zn)
+            self.along.append(
+                remote(held.at[zz, y, x], ends.at[j - 1], send.at[5 + j], recv.at[5 + j], device(zz, y, x, k))
+            )
+
+    def stage(self, n):
+        z, y, x, k = self.at
+        zn, hz = self.zn, self.zn // 2
+        held = self.held
+        if n == 0:
+            self.to_twin.start()
+            self.load.start()
+        elif n == 1:
+            self.load.wait()
+            self.to_twin.wait_recv()
+
+            def add(i, _):
+                for yy in range(2):
+                    for xx in range(2):
+                        held[i, yy, xx] = held[i, yy, xx] + self.twin[i, yy, xx]
+                return 0
+
+            lax.fori_loop(0, zn, add, 0)
+            for c in self.to_corner:
+                c.start()
+        elif n == 2:
+            for c in self.to_corner:
+                c.wait_recv()
+            for i in range(hz):
+                held[i, y, 1 - x] = held[i, y, 1 - x] + self.corners[0, i]
+                held[hz + i, 1 - y, x] = held[hz + i, 1 - y, x] + self.corners[1, i]
+            for c in self.to_col:
+                c.start()
+        elif n == 3:
+            for c in self.to_col:
+                c.wait_recv()
+
+            def add(i, _):
+                f = jnp.float32
+                held[i, y, x] = (
+                    held[i, y, x].astype(f) + self.colsums[0, i].astype(f) + self.colsums[1, i].astype(f)
+                ).astype(jnp.bfloat16)
+                return 0
+
+            lax.fori_loop(0, zn, add, 0)
+            for c in self.along:
+                c.start()
+        elif n == 4:
+            for c in self.along:
+                c.wait_recv()
+            total = held[z, y, x].astype(jnp.float32)
+            for j in range(zn - 1):
+                total = total + self.ends[j].astype(jnp.float32)
+            self.out[...] = total
+            for c in [self.to_twin] + self.to_corner + self.to_col + self.along:
+                c.wait_send()
+
+
+def scatter_all(parts, cuts, collective_id):
+    zn = lax.axis_size("ctx") // 2
+    n = len(parts)
+    work = [
+        (a, piece) for a in range(n) for piece in pieces_of(*parts[a].shape[4:], *cuts[a])
+    ]
+    scratch = []
+    for a, (r0, nr, c0, nc) in work:
+        scratch += Scatter.scratch(zn, nr, nc)
+
+    def kernel(*refs):
+        ins, outs, bufs, (send, recv) = refs[:n], refs[n : 2 * n], refs[2 * n : -2], refs[-2:]
+        greet(zn)
+        items = []
+        for i, (a, (r0, nr, c0, nc)) in enumerate(work):
+            part = ins[a].at[:, :, :, :, pl.ds(r0, nr), pl.ds(c0, nc)]
+            out = outs[a].at[pl.ds(r0, nr), pl.ds(c0, nc)]
+            items.append(Scatter(part, out, bufs[5 * i : 5 * i + 5], send.at[i], recv.at[i], zn))
+        run_stages(items, 5)
+
+    return pl.pallas_call(
+        kernel,
+        out_shape=[jax.ShapeDtypeStruct(p.shape[4:], jnp.float32) for p in parts],
+        in_specs=[pl.BlockSpec(memory_space=pl.ANY)] * n,
+        out_specs=[pl.BlockSpec(memory_space=pltpu.VMEM)] * n,
+        scratch_shapes=scratch
+        + [
+            pltpu.SemaphoreType.DMA((len(work), Scatter.SEMS)),
+            pltpu.SemaphoreType.DMA((len(work), Scatter.SEMS)),
+        ],
+        compiler_params=pltpu.CompilerParams(
+            collective_id=collective_id, has_side_effects=True, vmem_limit_bytes=VMEM_LIMIT
+        ),
+    )(*parts)
+
+
+def head_lanes(block, head, group):
+    t = block.astype(jnp.float32)
+    if head % 2 != group % 2:
+        t = pltpu.roll(t, HEAD_SIZE, 1)
+    lane = lax.broadcasted_iota(jnp.int32, t.shape, 1)
+    return jnp.where((lane // HEAD_SIZE) == group % 2, t, 0.0)
+
+
+def spread_heads(src, dst, mb, scale):
+    per = QUERY_HEADS // KEY_VALUE_HEADS
+    rows = src.shape[1] // 2
+    for half in range(2):
+        for g in range(KEY_VALUE_HEADS):
+            for j in range(per):
+                h = per * g + j
+                block = src[mb, half * rows : (half + 1) * rows, WIDE * (h // 2) : WIDE * (h // 2) + WIDE]
+                t = head_lanes(block, h, g) * scale
+                dst[half, g, j * rows : (j + 1) * rows, :] = t.astype(dst.dtype)
+
+
+def join_heads(get, half, mb, dst, rows):
+    per = QUERY_HEADS // KEY_VALUE_HEADS
+    vals = {}
+    for g in range(KEY_VALUE_HEADS):
+        t = get(g)
+        for j in range(per):
+            vals[per * g + j] = (t[j * rows : (j + 1) * rows], g)
+    lane = lax.broadcasted_iota(jnp.int32, (rows, WIDE), 1)
+    for m in range(QUERY_HEADS // 2):
+        sides = []
+        for h in (2 * m, 2 * m + 1):
+            t, g = vals[h]
+            if h % 2 != g % 2:
+                t = pltpu.roll(t, HEAD_SIZE, 1)
+            sides.append(t)
+        both = jnp.where(lane < HEAD_SIZE, sides[0], sides[1])
+        dst[mb, half * rows : (half + 1) * rows, WIDE * m : WIDE * m + WIDE] = both.astype(dst.dtype)
+
+
+def span_of(t, c, cn):
+    half = (t > c).astype(jnp.int32)
+    j = jnp.where(half == 1, t - c - 1, t)
+    last = jnp.where(half == 1, 2 * cn - 1 - c, c)
+    late = (j >= cn).astype(jnp.int32)
+    src = jnp.where(late == 1, 2 * cn - 1 - j, j)
+    return half, src, late, j == last
+
+
+def hidden_bias(diag, w, rows, per, wn):
+    shape = (per * rows, wn * rows)
+    i = lax.rem(lax.broadcasted_iota(jnp.int32, shape, 0), rows)
+    key = lax.broadcasted_iota(jnp.int32, shape, 1)
+    limit = jnp.where(diag, w * rows, wn * rows)
+    return jnp.where(key <= i + limit, 0.0, NEG)
+
+
+NT = (((1,), (1,)), ((), ()))
+TN = (((0,), (0,)), ((), ()))
+
+
+def nt(a, b):
+    return lax.dot_general(a, b, NT, preferred_element_type=jnp.float32)
+
+
+def tn(a, b):
+    return lax.dot_general(a, b, TN, preferred_element_type=jnp.float32)
+
+
+def attention(q, kv):
+    mbs, tokens, qw = q.shape
+    cn, wn = kv.shape[:2]
+    rows = tokens // 2
+    per = QUERY_HEADS // KEY_VALUE_HEADS
+    hid = KEY_VALUE_HEADS * HEAD_SIZE
+    groups = range(KEY_VALUE_HEADS)
+
+    def kernel(q_ref, kv_ref, o_ref, lse_ref, qs, m_s, l_s, acc):
+        c, w = lax.axis_index("ctx"), lax.axis_index("ws")
+
+        def one(mb, _):
+            spread_heads(q_ref, qs, mb, HEAD_SIZE**-0.5)
+            m_s[...] = jnp.full(m_s.shape, NEG, jnp.float32)
+            l_s[...] = jnp.zeros(l_s.shape, jnp.float32)
+            acc[...] = jnp.zeros(acc.shape, jnp.float32)
+
+            def step(t, _):
+                half, src, late, diag = span_of(t, c, cn)
+                bias = hidden_bias(diag, w, rows, per, wn)
+                for g in groups:
+                    lo = WIDE * (g // 2)
+                    kb = kv_ref[src, :, mb, late, :, lo : lo + WIDE].reshape(wn * rows, WIDE)
+                    vb = kv_ref[src, :, mb, late, :, hid + lo : hid + lo + WIDE].reshape(wn * rows, WIDE)
+                    s = nt(qs[half, g], kb) + bias
+                    m_old = m_s[half, g]
+                    m_new = jnp.maximum(m_old, jnp.max(s, axis=1, keepdims=True))
+                    alpha = jnp.exp(m_old - m_new)
+                    p = jnp.exp(s - m_new[:, :1])
+                    m_s[half, g] = m_new
+                    l_s[half, g] = l_s[half, g] * alpha + jnp.sum(p, axis=1, keepdims=True)
+                    acc[half, g] = acc[half, g] * alpha + jnp.dot(
+                        p.astype(jnp.bfloat16), vb, preferred_element_type=jnp.float32
+                    )
+                return 0
+
+            lax.fori_loop(0, 2 * cn + 1, step, 0)
+            for half in range(2):
+                join_heads(lambda g: acc[half, g] / l_s[half, g], half, mb, o_ref, rows)
+                for g in groups:
+                    lse_ref[mb, half, g] = m_s[half, g] + jnp.log(l_s[half, g])
+            return 0
+
+        lax.fori_loop(0, mbs, one, 0)
+
+    stat = (2, KEY_VALUE_HEADS, per * rows, WIDE)
+    return pl.pallas_call(
+        kernel,
+        out_shape=[
+            jax.ShapeDtypeStruct(q.shape, jnp.bfloat16),
+            jax.ShapeDtypeStruct((mbs,) + stat, jnp.float32),
+        ],
+        in_specs=[pl.BlockSpec(memory_space=pltpu.VMEM)] * 2,
+        out_specs=[pl.BlockSpec(memory_space=pltpu.VMEM)] * 2,
+        scratch_shapes=[
+            pltpu.VMEM(stat, jnp.bfloat16),
+            pltpu.VMEM(stat, jnp.float32),
+            pltpu.VMEM(stat, jnp.float32),
+            pltpu.VMEM(stat, jnp.float32),
+        ],
+        compiler_params=pltpu.CompilerParams(vmem_limit_bytes=VMEM_LIMIT),
+    )(q, kv)
+
+
+def attention_back(q, kv, o, do, lse):
+    mbs, tokens, qw = q.shape
+    cn, wn = kv.shape[:2]
+    rows = tokens // 2
+    per = QUERY_HEADS // KEY_VALUE_HEADS
+    hid = KEY_VALUE_HEADS * HEAD_SIZE
+    groups = range(KEY_VALUE_HEADS)
+    scale = HEAD_SIZE**-0.5
+
+    def kernel(q_ref, kv_ref, o_ref, do_ref, lse_ref, dq_ref, dkv_ref, qs, dos, delta, dq, dkv, stage, sems):
+        c, w = lax.axis_index("ctx"), lax.axis_index("ws")
+
+        def flush(mb):
+            return pltpu.make_async_copy(stage, dkv_ref.at[:, :, mb], sems.at[0])
+
+        for mb in range(mbs):
+            spread_heads(q_ref, qs, mb, scale)
+            spread_heads(do_ref, dos, mb, 1.0)
+            for half in range(2):
+                for g in groups:
+                    for j in range(per):
+                        h = per * g + j
+                        lo = WIDE * (h // 2)
+                        block = o_ref[mb, half * rows : (half + 1) * rows, lo : lo + WIDE]
+                        oh = head_lanes(block, h, g)
+                        d = jnp.sum(oh * dos[half, g, j * rows : (j + 1) * rows, :].astype(jnp.float32), axis=1, keepdims=True)
+                        delta[half, g, j * rows : (j + 1) * rows, :] = jnp.broadcast_to(d, (rows, WIDE))
+            dq[...] = jnp.zeros(dq.shape, jnp.float32)
+
+            def clear(i, _):
+                dkv[i] = jnp.zeros(dkv.shape[1:], jnp.float32)
+                return 0
+
+            lax.fori_loop(0, cn, clear, 0)
+
+            def step(t, _):
+                half, src, late, diag = span_of(t, c, cn)
+                bias = hidden_bias(diag, w, rows, per, wn)
+                for g in groups:
+                    lo = WIDE * (g // 2)
+                    kb = kv_ref[src, :, mb, late, :, lo : lo + WIDE].reshape(wn * rows, WIDE)
+                    vb = kv_ref[src, :, mb, late, :, hid + lo : hid + lo + WIDE].reshape(wn * rows, WIDE)
+                    qg, dog = qs[half, g], dos[half, g]
+                    p = jnp.exp(nt(qg, kb) + bias - lse_ref[mb, half, g][:, :1])
+                    ds = (p * (nt(dog, vb) - delta[half, g][:, :1])).astype(jnp.bfloat16)
+                    dq[half, g] += jnp.dot(ds, kb, preferred_element_type=jnp.float32)
+                    dk = tn(ds, qg).reshape(wn, rows, WIDE)
+                    dv = tn(p.astype(jnp.bfloat16), dog).reshape(wn, rows, WIDE)
+                    dkv[src, :, late, :, lo : lo + WIDE] += dk
+                    dkv[src, :, late, :, hid + lo : hid + lo + WIDE] += dv
+                return 0
+
+            lax.fori_loop(0, 2 * cn + 1, step, 0)
+            for half in range(2):
+                join_heads(lambda g: dq[half, g] * scale, half, mb, dq_ref, rows)
+            if mb > 0:
+                flush(mb - 1).wait()
+
+            def pack(i, _):
+                stage[i] = dkv[i].astype(jnp.bfloat16)
+                return 0
+
+            lax.fori_loop(0, cn, pack, 0)
+            flush(mb).start()
+        flush(mbs - 1).wait()
+
+    stat = (2, KEY_VALUE_HEADS, per * rows, WIDE)
+    return pl.pallas_call(
+        kernel,
+        out_shape=[
+            jax.ShapeDtypeStruct(q.shape, jnp.float32),
+            jax.ShapeDtypeStruct(kv.shape, jnp.bfloat16),
+        ],
+        in_specs=[pl.BlockSpec(memory_space=pltpu.VMEM)] * 5,
+        out_specs=[pl.BlockSpec(memory_space=pltpu.VMEM), pl.BlockSpec(memory_space=pl.ANY)],
+        scratch_shapes=[
+            pltpu.VMEM(stat, jnp.bfloat16),
+            pltpu.VMEM(stat, jnp.bfloat16),
+            pltpu.VMEM(stat, jnp.float32),
+            pltpu.VMEM(stat, jnp.float32),
+            pltpu.VMEM((cn, wn, 2, rows, 2 * hid), jnp.float32),
+            pltpu.VMEM((cn, wn, 2, rows, 2 * hid), jnp.bfloat16),
+            pltpu.SemaphoreType.DMA((1,)),
+        ],
+        compiler_params=pltpu.CompilerParams(vmem_limit_bytes=VMEM_LIMIT),
+    )(q, kv, o, do, lse)
+
+
+def rotate_lanes(t, cos, low, high):
+    quarter = HEAD_SIZE // 2
+    return t * cos + jnp.roll(t, -quarter, axis=-1) * low + jnp.roll(t, quarter, axis=-1) * high
+
+
+def lane_tables(positions, heads):
+    quarter = HEAD_SIZE // 2
+    frequency = 10000.0 ** (-2.0 * jnp.arange(quarter, dtype=jnp.float32) / HEAD_SIZE)
+    angles = positions.astype(jnp.float32)[:, None] * frequency[None, :]
+    cos, sin = jnp.cos(angles), jnp.sin(angles)
+    none = jnp.zeros_like(sin)
+    full = lambda a, b: jnp.tile(jnp.concatenate([a, b], axis=1), (1, heads))
+    return full(cos, cos), full(-sin, none), full(none, sin)
+
+
+def fast_device(
+    inputs,
+    attn_gain,
+    query_weight,
+    key_matrix,
+    value_matrix,
+    out_weight,
+    ffn_gain,
+    gate_weight,
+    up_weight,
+    down_weight,
+    cotangent,
+):
+    f32, b16 = jnp.float32, jnp.bfloat16
+    cn, wn = lax.axis_size("ctx"), lax.axis_size("ws")
+    dn = cn * wn
+    zn = cn // 2
+    mbs, tokens, width = inputs.shape
+    own = query_weight.shape[0]
+    ra = own // 16 * 16
+    rb = own - ra
+    q_width = query_weight.shape[1]
+    hid = KEY_VALUE_HEADS * HEAD_SIZE
+    ff = gate_weight.shape[1]
+    rows = mbs * tokens
+    wa = dn * ra
+
+    new = jnp.arange(width)
+    old = jnp.where(
+        new < wa, own * (new // ra) + new % ra, own * ((new - wa) // rb) + ra + (new - wa) % rb
+    )
+    order = (jnp.arange(width)[:, None] == old[None, :]).astype(b16)
+
+    def to_order(t):
+        return jnp.dot(t, order, preferred_element_type=f32).astype(t.dtype)
+
+    def from_order(t):
+        return lax.dot_general(t, order, NT, preferred_element_type=f32).astype(t.dtype)
+
+    fold = 16 // rb
+
+    def folded(t):
+        return t.reshape(t.shape[0], fold, -1).transpose(1, 0, 2).reshape(16, -1)
+
+    qkv_w = q_width + 2 * hid
+    pad1 = -qkv_w % (fold * WIDE)
+    rest_w = width + 2 * ff
+    pad2 = -rest_w % (fold * WIDE)
+    moved = to_order(
+        jnp.concatenate(
+            [inputs.reshape(rows, width), cotangent.reshape(rows, width), out_weight, down_weight]
+        )
+    )
+    x_low, gy_low = moved[:rows], moved[rows : 2 * rows]
+    out_p, down_p = moved[2 * rows : 2 * rows + own], moved[2 * rows + own :]
+    qkv = jnp.concatenate([query_weight, key_matrix, value_matrix], axis=1)
+    gains = jnp.stack([attn_gain, ffn_gain])
+    gains = jnp.pad(gains, ((0, rb - 2), (0, pad1 - own)))
+    b1 = folded(jnp.concatenate([qkv[ra:], gains], axis=1))
+    b2 = folded(
+        jnp.pad(
+            jnp.concatenate([out_p[ra:], gate_weight[ra:], up_weight[ra:]], axis=1), ((0, 0), (0, pad2))
+        )
+    )
+    arrays = [qkv, b1, out_p, gate_weight, up_weight, down_p, b2]
+    used = [ra, 16, ra, ra, ra, down_p.shape[0], 16]
+    cuts = [(1, 1), (1, 1), (1, 1), (1, 2), (1, 2), (2, 1), (1, 1)]
+    qkv_a, b1g, out_a, gate_a, up_a, down_a, b2g = gather_all(arrays, used, cuts, 1)
+
+    def unfolded(t):
+        cols = t.shape[-1]
+        return t.reshape(dn, fold, rb, cols).transpose(0, 2, 1, 3).reshape(dn * rb, fold * cols)
+
+    flat = lambda t: t.reshape(-1, t.shape[-1])
+    qkv_a, out_a, gate_a, up_a, down_w = map(flat, (qkv_a, out_a, gate_a, up_a, down_a))
+    b1u, b2u = unfolded(b1g), unfolded(b2g)
+    qkv_b, out_b = b1u[:, :qkv_w], b2u[:, :width]
+    gate_b, up_b = b2u[:, width : width + ff], b2u[:, width + ff : width + 2 * ff]
+    gains_all = b1u[:, qkv_w : qkv_w + own].reshape(dn, rb, own)
+    in_order = lambda t: jnp.concatenate([t[:, :ra].reshape(-1), t[:, ra:].reshape(-1)]).astype(f32)
+    gain1, gain2 = in_order(gains_all[:, 0]), in_order(gains_all[:, 1])
+
+    def mm(h, a, b):
+        return matrix_multiply(h[:, :wa], a) + matrix_multiply(h[:, wa:], b)
+
+    def mm_back(g, a, b):
+        return jnp.concatenate([back_product(g, a), back_product(g, b)], axis=1)
+
+    c, w = lax.axis_index("ctx"), lax.axis_index("ws")
+    places = query_places(c, w, tokens, cn, wn)
+    cos, low, high = (jnp.tile(t, (mbs, 1)) for t in lane_tables(places, QUERY_HEADS))
+    x = x_low.astype(f32)
+    hn, inv1 = normalize(x, gain1)
+    hn = hn.astype(b16)
+    proj = mm(hn, qkv_a, qkv_b)
+    q = rotate_lanes(proj[:, :q_width], cos, low, high).astype(b16)
+    k = rotate_lanes(proj[:, q_width : q_width + hid], cos[:, :hid], low[:, :hid], high[:, :hid]).astype(b16)
+    v = proj[:, q_width + hid :].astype(b16)
+    kv = jnp.concatenate([k, v], axis=1)
+    (kv_all,) = gather_all([kv], [rows], [(2, 2)], 2)
+    kv_all = kv_all.reshape(cn, wn, mbs, 2, tokens // 2, 2 * hid)
+    q3 = q.reshape(mbs, tokens, q_width)
+    o3, lse = attention(q3, kv_all)
+    o_p = to_order(o3.reshape(rows, q_width))
+    x1 = x + mm(o_p, out_a, out_b)
+    h2, inv2 = normalize(x1, gain2)
+    h2 = h2.astype(b16)
+    gate = mm(h2, gate_a, gate_b)
+    up = mm(h2, up_a, up_b)
+    sig = jax.nn.sigmoid(gate)
+    silu = gate * sig
+    act = (silu * up).astype(b16)
+    out = from_order((x1 + matrix_multiply(act, down_w)).astype(b16))
+    gy = gy_low.astype(f32)
+    ga = back_product(gy_low, down_w)
+    g_gate = (ga * up * sig * (1.0 + gate * (1.0 - sig))).astype(b16)
+    g_up = (ga * silu).astype(b16)
+    gh2 = mm_back(g_gate, gate_a, gate_b) + mm_back(g_up, up_a, up_b)
+    mid, gain2_sum = normalize_back(x1, inv2, gain2, gh2)
+    gx1 = mid + gy
+    gb = gx1.astype(b16)
+    gattn = from_order(mm_back(gb, out_a, out_b).astype(b16))
+    dq, dkv = attention_back(q3, kv_all, o3, gattn.reshape(q3.shape), lse)
+
+    gb_plain = from_order(gb)
+    gy_plain = cotangent.reshape(rows, width)
+
+    def sums(h, g):
+        s = outer_sum(h, g).astype(b16)
+        return s[:wa].reshape(zn, 2, 2, 2, ra, -1), s[wa:]
+
+    def fold_sums(parts):
+        t = jnp.concatenate(parts, axis=1)
+        return (
+            t.reshape(dn, rb, fold, -1).transpose(0, 2, 1, 3).reshape(zn, 2, 2, 2, 16, -1)
+        )
+
+    d_out_a, d_out_b = sums(o_p, gb_plain)
+    d_gate_a, d_gate_b = sums(h2, g_gate)
+    d_up_a, d_up_b = sums(h2, g_up)
+    d_down = outer_sum(act, gy_plain).astype(b16).reshape(zn, 2, 2, 2, -1, width)
+    d_b2 = fold_sums([d_out_b, d_gate_b, d_up_b, jnp.zeros((dn * rb, pad2), b16)])
+
+    (dkv_own,) = scatter_all([dkv.reshape(zn, 2, 2, 2, rows, 2 * hid)], [(2, 2)], 3)
+    dk, dv = dkv_own[:, :hid], dkv_own[:, hid:].astype(b16)
+    gkr = rotate_lanes(dk, cos[:, :hid], -low[:, :hid], -high[:, :hid]).astype(b16)
+    gqr = rotate_lanes(dq.reshape(rows, q_width), cos, -low, -high).astype(b16)
+    g_qkv = jnp.concatenate([gqr, gkr, dv], axis=1)
+    ghn = mm_back(g_qkv, qkv_a, qkv_b)
+    first, gain1_sum = normalize_back(x, inv1, gain1, ghn)
+    input_grad = from_order((gx1 + first).astype(b16))
+    d_qkv_a, d_qkv_b = sums(hn, g_qkv)
+    by_owner = lambda t: jnp.concatenate([t[:wa].reshape(dn, ra), t[wa:].reshape(dn, rb)], axis=1)
+    gain_sums = jnp.stack([by_owner(gain1_sum), by_owner(gain2_sum)], axis=1).astype(b16)
+    gain_sums = jnp.pad(gain_sums, ((0, 0), (0, rb - 2), (0, pad1 - own))).reshape(dn * rb, pad1)
+    d_b1 = fold_sums([d_qkv_b, gain_sums])
+    r_out, r_gate, r_up, r_down, r_b2, r_qkv, r_b1 = scatter_all(
+        [d_out_a, d_gate_a, d_up_a, d_down, d_b2, d_qkv_a, d_b1],
+        [(1, 1), (1, 2), (1, 2), (2, 1), (1, 1), (1, 1), (1, 1)],
+        4,
+    )
+
+    def own_rows(t):
+        return t.reshape(fold, rb, -1).transpose(1, 0, 2).reshape(rb, -1)
+
+    e1, e2 = own_rows(r_b1), own_rows(r_b2)
+    whole = lambda a, b: jnp.concatenate([a, b], axis=0)
+    d_qkv = whole(r_qkv, e1[:, :qkv_w])
+    return (
+        out.reshape(inputs.shape),
+        input_grad.reshape(inputs.shape),
+        e1[0, qkv_w : qkv_w + own],
+        d_qkv[:, :q_width],
+        d_qkv[:, q_width : q_width + hid],
+        d_qkv[:, q_width + hid :],
+        whole(r_out, e2[:, :width]),
+        e1[1, qkv_w : qkv_w + own],
+        whole(r_gate, e2[:, width : width + ff]),
+        whole(r_up, e2[:, width + ff : width + 2 * ff]),
+        r_down,
+    )
+
+
 def solution(mesh):
     in_specs = (
         P(None, ("ctx", "ws"), None),
@@ -577,6 +1276,7 @@
         P(("ctx", "ws"), None),
         P(("ctx", "ws"), None),
     )
+    body = fast_device if fits_fast(mesh) else per_device
     return jax.shard_map(
-        per_device, mesh=mesh, in_specs=in_specs, out_specs=out_specs, check_vma=False
-    )
+        body, mesh=mesh, in_specs=in_specs, out_specs=out_specs, check_vma=False
+    )

time: 2660 us -> 743 us (0.28)
  blocking collectives: 734 us -> 0 us
  local copies, waits for them, and re-layouts: 670 us -> 68.4 us
  Pallas kernels: 0 us -> 578 us
  waiting for transfers between devices: 513 us -> 0 us
  other arithmetic: 239 us -> 19 us
  matrix products: 267 us -> 68 us
  starting transfers between devices: 154 us -> 0 us
  loops' own time: 42.9 us -> 0 us
    unnamed x3 -> x0, blocking collectives: 624 us -> none
    pallas_call x0 -> x6, Pallas kernels: none -> 578 us  [the longest x2 207 us: scatter_all(): pl.pallas_call(kernel, out_shape=[jax.ShapeDtypeStruct(p.shape[4:], jnp.f...]
    ppermute x32 -> x0, waiting for transfers between devices: 443 us -> none  [shifted(): return lax.ppermute(block, axis, route)]
    reshape x98 -> x18, local copies, waits for them, and re-layouts: 211 us -> 19.6 us  [the longest x6 11.5 us: fold_sums(): t.reshape(dn, rb, fold, -1).transpose(0, 2, 1, 3)]
    unnamed x40 -> x0, starting transfers between devices: 152 us -> none
    dot_general x112 -> x5, matrix products: 144 us -> 19.3 us  [the longest x3 13.1 us: from_order(): lax.dot_general(t, order, NT, preferred_element_type=f32).astype(t.dtype)]
    all_gather x4 -> x0, blocking collectives: 110 us -> none  [the longest x1 47.6 us: per_device(): lax.all_gather(value_matrix, ('ctx', 'ws'), axis=0, tiled=True)]
    unnamed x284 -> x151, local copies, waits for them, and re-layouts: 104 us -> 15 us
  transfers between devices with their start and end apart: 82 -> 0, of which waited for: 34 -> 0; matrix products, arithmetic and copies ran while one was open for 52% -> 0% of each run, Pallas kernels for 0% -> 0%
where the time goes in v1:
time: 743 us; the launch traced here: 736 us
  Pallas kernels  578 us (78%)
  local copies, waits for them, and re-layouts  68.4 us (9%)
  matrix products  68 us (9%)
  other arithmetic  19 us (3%)
    pallas_call x2, Pallas kernels, scatter_all(): pl.pallas_call(kernel, out_shape=[jax.ShapeDtypeStruct(p.shape[4:], jnp.f...  207 us
    pallas_call x2, Pallas kernels, gather_all(): pl.pallas_call(kernel, out_shape=[jax.ShapeDtypeStruct((zn, 2, 2, 2, rows...  207 us
    pallas_call x1, Pallas kernels, attention_back(): pl.pallas_call(kernel, out_shape=[jax.ShapeDtypeStruct(q.shape, jnp.float...  86.8 us
    pallas_call x1, Pallas kernels, attention(): pl.pallas_call(kernel, out_shape=[jax.ShapeDtypeStruct(q.shape, jnp.bfloa...  76.4 us
    dot_general x8, matrix products, matrix_multiply(): return jnp.dot(left, right, preferred_element_type=jnp.float32)  21.8 us
    slice x9, local copies, waits for them, and re-layouts, sums(): return (s[:wa].reshape(zn, 2, 2, 2, ra, -1), s[wa:])  16.3 us
    dot_general x5, matrix products, outer_sum(): jnp.einsum('ri,rj->ij', left, right, preferred_element_type=jnp.float32)  15.3 us
    unnamed x151, local copies, waits for them, and re-layouts  15 us

profile of v1, /device:TPU:0, one launch (start us, length us, event | category | flops | bytes accessed | tf_op | source)
XLA Modules:
  0.0 735.5 jit_solution(392700935934890861)
XLA Ops:
  0.8 3.8 fusion.6
  7.6 134.0 %shard_map.194 = (bf16[4,2,2,2,32,1920]{5,4,3,2,1,0:T(8,128)(2,1)}, bf16[4,2,2,2,16,512]{5,4,3,2,1,0:T(8,128)(2,1)}, bf16[4,2,2,2,32,1152]{5,4,3,2,1,0:T(8,128)(...) custom-call(bf16[36,1920]{1,0:T(8,128)(2,1)} %copy-done.41, ...), custom_call_target="tpu_custom_call" | custom-call | tf_op jit(solution)/shard_map/pallas_call | solution.py:689
  144.9 3.4 fusion.56
  153.6 1.3 copy.46
  156.9 2.1 copy.47
  160.3 1.7 fusion.69
  162.8 73.3 %shard_map.195 = bf16[4,2,2,2,256,768]{5,4,3,2,1,0:T(8,128)(2,1)} custom-call(bf16[256,768]{1,0:T(8,128)(2,1)} %pad_maximum_fusion.5.refs_0_), custom_call_target="tpu_custom_call" | custom-call | tf_op jit(solution)/shard_map/pallas_call | solution.py:689
  237.3 1.4 fusion.40
  238.7 76.4 %shard_map.196 = (bf16[2,128,1152]{2,1,0:T(8,128)(2,1)}, f32[2,2,6,192,128]{4,3,2,1,0:T(8,128)}) custom-call(bf16[2,128,1152]{2,1,0:T(8,128)(2,1)} %bitcast.133, bf16[8,4,2,2,64,768]{5,4,3,2,1,0:T(8,128)(2,1)} %bitcast.111), custom_call_target="tpu_custom_call" | custom-call | tf_op jit(solution)/shard_map/pallas_call | solution.py:948
  315.1 2.4 fusion.15
  317.5 1.9 fusion.54
  319.4 3.2 reshape.377
  323.6 1.4 copy-done.18
  325.0 1.5 multiply_reduce_fusion.2
  327.7 6.5 fusion.62
  334.2 1.8 fusion.60
  337.6 4.0 fusion.58
  341.5 5.7 multiply_convert_fusion.1
  347.2 1.8 fusion.136
  349.6 1.8 fusion.137
  355.7 2.1 fusion.17
  357.7 86.8 %shard_map.197 = (f32[2,128,1152]{2,1,0:T(8,128)}, bf16[8,4,2,2,64,768]{5,4,3,2,1,0:T(8,128)(2,1)}) custom-call(bf16[2,128,1152]{2,1,0:T(8,128)(2,1)} %bitcast.134, bf16[8,4,2,2,64,768]{5,4,3,2,1,0:T(8,128)(2,1)} %bitcast.112, bf16[2,128,1152]{2,1,0:T(8,128)(2,1)} %get-tuple-element.31.o_ref, bf16[2,128,1152]{2,1,0:T(8,128)(2,1)} %bitcast.152, ...), custom_call_target="tpu_custom_call" | custom-call | tf_op jit(solution)/shard_map/pallas_call | solution.py:1033
  444.6 2.1 fusion.131
  447.5 71.6 %shard_map.198 = f32[256,768]{1,0:T(8,128)} custom-call(bf16[4,2,2,2,256,768]{5,4,3,2,1,0:T(8,128)(2,1)} %bitcast.119), custom_call_target="tpu_custom_call" | custom-call | tf_op jit(solution)/shard_map/pallas_call | solution.py:818
  519.1 1.5 fusion.133
  520.6 1.5 fusion.72
  522.2 1.3 fusion.126
  524.5 2.0 fusion.37
  527.2 1.4 convolution_convert_fusion.4
  528.6 2.1 copy-done.19
  532.4 4.5 slice.392
  536.9 2.0 convolution_convert_fusion.1
  538.9 2.6 copy-done.27
  541.5 2.0 convolution_convert_fusion.2
  543.5 2.9 copy-done.1
  547.1 4.7 convolution_convert_fusion.3
  552.8 1.6 maximum_maximum_fusion
  554.4 3.7 reshape.391
  558.2 2.0 copy.69
  560.2 4.3 reshape.392.refs_4_
  564.4 6.0 slice.388
  570.4 3.1 slice.387
  573.6 1.6 slice.386
  576.0 5.1 convolution_convert_fusion
  581.1 135.8 %shard_map.199 = (f32[32,1152]{1,0:T(8,128)}, f32[32,3072]{1,0:T(8,128)}, f32[32,3072]{1,0:T(8,128)}, f32[96,1152]{1,0:T(8,128)}, f32[16,1920]{1,0:T(8,128)}, /*index=5*/f32[32,1920]{1,0:T(8,128)}, f32[16,512]{1,0:T(8,128)}) custom-call(bf16[4,2,2,2,32,1152]{5,4,3,2,1,0:T(8,128)(2,1)} %bitcast.122, bf16[4,2,2,2,32,3072]{5,4,3,2,1,0:T(8,128)(2,1)} %bitcast.117, ...), custom_call_target="tpu_custom_call" | custom-call | tf_op jit(solution)/shard_map/pallas_call | solution.py:818
  718.0 2.0 pad_maximum_fusion.4
  723.4 3.5 fusion.18
  726.9 7.5 %fusion.16 = bf16[256,1152]{1,0:T(8,128)(2,1)} fusion(s32[1152]{0:T(1024)} %copy-done.54, f32[256,1152]{1,0:T(8,128)S(1)} %copy-done.3, bf16[256,3072]{1,0:T(8,128)(2,1)} %get-tuple-element.53, bf16[3072,1152]{1,0:T(8,128)(2,1)} %bitcast.165), kind=kOutput, calls=%fused_computation.36 | convolution fusion | flops 2493628416 | bytes 10424832 | tf_op jit(solution)/shard_map/dot_general | solution.py:1106
  (250 shorter events, 36.6 us)
Async XLA Ops:
  0.7 3.9 copy-start.54
  0.7 4.8 slice-start.3
  0.7 4.8 slice-start.4
  0.7 6.1 copy-start.45
  0.7 6.1 copy-start.49
  0.7 6.1 copy-start.50
  0.7 6.2 copy-start.61
  0.7 6.2 copy-start.62
  4.6 139.7 %copy-start.14 = (bf16[644,1152]{1,0:T(8,128)(2,1)}, bf16[644,1152]{1,0:T(8,128)(2,1)S(1)}, u32[]{:S(2)}) copy-start(bf16[644,1152]{1,0:T(8,128)(2,1)S(1)} %fusion.6) | copy-start | bytes 4451332
  143.2 5.1 copy-start.23
  144.5 3.8 copy-start.33
  238.7 76.4 %copy-start.55 = (s32[1152]{0:T(1024)S(1)}, s32[1152]{0:T(1024)}, u32[]{:S(2)}) copy-start(s32[1152]{0:T(1024)} %copy-done.54) | copy-start | bytes 13828
  315.1 2.4 copy-start.9
  323.6 2.9 copy-start.16
  326.5 25.9 %copy-start.2 = (f32[256,1152]{1,0:T(8,128)}, f32[256,1152]{1,0:T(8,128)S(1)}, u32[]{:S(2)}) copy-start(f32[256,1152]{1,0:T(8,128)S(1)} %get-tuple-element.86) | copy-start | bytes 3538948
  327.2 24.9 %copy-start.51 = (f32[256]{0:T(256)}, f32[256]{0:T(256)S(1)}, u32[]{:S(2)}) copy-start(f32[256]{0:T(256)S(1)} %get-tuple-element.81) | copy-start | bytes 3076
  327.5 6.8 slice-start.7
  327.6 13.9 %copy-start.11 = (bf16[256,1152]{1,0:T(8,128)(2,1)}, bf16[256,1152]{1,0:T(8,128)(2,1)S(1)}, u32[]{:S(2)}) copy-start(bf16[256,1152]{1,0:T(8,128)(2,1)S(1)} %multiply_convert_fusion.3) | copy-start | bytes 1769476
  327.7 6.6 slice-start.8
  327.7 9.0 %slice-start.5 = ((s8[7077888]{0:T(1024)(128)(4,1)}), s8[4194304]{0:T(1024)(128)(4,1)S(1)}, s32[]{:S(2)}) async-start(s8[7077888]{0:T(1024)(128)(4,1)} %bitcast.166), calls=%async_computation.5 | async-start | bytes 8388608
  334.2 2.4 slice-start.6
  337.6 9.6 %slice-start.9 = ((s8[6291456]{0:T(1024)(128)(4,1)}), s8[4194304]{0:T(1024)(128)(4,1)S(1)}, s32[]{:S(2)}) async-start(s8[6291456]{0:T(1024)(128)(4,1)} %bitcast.174), calls=%async_computation.9 | async-start | bytes 8388608
  341.5 5.7 slice-start.10
  347.2 4.3 copy-start.28
  354.4 192.1 %copy-start.5 = (f32[256,1152]{1,0:T(8,128)}, f32[256,1152]{1,0:T(8,128)S(1)}, u32[]{:S(2)}) copy-start(f32[256,1152]{1,0:T(8,128)S(1)} %convert_add_fusion) | copy-start | bytes 3538948
  444.6 2.3 copy-start.8
  519.0 3.2 copy-start.63
  524.5 2.7 copy-start.34
  532.3 4.5 copy-start.12
  532.3 4.5 copy-start.29
  538.9 4.6 copy-start
  538.9 2.6 copy-start.27
  543.5 2.9 copy-start.1
  547.1 5.7 slice-start
  560.2 10.3 %slice-start.1 = ((s8[7077888]{0:T(1024)(128)(4,1)}), s8[2883584]{0:T(1024)(128)(4,1)S(1)}, s32[]{:S(2)}) async-start(s8[7077888]{0:T(1024)(128)(4,1)} %bitcast.114), calls=%async_computation.1 | async-start | bytes 5767168
  564.4 6.0 slice-start.2
  570.4 3.1 copy-start.22
  573.6 2.4 copy-start.35
  716.9 3.1 copy-start.43
  716.9 3.9 copy-start.44
  716.9 4.6 copy-start.48
  716.9 4.6 copy-start.32
  717.9 5.4 copy-start.58
  718.0 5.4 copy-start.6
  718.0 5.4 copy-start.31
  718.0 5.4 copy-start.60
  723.4 3.5 copy-start.3
  726.9 7.5 %copy-start.42 = (f32[96,1152]{1,0:T(8,128)S(1)}, f32[96,1152]{1,0:T(8,128)}, u32[]{:S(2)}) copy-start(f32[96,1152]{1,0:T(8,128)} %get-tuple-element.110) | copy-start | bytes 1327108
  (27 other events, 36.4 us)

commit v2 on v1

--- a/solution.py
+++ b/solution.py
@@ -556,7 +556,7 @@
 MESH = pl.DeviceIdType.MESH
 NEG = -1e30
 WIDE = 128
-VMEM_LIMIT = 60 * 1024 * 1024
+VMEM_LIMIT = 61 * 1024 * 1024
 
 
 def fits_fast(mesh):
@@ -604,11 +604,11 @@
         def col(yy, xx, lo=0, n=zn):
             return dst.at[pl.ds(lo, n), yy, xx, k]
 
-        self.local = pltpu.make_async_copy(src, own, send.at[0])
-        self.along = [
-            remote(src, own, send.at[j], recv.at[j], device(lax.rem(z + j, zn), y, x, k))
-            for j in range(1, zn)
-        ]
+        self.local = pltpu.make_async_copy(src(z), own, send.at[0])
+        self.along = []
+        for j in range(1, zn):
+            zz = lax.rem(z + j, zn)
+            self.along.append(remote(src(zz), own, send.at[j], recv.at[j], device(zz, y, x, k)))
         self.cols = [push(4, col(y, x), xn), push(5, col(y, x), yn)]
         self.corner = [push(7, col(1 - y, x, 0, hz), xn), push(8, col(y, 1 - x, hz, hz), yn)]
         self.twin_own = push(6, col(y, x), sib)
@@ -652,11 +652,15 @@
                 c.wait_send()
 
 
+def stage_step(items, stages, t):
+    for n in range(stages):
+        if 0 <= t - n < len(items):
+            items[t - n].stage(n)
+
+
 def run_stages(items, stages):
     for t in range(len(items) + stages - 1):
-        for n in range(stages):
-            if 0 <= t - n < len(items):
-                items[t - n].stage(n)
+        stage_step(items, stages, t)
 
 
 def pieces_of(rows, cols, nrow, ncol):
@@ -665,6 +669,36 @@
         for i in range(nrow)
         for j in range(ncol)
     ]
+
+
+def gather_item(ref, out, r0, nr, c0, nc, send, recv, zn):
+    src = ref.at[pl.ds(r0, nr), pl.ds(c0, nc)]
+    dst = out.at[:, :, :, :, pl.ds(r0, nr), pl.ds(c0, nc)]
+    return Gather(lambda zz: src, dst, send, recv, zn)
+
+
+class Exchange:
+    def __init__(self, src, dst, send, recv, zn):
+        z, y, x, k = place()
+        self.local = pltpu.make_async_copy(src(z), dst(z), send.at[0])
+        self.along = []
+        for j in range(1, zn):
+            zz = lax.rem(z + j, zn)
+            self.along.append(remote(src(zz), dst(z), send.at[j], recv.at[j], device(zz, y, x, k)))
+
+    def start(self):
+        self.local.start()
+        for c in self.along:
+            c.start()
+
+    def arrived(self):
+        self.local.wait()
+        for c in self.along:
+            c.wait_recv()
+
+    def sent(self):
+        for c in self.along:
+            c.wait_send()
 
 
 def gather_all(arrays, rows_used, cuts, collective_id):
@@ -681,9 +715,7 @@
         greet(zn)
         items = []
         for i, (a, (r0, nr, c0, nc)) in enumerate(work):
-            src = ins[a].at[pl.ds(r0, nr), pl.ds(c0, nc)]
-            dst = outs[a].at[:, :, :, :, pl.ds(r0, nr), pl.ds(c0, nc)]
-            items.append(Gather(src, dst, send.at[i], recv.at[i], zn))
+            items.append(gather_item(ins[a], outs[a], r0, nr, c0, nc, send.at[i], recv.at[i], zn))
         run_stages(items, 5)
 
     return pl.pallas_call(
@@ -718,15 +750,18 @@
             pltpu.VMEM((zn - 1, nr, nc), b),
         ]
 
-    def __init__(self, part, out, bufs, send, recv, zn):
+    def __init__(self, part, out, bufs, send, recv, zn, give=None):
         z, y, x, k = self.at = place()
         self.zn = zn
         hz = zn // 2
         xn, yn, sib = device(z, y, 1 - x, k), device(z, 1 - y, x, k), device(z, y, x, 1 - k)
         self.held, self.twin, self.corners, self.colsums, self.ends = held, twin, corners, colsums, ends = bufs
         self.out = out
-        self.load = pltpu.make_async_copy(part.at[:, :, :, k], held, send.at[0])
-        self.to_twin = remote(part.at[:, :, :, 1 - k], twin, send.at[1], recv.at[1], sib)
+        self.load = None
+        if give is None:
+            self.load = pltpu.make_async_copy(part.at[:, :, :, k], held, send.at[0])
+            give = part.at[:, :, :, 1 - k]
+        self.to_twin = remote(give, twin, send.at[1], recv.at[1], sib)
         self.to_corner = [
             remote(held.at[pl.ds(0, hz), 1 - y, 1 - x], corners.at[0], send.at[2], recv.at[2], yn),
             remote(held.at[pl.ds(hz, hz), 1 - y, 1 - x], corners.at[1], send.at[3], recv.at[3], xn),
@@ -738,9 +773,11 @@
         self.along = []
         for j in range(1, zn):
             zz = lax.rem(z + j, zn)
+            dst = out.at[z] if ends is None else ends.at[j - 1]
             self.along.append(
-                remote(held.at[zz, y, x], ends.at[j - 1], send.at[5 + j], recv.at[5 + j], device(zz, y, x, k))
+                remote(held.at[zz, y, x], dst, send.at[5 + j], recv.at[5 + j], device(zz, y, x, k))
             )
+        self.last = pltpu.make_async_copy(held.at[z, y, x], out.at[z], send.at[0]) if ends is None else None
 
     def stage(self, n):
         z, y, x, k = self.at
@@ -748,9 +785,11 @@
         held = self.held
         if n == 0:
             self.to_twin.start()
-            self.load.start()
+            if self.load is not None:
+                self.load.start()
         elif n == 1:
-            self.load.wait()
+            if self.load is not None:
+                self.load.wait()
             self.to_twin.wait_recv()
 
             def add(i, _):
@@ -784,13 +823,18 @@
             lax.fori_loop(0, zn, add, 0)
             for c in self.along:
                 c.start()
+            if self.last is not None:
+                self.last.start()
         elif n == 4:
             for c in self.along:
                 c.wait_recv()
-            total = held[z, y, x].astype(jnp.float32)
-            for j in range(zn - 1):
-                total = total + self.ends[j].astype(jnp.float32)
-            self.out[...] = total
+            if self.last is not None:
+                self.last.wait()
+            else:
+                total = held[z, y, x].astype(jnp.float32)
+                for j in range(zn - 1):
+                    total = total + self.ends[j].astype(jnp.float32)
+                self.out[...] = total
             for c in [self.to_twin] + self.to_corner + self.to_col + self.along:
                 c.wait_send()
 
@@ -831,224 +875,436 @@
     )(*parts)
 
 
-def head_lanes(block, head, group):
-    t = block.astype(jnp.float32)
-    if head % 2 != group % 2:
-        t = pltpu.roll(t, HEAD_SIZE, 1)
-    lane = lax.broadcasted_iota(jnp.int32, t.shape, 1)
-    return jnp.where((lane // HEAD_SIZE) == group % 2, t, 0.0)
-
-
-def spread_heads(src, dst, mb, scale):
-    per = QUERY_HEADS // KEY_VALUE_HEADS
-    rows = src.shape[1] // 2
-    for half in range(2):
-        for g in range(KEY_VALUE_HEADS):
-            for j in range(per):
-                h = per * g + j
-                block = src[mb, half * rows : (half + 1) * rows, WIDE * (h // 2) : WIDE * (h // 2) + WIDE]
-                t = head_lanes(block, h, g) * scale
-                dst[half, g, j * rows : (j + 1) * rows, :] = t.astype(dst.dtype)
-
-
-def join_heads(get, half, mb, dst, rows):
-    per = QUERY_HEADS // KEY_VALUE_HEADS
-    vals = {}
-    for g in range(KEY_VALUE_HEADS):
-        t = get(g)
-        for j in range(per):
-            vals[per * g + j] = (t[j * rows : (j + 1) * rows], g)
-    lane = lax.broadcasted_iota(jnp.int32, (rows, WIDE), 1)
-    for m in range(QUERY_HEADS // 2):
-        sides = []
-        for h in (2 * m, 2 * m + 1):
-            t, g = vals[h]
-            if h % 2 != g % 2:
-                t = pltpu.roll(t, HEAD_SIZE, 1)
-            sides.append(t)
-        both = jnp.where(lane < HEAD_SIZE, sides[0], sides[1])
-        dst[mb, half * rows : (half + 1) * rows, WIDE * m : WIDE * m + WIDE] = both.astype(dst.dtype)
-
-
-def span_of(t, c, cn):
-    half = (t > c).astype(jnp.int32)
-    j = jnp.where(half == 1, t - c - 1, t)
-    last = jnp.where(half == 1, 2 * cn - 1 - c, c)
+NT = (((1,), (1,)), ((), ()))
+PER = QUERY_HEADS // KEY_VALUE_HEADS
+HALF_GROUPS = KEY_VALUE_HEADS // 2
+HALF_HEADS = QUERY_HEADS // 2
+KV_LANES = 2 * HALF_GROUPS * HEAD_SIZE
+
+
+def lane_slot(n):
+    return n // 2, n % 2
+
+
+def key_slot(g):
+    return lane_slot(g)
+
+
+def value_slot(g):
+    return lane_slot(HALF_GROUPS + g)
+
+
+def pair_index(half, zp):
+    return zp if half == 0 else 3 - zp
+
+
+def pair_tile(src, g, half, zp):
+    tiles = []
+    for j in range(PER):
+        lo = HEAD_SIZE * (PER * g + j)
+        a = src[2 * zp, lo : lo + HEAD_SIZE, :].astype(jnp.float32)
+        b = src[2 * zp + 1, lo : lo + HEAD_SIZE, :].astype(jnp.float32)
+        low = lax.broadcasted_iota(jnp.int32, a.shape, 1) < WIDE // 2
+        if half == 0:
+            tiles.append(jnp.where(low, a, pltpu.roll(b, WIDE // 2, 1)))
+        else:
+            tiles.append(jnp.where(low, pltpu.roll(a, WIDE // 2, 1), b))
+    return jnp.concatenate(tiles, axis=1)
+
+
+def unpair(get, dst):
+    for zp in range(2):
+        for g in range(HALF_GROUPS):
+            first, second = get(g, pair_index(0, zp)), get(g, pair_index(1, zp))
+            for j in range(PER):
+                lo = HEAD_SIZE * (PER * g + j)
+                a, b = first[:, WIDE * j : WIDE * j + WIDE], second[:, WIDE * j : WIDE * j + WIDE]
+                low = lax.broadcasted_iota(jnp.int32, a.shape, 1) < WIDE // 2
+                even = jnp.where(low, a, pltpu.roll(b, WIDE // 2, 1))
+                odd = jnp.where(low, pltpu.roll(a, WIDE // 2, 1), b)
+                dst[2 * zp, lo : lo + HEAD_SIZE, :] = even.astype(dst.dtype)
+                dst[2 * zp + 1, lo : lo + HEAD_SIZE, :] = odd.astype(dst.dtype)
+
+
+def set_padded(dst, g, p, tile, side):
+    tile = tile.astype(dst.dtype)
+    dst[g, p, side * HEAD_SIZE : (side + 1) * HEAD_SIZE, :] = tile
+    dst[g, p, (1 - side) * HEAD_SIZE : (2 - side) * HEAD_SIZE, :] = jnp.zeros_like(tile)
+
+
+def walk(t, y, cn):
+    b1, b2, b3 = 3 + y, 10 + 2 * y, 22 + y
+    p = (t >= b1).astype(jnp.int32) + (t >= b2).astype(jnp.int32) + (t >= b3).astype(jnp.int32)
+    j = t - jnp.where(p == 0, 0, jnp.where(p == 1, b1, jnp.where(p == 2, b2, b3)))
+    zp = jnp.where(p < 2, p, 3 - p)
+    low = jnp.where(p < 2, 4 * zp + y, 2 * cn - 3 - 4 * zp - y)
     late = (j >= cn).astype(jnp.int32)
     src = jnp.where(late == 1, 2 * cn - 1 - j, j)
-    return half, src, late, j == last
-
-
-def hidden_bias(diag, w, rows, per, wn):
-    shape = (per * rows, wn * rows)
-    i = lax.rem(lax.broadcasted_iota(jnp.int32, shape, 0), rows)
-    key = lax.broadcasted_iota(jnp.int32, shape, 1)
-    limit = jnp.where(diag, w * rows, wn * rows)
-    return jnp.where(key <= i + limit, 0.0, NEG)
-
-
-NT = (((1,), (1,)), ((), ()))
-TN = (((0,), (0,)), ((), ()))
-
-
-def nt(a, b):
-    return lax.dot_general(a, b, NT, preferred_element_type=jnp.float32)
-
-
-def tn(a, b):
-    return lax.dot_general(a, b, TN, preferred_element_type=jnp.float32)
-
-
-def attention(q, kv):
-    mbs, tokens, qw = q.shape
-    cn, wn = kv.shape[:2]
+    return p, j, src // 2, lax.rem(src, 2), pl.multiple_of(late * HEAD_SIZE, HEAD_SIZE), j >= low
+
+
+STEPS = 38
+
+
+def visible(p, j, y, w, cn, wn, rows):
+    shape = (wn * rows, PER * WIDE)
+    lane = lax.rem(lax.broadcasted_iota(jnp.int32, shape, 1), WIDE)
+    zp = jnp.where(p < 2, p, 3 - p)
+    c = 2 * (2 * zp + lane // rows) + y
+    span = jnp.where(p < 2, c, 2 * cn - 1 - c)
+    query = span * (wn * rows) + w * rows + lax.rem(lane, rows)
+    key = j * (wn * rows) + lax.broadcasted_iota(jnp.int32, shape, 0)
+    return key <= query
+
+
+def key_block(kvg, zz, yy, late, rows, block):
+    t = kvg[zz, yy, :, :, pl.ds(late, rows), WIDE * block : WIDE * block + WIDE]
+    return t.reshape(4 * rows, WIDE)
+
+
+def turned(t):
+    return t.astype(jnp.float32).T.astype(t.dtype)
+
+
+def by_span(body, kvg, cn, rows):
+    def one(j, _):
+        late = (j >= cn).astype(jnp.int32)
+        src = jnp.where(late == 1, 2 * cn - 1 - j, j)
+        at = pl.multiple_of(late * rows, rows)
+        body(j, lambda b: key_block(kvg, src // 2, lax.rem(src, 2), at, rows, b))
+        return 0
+
+    lax.fori_loop(0, 2 * cn, one, 0)
+
+
+def gather_attend(q, kv, arrays, used, cuts, collective_id):
+    cn, wn = lax.axis_size("ctx"), lax.axis_size("ws")
+    zn = cn // 2
+    mbs, q_rows, tokens = q.shape
     rows = tokens // 2
-    per = QUERY_HEADS // KEY_VALUE_HEADS
-    hid = KEY_VALUE_HEADS * HEAD_SIZE
-    groups = range(KEY_VALUE_HEADS)
-
-    def kernel(q_ref, kv_ref, o_ref, lse_ref, qs, m_s, l_s, acc):
-        c, w = lax.axis_index("ctx"), lax.axis_index("ws")
-
-        def one(mb, _):
-            spread_heads(q_ref, qs, mb, HEAD_SIZE**-0.5)
-            m_s[...] = jnp.full(m_s.shape, NEG, jnp.float32)
-            l_s[...] = jnp.zeros(l_s.shape, jnp.float32)
-            acc[...] = jnp.zeros(acc.shape, jnp.float32)
-
-            def step(t, _):
-                half, src, late, diag = span_of(t, c, cn)
-                bias = hidden_bias(diag, w, rows, per, wn)
+    mine = q_rows // 2
+    n = len(arrays)
+    f32, b16 = jnp.float32, jnp.bfloat16
+    work = [(a, piece) for a in range(n) for piece in pieces_of(used[a], arrays[a].shape[1], *cuts[a])]
+    groups = range(HALF_GROUPS)
+
+    def kernel(*refs):
+        q_ref, kv_ref = refs[:2]
+        ins = refs[2 : 2 + n]
+        o_out, q_out, kv_out, oh_out, lse_out = refs[2 + n : 7 + n]
+        outs = refs[7 + n : 7 + 2 * n]
+        qh, kvg, oh, qpad, vt, m_s, l_s, acc, send, recv, xs, xr, ks, kr, save = refs[7 + 2 * n :]
+        greet(zn)
+        z, y, x, k = place()
+        w = 2 * x + k
+
+        def lanes_of(zz):
+            return kv_ref.at[zz // 2, :, pl.ds(pl.multiple_of(lax.rem(zz, 2) * KV_LANES, WIDE), KV_LANES)]
+
+        def heads_of(ref, zz):
+            return ref.at[zz // 2, pl.ds(pl.multiple_of(lax.rem(zz, 2) * mine, 16), mine), :]
+
+        items = [
+            gather_item(ins[a], outs[a], r0, nr, c0, nc, send.at[i], recv.at[i], zn)
+            for i, (a, (r0, nr, c0, nc)) in enumerate(work)
+        ]
+        kvx = Gather(lanes_of, kvg, ks, kr, zn)
+        qx = Exchange(lambda zz: heads_of(q_ref, zz), lambda zz: qh.at[zz], xs.at[0], xr.at[0], zn)
+        ox = Exchange(lambda zz: oh.at[zz], lambda zz: heads_of(o_out, zz), xs.at[1], xr.at[1], zn)
+        kvx.stage(0)
+        qx.start()
+        stage_step(items, 5, 0)
+        m_s[...] = jnp.full(m_s.shape, NEG, f32)
+        l_s[...] = jnp.zeros(l_s.shape, f32)
+        acc[...] = jnp.zeros(acc.shape, f32)
+        kvx.stage(1)
+        kvx.stage(2)
+        stage_step(items, 5, 1)
+        kvx.stage(3)
+        qx.arrived()
+        for half in range(2):
+            for zp in range(2):
                 for g in groups:
-                    lo = WIDE * (g // 2)
-                    kb = kv_ref[src, :, mb, late, :, lo : lo + WIDE].reshape(wn * rows, WIDE)
-                    vb = kv_ref[src, :, mb, late, :, hid + lo : hid + lo + WIDE].reshape(wn * rows, WIDE)
-                    s = nt(qs[half, g], kb) + bias
-                    m_old = m_s[half, g]
-                    m_new = jnp.maximum(m_old, jnp.max(s, axis=1, keepdims=True))
+                    set_padded(qpad, g, pair_index(half, zp), pair_tile(qh, g, half, zp), key_slot(g)[1])
+        kvx.stage(4)
+
+        def turn(j, block):
+            flat = {b: turned(block(b)) for b in sorted({value_slot(g)[0] for g in groups})}
+            for g in groups:
+                b, side = value_slot(g)
+                vt[j, g] = flat[b][side * HEAD_SIZE : (side + 1) * HEAD_SIZE]
+
+        by_span(turn, kvg, cn, rows)
+        saves = [
+            pltpu.make_async_copy(qh, q_out, save.at[0]),
+            pltpu.make_async_copy(kvg, kv_out, save.at[1]),
+        ]
+        for s in saves:
+            s.start()
+
+        def step(t, _):
+            p, j, zz, yy, late, edge = walk(t, y, cn)
+
+            def run(masked):
+                seen = visible(p, j, y, w, cn, wn, rows) if masked else None
+                for g in groups:
+                    s = jnp.dot(
+                        key_block(kvg, zz, yy, late, rows, key_slot(g)[0]), qpad[g, p], preferred_element_type=f32
+                    )
+                    if masked:
+                        s = jnp.where(seen, s, NEG)
+                    m_old = m_s[g, p]
+                    m_new = jnp.maximum(m_old, jnp.max(s, axis=0, keepdims=True))
                     alpha = jnp.exp(m_old - m_new)
-                    p = jnp.exp(s - m_new[:, :1])
-                    m_s[half, g] = m_new
-                    l_s[half, g] = l_s[half, g] * alpha + jnp.sum(p, axis=1, keepdims=True)
-                    acc[half, g] = acc[half, g] * alpha + jnp.dot(
-                        p.astype(jnp.bfloat16), vb, preferred_element_type=jnp.float32
+                    e = jnp.exp(s - m_new)
+                    m_s[g, p] = m_new
+                    l_s[g, p] = l_s[g, p] * alpha + jnp.sum(e, axis=0, keepdims=True)
+                    acc[g, p] = acc[g, p] * alpha + jnp.dot(
+                        vt[j, g], e.astype(b16), preferred_element_type=f32
                     )
-                return 0
-
-            lax.fori_loop(0, 2 * cn + 1, step, 0)
-            for half in range(2):
-                join_heads(lambda g: acc[half, g] / l_s[half, g], half, mb, o_ref, rows)
-                for g in groups:
-                    lse_ref[mb, half, g] = m_s[half, g] + jnp.log(l_s[half, g])
+
+            pl.when(edge)(lambda: run(True))
+            pl.when(jnp.logical_not(edge))(lambda: run(False))
             return 0
 
-        lax.fori_loop(0, mbs, one, 0)
-
-    stat = (2, KEY_VALUE_HEADS, per * rows, WIDE)
+        last = len(items) + 4
+        t = 0
+        for s in range(2, last):
+            upto = min(STEPS, 5 * (s - 1))
+            if t < upto:
+                lax.fori_loop(t, upto, step, 0)
+                t = upto
+                if t == STEPS:
+                    unpair(lambda g, p: acc[g, p] / l_s[g, p], oh)
+                    ox.start()
+                    saves.append(pltpu.make_async_copy(oh, oh_out, save.at[2]))
+                    saves[-1].start()
+                    lse_out[...] = m_s[...] + jnp.log(l_s[...])
+            stage_step(items, 5, s)
+        ox.arrived()
+        ox.sent()
+        qx.sent()
+        for s in saves:
+            s.wait()
+
+    stat = (HALF_GROUPS, 4, 1, PER * WIDE)
+    block = (zn, mine, tokens)
+    kv_shape = (zn, 2, 2, 2, tokens, KV_LANES)
+    any_ = pl.BlockSpec(memory_space=pl.ANY)
     return pl.pallas_call(
         kernel,
         out_shape=[
-            jax.ShapeDtypeStruct(q.shape, jnp.bfloat16),
-            jax.ShapeDtypeStruct((mbs,) + stat, jnp.float32),
+            jax.ShapeDtypeStruct(q.shape, b16),
+            jax.ShapeDtypeStruct(block, b16),
+            jax.ShapeDtypeStruct(kv_shape, b16),
+            jax.ShapeDtypeStruct(block, b16),
+            jax.ShapeDtypeStruct(stat, f32),
+        ]
+        + [
+            jax.ShapeDtypeStruct((zn, 2, 2, 2, used[a], arrays[a].shape[1]), arrays[a].dtype)
+            for a in range(n)
         ],
-        in_specs=[pl.BlockSpec(memory_space=pltpu.VMEM)] * 2,
-        out_specs=[pl.BlockSpec(memory_space=pltpu.VMEM)] * 2,
+        in_specs=[any_] * (2 + n),
+        out_specs=[any_] * 4 + [pl.BlockSpec(memory_space=pltpu.VMEM)] + [any_] * n,
         scratch_shapes=[
-            pltpu.VMEM(stat, jnp.bfloat16),
-            pltpu.VMEM(stat, jnp.float32),
-            pltpu.VMEM(stat, jnp.float32),
-            pltpu.VMEM(stat, jnp.float32),
+            pltpu.VMEM(block, b16),
+            pltpu.VMEM(kv_shape, b16),
+            pltpu.VMEM(block, b16),
+            pltpu.VMEM((HALF_GROUPS, 4, WIDE, PER * WIDE), b16),
+            pltpu.VMEM((2 * cn, HALF_GROUPS, HEAD_SIZE, wn * rows), b16),
+            pltpu.VMEM(stat, f32),
+            pltpu.VMEM(stat, f32),
+            pltpu.VMEM((HALF_GROUPS, 4, HEAD_SIZE, PER * WIDE), f32),
+            pltpu.SemaphoreType.DMA((len(work), Gather.SEMS)),
+            pltpu.SemaphoreType.DMA((len(work), Gather.SEMS)),
+            pltpu.SemaphoreType.DMA((2, zn)),
+            pltpu.SemaphoreType.DMA((2, zn)),
+            pltpu.SemaphoreType.DMA((Gather.SEMS,)),
+            pltpu.SemaphoreType.DMA((Gather.SEMS,)),
+            pltpu.SemaphoreType.DMA((3,)),
         ],
-        compiler_params=pltpu.CompilerParams(vmem_limit_bytes=VMEM_LIMIT),
-    )(q, kv)
-
-
-def attention_back(q, kv, o, do, lse):
-    mbs, tokens, qw = q.shape
-    cn, wn = kv.shape[:2]
+        compiler_params=pltpu.CompilerParams(
+            collective_id=collective_id, has_side_effects=True, vmem_limit_bytes=VMEM_LIMIT
+        ),
+    )(q, kv, *arrays)
+
+
+def scatter_attend(do, qh, kvg, oh, lse, parts, cuts, collective_id):
+    cn, wn = lax.axis_size("ctx"), lax.axis_size("ws")
+    zn = cn // 2
+    mbs, q_rows, tokens = do.shape
     rows = tokens // 2
-    per = QUERY_HEADS // KEY_VALUE_HEADS
-    hid = KEY_VALUE_HEADS * HEAD_SIZE
-    groups = range(KEY_VALUE_HEADS)
+    mine = q_rows // 2
+    n = len(parts)
+    f32, b16 = jnp.float32, jnp.bfloat16
+    work = [(a, piece) for a in range(n) for piece in pieces_of(*parts[a].shape[4:], *cuts[a])]
+    scratch = []
+    for a, (r0, nr, c0, nc) in work:
+        scratch += Scatter.scratch(zn, nr, nc)
+    groups = range(HALF_GROUPS)
     scale = HEAD_SIZE**-0.5
 
-    def kernel(q_ref, kv_ref, o_ref, do_ref, lse_ref, dq_ref, dkv_ref, qs, dos, delta, dq, dkv, stage, sems):
-        c, w = lax.axis_index("ctx"), lax.axis_index("ws")
-
-        def flush(mb):
-            return pltpu.make_async_copy(stage, dkv_ref.at[:, :, mb], sems.at[0])
-
-        for mb in range(mbs):
-            spread_heads(q_ref, qs, mb, scale)
-            spread_heads(do_ref, dos, mb, 1.0)
-            for half in range(2):
+    def kernel(*refs):
+        do_ref, qh, kvg, oh, lse_ref = refs[:5]
+        ins = refs[5 : 5 + n]
+        dq_out, dkv_out = refs[5 + n : 7 + n]
+        outs = refs[7 + n : 7 + 2 * n]
+        rest = refs[7 + 2 * n :]
+        bufs, rest = rest[: len(scratch)], rest[len(scratch) :]
+        gh, qt, dot_, qr, dor, kt, delta, dq, dkv, give, kb, send, recv, xs, xr, ks, kr = (
+            rest[:10] + (rest[10:14],) + rest[14:]
+        )
+        dqh = gh
+        greet(zn)
+        z, y, x, k = place()
+        w = 2 * x + k
+
+        def heads_of(ref, zz):
+            return ref.at[zz // 2, pl.ds(pl.multiple_of(lax.rem(zz, 2) * mine, 16), mine), :]
+
+        gx = Exchange(lambda zz: heads_of(do_ref, zz), lambda zz: gh.at[zz], xs.at[0], xr.at[0], zn)
+        dx = Exchange(lambda zz: dqh.at[zz], lambda zz: heads_of(dq_out, zz), xs.at[1], xr.at[1], zn)
+        kvx = Scatter(None, dkv_out, tuple(kb) + (None,), ks, kr, zn, give)
+        items = []
+        for i, (a, (r0, nr, c0, nc)) in enumerate(work):
+            part = ins[a].at[:, :, :, :, pl.ds(r0, nr), pl.ds(c0, nc)]
+            out = outs[a].at[pl.ds(r0, nr), pl.ds(c0, nc)]
+            items.append(Scatter(part, out, bufs[5 * i : 5 * i + 5], send.at[i], recv.at[i], zn))
+        gx.start()
+        stage_step(items, 5, 0)
+        dq[...] = jnp.zeros(dq.shape, f32)
+
+        def clear(i, _):
+            dkv[i] = jnp.zeros(dkv.shape[1:], f32)
+            return 0
+
+        lax.fori_loop(0, zn, clear, 0)
+
+        def turn(j, block):
+            flat = {b: turned(block(b)) for b in sorted({key_slot(g)[0] for g in groups})}
+            for g in groups:
+                b, side = key_slot(g)
+                kt[j, g] = flat[b][side * HEAD_SIZE : (side + 1) * HEAD_SIZE]
+
+        by_span(turn, kvg, cn, rows)
+        stage_step(items, 5, 1)
+        gx.arrived()
+        for half in range(2):
+            for zp in range(2):
+                p = pair_index(half, zp)
                 for g in groups:
-                    for j in range(per):
-                        h = per * g + j
-                        lo = WIDE * (h // 2)
-                        block = o_ref[mb, half * rows : (half + 1) * rows, lo : lo + WIDE]
-                        oh = head_lanes(block, h, g)
-                        d = jnp.sum(oh * dos[half, g, j * rows : (j + 1) * rows, :].astype(jnp.float32), axis=1, keepdims=True)
-                        delta[half, g, j * rows : (j + 1) * rows, :] = jnp.broadcast_to(d, (rows, WIDE))
-            dq[...] = jnp.zeros(dq.shape, jnp.float32)
-
-            def clear(i, _):
-                dkv[i] = jnp.zeros(dkv.shape[1:], jnp.float32)
-                return 0
-
-            lax.fori_loop(0, cn, clear, 0)
-
-            def step(t, _):
-                half, src, late, diag = span_of(t, c, cn)
-                bias = hidden_bias(diag, w, rows, per, wn)
+                    g_tile = pair_tile(gh, g, half, zp)
+                    o_tile = pair_tile(oh, g, half, zp)
+                    delta[g, p] = jnp.sum(g_tile * o_tile, axis=0, keepdims=True)
+                    set_padded(qt, g, p, pair_tile(qh, g, half, zp), key_slot(g)[1])
+                    set_padded(dot_, g, p, g_tile, value_slot(g)[1])
+                    qr[g, p] = turned(qt[g, p])
+                    dor[g, p] = turned(dot_[g, p])
+
+        def step(t, _):
+            p, j, zz, yy, late, edge = walk(t, y, cn)
+
+            def run(masked):
+                seen = visible(p, j, y, w, cn, wn, rows) if masked else None
+                blocks = [key_block(kvg, zz, yy, late, rows, b) for b in range(KV_LANES // WIDE)]
+                sums = [None] * len(blocks)
+
+                def put(b, v):
+                    sums[b] = v if sums[b] is None else sums[b] + v
+
                 for g in groups:
-                    lo = WIDE * (g // 2)
-                    kb = kv_ref[src, :, mb, late, :, lo : lo + WIDE].reshape(wn * rows, WIDE)
-                    vb = kv_ref[src, :, mb, late, :, hid + lo : hid + lo + WIDE].reshape(wn * rows, WIDE)
-                    qg, dog = qs[half, g], dos[half, g]
-                    p = jnp.exp(nt(qg, kb) + bias - lse_ref[mb, half, g][:, :1])
-                    ds = (p * (nt(dog, vb) - delta[half, g][:, :1])).astype(jnp.bfloat16)
-                    dq[half, g] += jnp.dot(ds, kb, preferred_element_type=jnp.float32)
-                    dk = tn(ds, qg).reshape(wn, rows, WIDE)
-                    dv = tn(p.astype(jnp.bfloat16), dog).reshape(wn, rows, WIDE)
-                    dkv[src, :, late, :, lo : lo + WIDE] += dk
-                    dkv[src, :, late, :, hid + lo : hid + lo + WIDE] += dv
-                return 0
-
-            lax.fori_loop(0, 2 * cn + 1, step, 0)
-            for half in range(2):
-                join_heads(lambda g: dq[half, g] * scale, half, mb, dq_ref, rows)
-            if mb > 0:
-                flush(mb - 1).wait()
-
-            def pack(i, _):
-                stage[i] = dkv[i].astype(jnp.bfloat16)
-                return 0
-
-            lax.fori_loop(0, cn, pack, 0)
-            flush(mb).start()
-        flush(mbs - 1).wait()
-
-    stat = (2, KEY_VALUE_HEADS, per * rows, WIDE)
+                    s = jnp.dot(blocks[key_slot(g)[0]], qt[g, p], preferred_element_type=f32)
+                    if masked:
+                        s = jnp.where(seen, s, NEG)
+                    e = jnp.exp(s - lse_ref[g, p])
+                    dp = jnp.dot(blocks[value_slot(g)[0]], dot_[g, p], preferred_element_type=f32)
+                    ds = (e * (dp - delta[g, p])).astype(b16)
+                    put(value_slot(g)[0], jnp.dot(e.astype(b16), dor[g, p], preferred_element_type=f32))
+                    put(key_slot(g)[0], jnp.dot(ds, qr[g, p], preferred_element_type=f32))
+                    dq[g, p] += jnp.dot(kt[j, g], ds, preferred_element_type=f32)
+                for b, v in enumerate(sums):
+                    dkv[zz, yy, :, :, pl.ds(late, rows), WIDE * b : WIDE * b + WIDE] += v.reshape(
+                        2, 2, rows, WIDE
+                    )
+
+            pl.when(edge)(lambda: run(True))
+            pl.when(jnp.logical_not(edge))(lambda: run(False))
+            return 0
+
+        last = len(items) + 4
+        t = 0
+        kv_stage = 0
+        for s in range(2, last):
+            upto = min(STEPS, 6 * (s - 1))
+            if t < upto:
+                lax.fori_loop(t, upto, step, 0)
+                t = upto
+                if t == STEPS:
+
+                    def pack(i, _):
+                        for yy in range(2):
+                            for xx in range(2):
+                                kb[0][i, yy, xx] = dkv[i, yy, xx, k].astype(b16)
+                                give[i, yy, xx] = dkv[i, yy, xx, 1 - k].astype(b16)
+                        return 0
+
+                    lax.fori_loop(0, zn, pack, 0)
+                    kvx.stage(0)
+                    unpair(lambda g, p: dq[g, p] * scale, dqh)
+                    dx.start()
+                    kv_stage = 1
+            elif t == STEPS and kv_stage < 5:
+                kvx.stage(kv_stage)
+                kv_stage += 1
+            stage_step(items, 5, s)
+        while kv_stage < 5:
+            kvx.stage(kv_stage)
+            kv_stage += 1
+        dx.arrived()
+        dx.sent()
+        gx.sent()
+
+    stat = (HALF_GROUPS, 4, 1, PER * WIDE)
+    block = (zn, mine, tokens)
+    tile = (HALF_GROUPS, 4, WIDE, PER * WIDE)
+    tile_t = (HALF_GROUPS, 4, PER * WIDE, WIDE)
+    any_ = pl.BlockSpec(memory_space=pl.ANY)
+    vmem = pl.BlockSpec(memory_space=pltpu.VMEM)
     return pl.pallas_call(
         kernel,
         out_shape=[
-            jax.ShapeDtypeStruct(q.shape, jnp.float32),
-            jax.ShapeDtypeStruct(kv.shape, jnp.bfloat16),
+            jax.ShapeDtypeStruct(do.shape, b16),
+            jax.ShapeDtypeStruct((zn, tokens, KV_LANES), b16),
+        ]
+        + [jax.ShapeDtypeStruct(p.shape[4:], f32) for p in parts],
+        in_specs=[any_, vmem, vmem, vmem, vmem] + [any_] * n,
+        out_specs=[any_, any_] + [vmem] * n,
+        scratch_shapes=scratch
+        + [
+            pltpu.VMEM(block, b16),
+            pltpu.VMEM(tile, b16),
+            pltpu.VMEM(tile, b16),
+            pltpu.VMEM(tile_t, b16),
+            pltpu.VMEM(tile_t, b16),
+            pltpu.VMEM((2 * cn, HALF_GROUPS, HEAD_SIZE, wn * rows), b16),
+            pltpu.VMEM(stat, f32),
+            pltpu.VMEM((HALF_GROUPS, 4, HEAD_SIZE, PER * WIDE), f32),
+            pltpu.VMEM((zn, 2, 2, 2, tokens, KV_LANES), f32),
+            pltpu.VMEM((zn, 2, 2, tokens, KV_LANES), b16),
+        ]
+        + Scatter.scratch(zn, tokens, KV_LANES)[:4]
+        + [
+            pltpu.SemaphoreType.DMA((len(work), Scatter.SEMS)),
+            pltpu.SemaphoreType.DMA((len(work), Scatter.SEMS)),
+            pltpu.SemaphoreType.DMA((2, zn)),
+            pltpu.SemaphoreType.DMA((2, zn)),
+            pltpu.SemaphoreType.DMA((Scatter.SEMS,)),
+            pltpu.SemaphoreType.DMA((Scatter.SEMS,)),
         ],
-        in_specs=[pl.BlockSpec(memory_space=pltpu.VMEM)] * 5,
-        out_specs=[pl.BlockSpec(memory_space=pltpu.VMEM), pl.BlockSpec(memory_space=pl.ANY)],
-        scratch_shapes=[
-            pltpu.VMEM(stat, jnp.bfloat16),
-            pltpu.VMEM(stat, jnp.bfloat16),
-            pltpu.VMEM(stat, jnp.float32),
-            pltpu.VMEM(stat, jnp.float32),
-            pltpu.VMEM((cn, wn, 2, rows, 2 * hid), jnp.float32),
-            pltpu.VMEM((cn, wn, 2, rows, 2 * hid), jnp.bfloat16),
-            pltpu.SemaphoreType.DMA((1,)),
-        ],
-        compiler_params=pltpu.CompilerParams(vmem_limit_bytes=VMEM_LIMIT),
-    )(q, kv, o, do, lse)
+        compiler_params=pltpu.CompilerParams(
+            collective_id=collective_id, has_side_effects=True, vmem_limit_bytes=VMEM_LIMIT
+        ),
+    )(do, qh, kvg, oh, lse, *parts)
 
 
 def rotate_lanes(t, cos, low, high):
@@ -1056,14 +1312,20 @@
     return t * cos + jnp.roll(t, -quarter, axis=-1) * low + jnp.roll(t, quarter, axis=-1) * high
 
 
-def lane_tables(positions, heads):
+def lane_tables(positions):
     quarter = HEAD_SIZE // 2
     frequency = 10000.0 ** (-2.0 * jnp.arange(quarter, dtype=jnp.float32) / HEAD_SIZE)
     angles = positions.astype(jnp.float32)[:, None] * frequency[None, :]
     cos, sin = jnp.cos(angles), jnp.sin(angles)
     none = jnp.zeros_like(sin)
-    full = lambda a, b: jnp.tile(jnp.concatenate([a, b], axis=1), (1, heads))
-    return full(cos, cos), full(-sin, none), full(none, sin)
+
+    def full(a, b, still):
+        head = jnp.concatenate([a, b], axis=1)
+        keys = jnp.tile(head, (1, HALF_GROUPS))
+        still = jnp.full_like(keys, still)
+        return jnp.concatenate([keys, still, keys, still, jnp.tile(head, (1, QUERY_HEADS))], axis=1)
+
+    return full(cos, cos, 1.0), full(-sin, none, 0.0), full(none, sin, 0.0)
 
 
 def fast_device(
@@ -1121,7 +1383,17 @@
     )
     x_low, gy_low = moved[:rows], moved[rows : 2 * rows]
     out_p, down_p = moved[2 * rows : 2 * rows + own], moved[2 * rows + own :]
-    qkv = jnp.concatenate([query_weight, key_matrix, value_matrix], axis=1)
+    half_hid = hid // 2
+    qkv = jnp.concatenate(
+        [
+            key_matrix[:, :half_hid],
+            value_matrix[:, :half_hid],
+            key_matrix[:, half_hid:],
+            value_matrix[:, half_hid:],
+            query_weight,
+        ],
+        axis=1,
+    )
     gains = jnp.stack([attn_gain, ffn_gain])
     gains = jnp.pad(gains, ((0, rb - 2), (0, pad1 - own)))
     b1 = folded(jnp.concatenate([qkv[ra:], gains], axis=1))
@@ -1130,20 +1402,15 @@
             jnp.concatenate([out_p[ra:], gate_weight[ra:], up_weight[ra:]], axis=1), ((0, 0), (0, pad2))
         )
     )
-    arrays = [qkv, b1, out_p, gate_weight, up_weight, down_p, b2]
-    used = [ra, 16, ra, ra, ra, down_p.shape[0], 16]
-    cuts = [(1, 1), (1, 1), (1, 1), (1, 2), (1, 2), (2, 1), (1, 1)]
-    qkv_a, b1g, out_a, gate_a, up_a, down_a, b2g = gather_all(arrays, used, cuts, 1)
+    qkv_a, b1g = gather_all([qkv, b1], [ra, 16], [(1, 1), (1, 1)], 1)
 
     def unfolded(t):
         cols = t.shape[-1]
         return t.reshape(dn, fold, rb, cols).transpose(0, 2, 1, 3).reshape(dn * rb, fold * cols)
 
     flat = lambda t: t.reshape(-1, t.shape[-1])
-    qkv_a, out_a, gate_a, up_a, down_w = map(flat, (qkv_a, out_a, gate_a, up_a, down_a))
-    b1u, b2u = unfolded(b1g), unfolded(b2g)
-    qkv_b, out_b = b1u[:, :qkv_w], b2u[:, :width]
-    gate_b, up_b = b2u[:, width : width + ff], b2u[:, width + ff : width + 2 * ff]
+    qkv_a, b1u = flat(qkv_a), unfolded(b1g)
+    qkv_b = b1u[:, :qkv_w]
     gains_all = b1u[:, qkv_w : qkv_w + own].reshape(dn, rb, own)
     in_order = lambda t: jnp.concatenate([t[:, :ra].reshape(-1), t[:, ra:].reshape(-1)]).astype(f32)
     gain1, gain2 = in_order(gains_all[:, 0]), in_order(gains_all[:, 1])
@@ -1156,20 +1423,27 @@
 
     c, w = lax.axis_index("ctx"), lax.axis_index("ws")
     places = query_places(c, w, tokens, cn, wn)
-    cos, low, high = (jnp.tile(t, (mbs, 1)) for t in lane_tables(places, QUERY_HEADS))
+    cos, low, high = (jnp.tile(t, (mbs, 1)) for t in lane_tables(places))
     x = x_low.astype(f32)
     hn, inv1 = normalize(x, gain1)
     hn = hn.astype(b16)
-    proj = mm(hn, qkv_a, qkv_b)
-    q = rotate_lanes(proj[:, :q_width], cos, low, high).astype(b16)
-    k = rotate_lanes(proj[:, q_width : q_width + hid], cos[:, :hid], low[:, :hid], high[:, :hid]).astype(b16)
-    v = proj[:, q_width + hid :].astype(b16)
-    kv = jnp.concatenate([k, v], axis=1)
-    (kv_all,) = gather_all([kv], [rows], [(2, 2)], 2)
-    kv_all = kv_all.reshape(cn, wn, mbs, 2, tokens // 2, 2 * hid)
-    q3 = q.reshape(mbs, tokens, q_width)
-    o3, lse = attention(q3, kv_all)
-    o_p = to_order(o3.reshape(rows, q_width))
+    proj = rotate_lanes(mm(hn, qkv_a, qkv_b), cos, low, high)
+    kv = proj[:, : 2 * hid].astype(b16).reshape(mbs, tokens, 2 * hid)
+    q = (proj[:, 2 * hid :] * HEAD_SIZE**-0.5).astype(b16)
+    q = q.reshape(mbs, tokens, q_width).transpose(0, 2, 1)
+    o_t, qh, kvg, oh, lse, out_a, gate_a, up_a, down_a, b2g = gather_attend(
+        q,
+        kv,
+        [out_p, gate_weight, up_weight, down_p, b2],
+        [ra, ra, ra, down_p.shape[0], 16],
+        [(1, 1), (1, 2), (1, 2), (2, 1), (1, 1)],
+        2,
+    )
+    out_a, gate_a, up_a, down_w = map(flat, (out_a, gate_a, up_a, down_a))
+    b2u = unfolded(b2g)
+    out_b = b2u[:, :width]
+    gate_b, up_b = b2u[:, width : width + ff], b2u[:, width + ff : width + 2 * ff]
+    o_p = to_order(o_t.transpose(0, 2, 1).reshape(rows, q_width))
     x1 = x + mm(o_p, out_a, out_b)
     h2, inv2 = normalize(x1, gain2)
     h2 = h2.astype(b16)
@@ -1188,14 +1462,12 @@
     gx1 = mid + gy
     gb = gx1.astype(b16)
     gattn = from_order(mm_back(gb, out_a, out_b).astype(b16))
-    dq, dkv = attention_back(q3, kv_all, o3, gattn.reshape(q3.shape), lse)
-
     gb_plain = from_order(gb)
     gy_plain = cotangent.reshape(rows, width)
 
     def sums(h, g):
-        s = outer_sum(h, g).astype(b16)
-        return s[:wa].reshape(zn, 2, 2, 2, ra, -1), s[wa:]
+        first, rest = outer_sum(h[:, :wa], g), outer_sum(h[:, wa:], g)
+        return first.astype(b16).reshape(zn, 2, 2, 2, ra, -1), rest.astype(b16)
 
     def fold_sums(parts):
         t = jnp.concatenate(parts, axis=1)
@@ -1209,11 +1481,19 @@
     d_down = outer_sum(act, gy_plain).astype(b16).reshape(zn, 2, 2, 2, -1, width)
     d_b2 = fold_sums([d_out_b, d_gate_b, d_up_b, jnp.zeros((dn * rb, pad2), b16)])
 
-    (dkv_own,) = scatter_all([dkv.reshape(zn, 2, 2, 2, rows, 2 * hid)], [(2, 2)], 3)
-    dk, dv = dkv_own[:, :hid], dkv_own[:, hid:].astype(b16)
-    gkr = rotate_lanes(dk, cos[:, :hid], -low[:, :hid], -high[:, :hid]).astype(b16)
-    gqr = rotate_lanes(dq.reshape(rows, q_width), cos, -low, -high).astype(b16)
-    g_qkv = jnp.concatenate([gqr, gkr, dv], axis=1)
+    dq, dkv, r_out, r_gate, r_up, r_down, r_b2 = scatter_attend(
+        gattn.reshape(mbs, tokens, q_width).transpose(0, 2, 1),
+        qh,
+        kvg,
+        oh,
+        lse,
+        [d_out_a, d_gate_a, d_up_a, d_down, d_b2],
+        [(1, 1), (1, 2), (1, 2), (2, 1), (1, 1)],
+        3,
+    )
+    dkv = dkv.reshape(mbs, 2, tokens, hid).transpose(0, 2, 1, 3).reshape(rows, 2 * hid)
+    dq = dq.transpose(0, 2, 1).reshape(rows, q_width)
+    g_qkv = rotate_lanes(jnp.concatenate([dkv, dq], axis=1).astype(f32), cos, -low, -high).astype(b16)
     ghn = mm_back(g_qkv, qkv_a, qkv_b)
     first, gain1_sum = normalize_back(x, inv1, gain1, ghn)
     input_grad = from_order((gx1 + first).astype(b16))
@@ -1222,11 +1502,7 @@
     gain_sums = jnp.stack([by_owner(gain1_sum), by_owner(gain2_sum)], axis=1).astype(b16)
     gain_sums = jnp.pad(gain_sums, ((0, 0), (0, rb - 2), (0, pad1 - own))).reshape(dn * rb, pad1)
     d_b1 = fold_sums([d_qkv_b, gain_sums])
-    r_out, r_gate, r_up, r_down, r_b2, r_qkv, r_b1 = scatter_all(
-        [d_out_a, d_gate_a, d_up_a, d_down, d_b2, d_qkv_a, d_b1],
-        [(1, 1), (1, 2), (1, 2), (2, 1), (1, 1), (1, 1), (1, 1)],
-        4,
-    )
+    r_qkv, r_b1 = scatter_all([d_qkv_a, d_b1], [(1, 1), (1, 1)], 4)
 
     def own_rows(t):
         return t.reshape(fold, rb, -1).transpose(1, 0, 2).reshape(rb, -1)
@@ -1238,9 +1514,9 @@
         out.reshape(inputs.shape),
         input_grad.reshape(inputs.shape),
         e1[0, qkv_w : qkv_w + own],
-        d_qkv[:, :q_width],
-        d_qkv[:, q_width : q_width + hid],
-        d_qkv[:, q_width + hid :],
+        d_qkv[:, 2 * hid :],
+        jnp.concatenate([d_qkv[:, :half_hid], d_qkv[:, hid : hid + half_hid]], axis=1),
+        jnp.concatenate([d_qkv[:, half_hid:hid], d_qkv[:, hid + half_hid : 2 * hid]], axis=1),
         whole(r_out, e2[:, :width]),
         e1[1, qkv_w : qkv_w + own],
         whole(r_gate, e2[:, width : width + ff]),

time: 743 us -> 560 us (0.75)
  Pallas kernels: 578 us -> 369 us
  local copies, waits for them, and re-layouts: 68.4 us -> 79.6 us
  other arithmetic: 19 us -> 27.1 us
    pallas_call x2 -> x1, Pallas kernels: 207 us -> 37.5 us  [gather_all(): pl.pallas_call(kernel, out_shape=[jax.ShapeDtypeStruct((zn, 2, 2, 2, rows...]
    pallas_call x2 -> x1, Pallas kernels: 207 us -> 41.8 us  [scatter_all(): pl.pallas_call(kernel, out_shape=[jax.ShapeDtypeStruct(p.shape[4:], jnp.f...]
    pallas_call x2, Pallas kernels: 163 us -> 290 us  [the longest x1 145 us: scatter_attend(): pl.pallas_call(kernel, out_shape=[jax.ShapeDtypeStruct(do.shape, b16), ja...]
    concatenate x3 -> x12, local copies, waits for them, and re-layouts: 0.02 us -> 16.6 us  [the longest x5 6.59 us: full(): jnp.concatenate([keys, still, keys, still, jnp.tile(head, (1, QUERY_HEADS...]
    slice x11 -> x2, local copies, waits for them, and re-layouts: 16.3 us -> 2.81 us  [the longest x1 1.92 us: fast_device(): kv = proj[:, :2 * hid].astype(b16).reshape(mbs, tokens, 2 * hid)]
    another operation x9 -> x6, local copies, waits for them, and re-layouts: 8.89 us -> 0.18 us  [the longest x3 0.15 us: full(): jnp.tile(head, (1, QUERY_HEADS))]
    dot_general x5 -> x9, matrix products: 15.3 us -> 23.5 us  [outer_sum(): jnp.einsum('ri,rj->ij', left, right, preferred_element_type=jnp.float32)]
    unnamed x151 -> x134, local copies, waits for them, and re-layouts: 15 us -> 17 us
where the time goes in v2:
time: 560 us; the launch traced here: 551 us
  Pallas kernels  369 us (66%)
  local copies, waits for them, and re-layouts  79.6 us (14%)
  matrix products  73.6 us (13%)
  other arithmetic  27.1 us (5%)
    pallas_call x1, Pallas kernels, scatter_attend(): pl.pallas_call(kernel, out_shape=[jax.ShapeDtypeStruct(do.shape, b16), ja...  145 us
    pallas_call x1, Pallas kernels, gather_attend(): pl.pallas_call(kernel, out_shape=[jax.ShapeDtypeStruct(q.shape, b16), jax...  145 us
    pallas_call x1, Pallas kernels, scatter_all(): pl.pallas_call(kernel, out_shape=[jax.ShapeDtypeStruct(p.shape[4:], jnp.f...  41.8 us
    pallas_call x1, Pallas kernels, gather_all(): pl.pallas_call(kernel, out_shape=[jax.ShapeDtypeStruct((zn, 2, 2, 2, rows...  37.5 us
    dot_general x9, matrix products, outer_sum(): jnp.einsum('ri,rj->ij', left, right, preferred_element_type=jnp.float32)  23.5 us
    reshape x6, local copies, waits for them, and re-layouts, fold_sums(): t.reshape(dn, rb, fold, -1).transpose(0, 2, 1, 3)  18.9 us
    dot_general x8, matrix products, matrix_multiply(): return jnp.dot(left, right, preferred_element_type=jnp.float32)  17.1 us
    unnamed x134, local copies, waits for them, and re-layouts  17 us

profile of v2, /device:TPU:0, one launch (start us, length us, event | category | flops | bytes accessed | tf_op | source)
XLA Modules:
  0.0 551.4 jit_solution(7066980484549690362)
XLA Ops:
  4.1 37.5 %shard_map.194 = (bf16[4,2,2,2,32,1920]{5,4,3,2,1,0:T(8,128)(2,1)}, bf16[4,2,2,2,16,512]{5,4,3,2,1,0:T(8,128)(2,1)}) custom-call(bf16[36,1920]{1,0:T(8,128)(2,1)} %copy-done.36, bf16[16,512]{1,0:T(8,128)(2,1)} %reshape.497.refs_1_), custom_call_target="tpu_custom_call" | custom-call | tf_op jit(solution)/shard_map/pallas_call | solution.py:721
  43.6 2.4 fusion.6
  48.9 2.6 fusion.138
  55.3 1.5 copy.62
  60.4 2.5 copy.63
  66.4 2.5 copy.96
  68.9 3.3 fusion.22
  72.2 1.3 copy-done.17
  74.7 1.9 slice.409
  78.7 144.7 %shard_map.195 = (bf16[2,1152,128]{2,1,0:T(8,128)(2,1)}, bf16[4,576,128]{2,1,0:T(8,128)(2,1)}, bf16[4,2,2,2,128,384]{5,4,3,2,1,0:T(8,128)(2,1)}, bf16[4,576,128]...) custom-call(bf16[2,1152,128]{2,1,0:T(8,128)(2,1)} %bitcast.180, ...), custom_call_target="tpu_custom_call" | custom-call | tf_op jit(solution)/shard_map/pallas_call | solution.py:1094
  223.3 3.2 reshape.508
  232.7 6.4 %fusion.74 = f32[256,3072]{1,0:T(8,128)} fusion(bf16[1024,3072]{1,0:T(8,128)(2,1)} %bitcast.225, bf16[256,1152]{1,0:T(8,128)(2,1)S(1)} %multiply_convert_fusion.3), kind=kOutput, calls=%fused_computation.131 | convolution fusion | flops 1610612736 | bytes 9961472 | tf_op jit(solution)/shard_map/dot_general | solution.py:33
  239.2 1.9 fusion.72
  242.6 3.9 fusion.59
  246.5 5.3 multiply_convert_fusion.1
  251.9 2.0 fusion.143
  254.5 2.0 fusion.144
  261.3 1.7 maximum_maximum_fusion
  263.0 4.5 reshape.519
  267.4 3.7 copy.105
  271.1 4.5 reshape.520.refs_9_
  275.6 6.0 %convolution_convert_fusion.1 = bf16[1024,3072]{1,0:T(8,128)(2,1)} fusion(bf16[256,3072]{1,0:T(8,128)(2,1)} %copy-done.20, bf16[256,1152]{1,0:T(8,128)(2,1)S(1)} %multiply_convert_fusion.3), kind=kOutput, calls=%fused_computation.1 | convolution fusion | flops 1613758464 | bytes 8388608 | tf_op jit(solution)/shard_map/ri,rj->ij/dot_general | solution.py:37
  281.6 4.5 convolution_convert_fusion.2
  286.2 2.3 convolution_convert_fusion.4
  288.4 5.2 convolution_convert_fusion
  298.2 144.8 %shard_map.196 = (bf16[2,1152,128]{2,1,0:T(8,128)(2,1)}, bf16[4,128,384]{2,1,0:T(8,128)(2,1)}, f32[32,1152]{1,0:T(8,128)}, f32[32,3072]{1,0:T(8,128)}, f32[32,30...) custom-call(bf16[2,1152,128]{2,1,0:T(8,128)(2,1)} %bitcast.181, ...), custom_call_target="tpu_custom_call" | custom-call | tf_op jit(solution)/shard_map/pallas_call | solution.py:1273
  444.1 1.9 pad_maximum_fusion.3
  446.0 1.8 pad_maximum_fusion.2
  451.2 2.5 fusion.136
  453.8 2.9 copy.77
  456.6 2.8 copy.81
  460.2 1.6 copy.78
  461.8 1.6 copy.80
  464.7 1.4 neg.22
  466.1 1.3 neg.23
  467.5 1.8 fusion.30
  469.3 1.5 copy.82
  470.9 3.8 fusion.145
  475.3 2.7 fusion.25
  481.6 2.2 reshape.531
  483.8 2.1 copy.106
  485.9 2.0 reshape.532.refs_1_
  487.9 3.2 convolution_convert_fusion.3
  491.1 41.8 %shard_map.197 = (f32[32,1920]{1,0:T(8,128)}, f32[16,512]{1,0:T(8,128)}) custom-call(bf16[4,2,2,2,32,1920]{5,4,3,2,1,0:T(8,128)(2,1)} %bitcast.153, bf16[4,2,2,2,16,512]{5,4,3,2,1,0:T(8,128)(2,1)} %reshape.532.refs_1_), custom_call_target="tpu_custom_call" | custom-call | tf_op jit(solution)/shard_map/pallas_call | solution.py:862
  534.6 1.4 fusion.85
  536.8 1.6 fusion.79
  538.9 3.7 fusion.19
  542.6 7.5 %fusion.16 = bf16[256,1152]{1,0:T(8,128)(2,1)} fusion(s32[1152]{0:T(1024)S(1)} %copy-done.45, f32[256,1152]{1,0:T(8,128)S(1)} %get-tuple-element.89, bf16[256,3072]{1,0:T(8,128)(2,1)} %get-tuple-element.59, bf16[3072,1152]{1,0:T(8,128)(2,1)} %bitcast.217), kind=kOutput, calls=%fused_computation.44 | convolution fusion | flops 2493628416 | bytes 10424832 | tf_op jit(solution)/shard_map/dot_general | solution.py:1368
  (241 shorter events, 53.7 us)
Async XLA Ops:
  1.5 42.0 %copy-start.37 = (bf16[2,128,1152]{2,1,0:T(8,128)(2,1)S(1)}, bf16[2,128,1152]{2,1,0:T(8,128)(2,1)}, u32[]{:S(2)}) copy-start(bf16[2,128,1152]{2,1,0:T(8,128)(2,1)} %param.21) | copy-start | bytes 1769476
  1.5 42.0 %copy-start.48 = (bf16[2,128,1152]{2,1,0:T(8,128)(2,1)S(1)}, bf16[2,128,1152]{2,1,0:T(8,128)(2,1)}, u32[]{:S(2)}) copy-start(bf16[2,128,1152]{2,1,0:T(8,128)(2,1)} %param.11) | copy-start | bytes 1769476
  1.6 42.0 %copy-start.49 = (bf16[96,1152]{1,0:T(8,128)(2,1)S(1)}, bf16[96,1152]{1,0:T(8,128)(2,1)}, u32[]{:S(2)}) copy-start(bf16[96,1152]{1,0:T(8,128)(2,1)} %param.20) | copy-start | bytes 663556
  1.6 42.0 %copy-start.50 = (bf16[36,1152]{1,0:T(8,128)(2,1)S(1)}, bf16[36,1152]{1,0:T(8,128)(2,1)}, u32[]{:S(2)}) copy-start(bf16[36,1152]{1,0:T(8,128)(2,1)} %param.16) | copy-start | bytes 248836
  43.1 5.3 copy-start.23
  43.5 252.3 %copy-start.44 = (s32[1152]{0:T(1024)}, s32[1152]{0:T(1024)S(1)}, u32[]{:S(2)}) copy-start(s32[1152]{0:T(1024)S(1)} %fusion.109) | copy-start | bytes 13828
  43.6 3.6 copy-start.47
  46.0 2.5 copy-start.12
  56.8 12.0 %copy-start.6 = (f32[128,1920]{1,0:T(8,128)}, f32[128,1920]{1,0:T(8,128)S(1)}, u32[]{:S(2)}) copy-start(f32[128,1920]{1,0:T(8,128)S(1)} %copy.62) | copy-start | bytes 2949124
  73.5 3.1 copy-start.13
  73.5 3.8 slice-start
  73.5 3.8 slice-start.1
  73.5 3.8 slice-start.2
  227.6 3.7 copy-start.21
  232.5 6.6 %slice-start.5 = ((s8[6291456]{0:T(1024)(128)(4,1)}), s8[4194304]{0:T(1024)(128)(4,1)S(1)}, s32[]{:S(2)}) async-start(s8[6291456]{0:T(1024)(128)(4,1)} %bitcast.221), calls=%async_computation.5 | async-start | bytes 8388608
  232.7 6.4 %slice-start.6 = ((s8[6291456]{0:T(1024)(128)(4,1)}), s8[2097152]{0:T(1024)(128)(4,1)S(1)}, s32[]{:S(2)}) async-start(s8[6291456]{0:T(1024)(128)(4,1)} %bitcast.221), calls=%async_computation.6 | async-start | bytes 4194304
  232.7 8.9 %slice-start.3 = ((s8[7077888]{0:T(1024)(128)(4,1)}), s8[4194304]{0:T(1024)(128)(4,1)S(1)}, s32[]{:S(2)}) async-start(s8[7077888]{0:T(1024)(128)(4,1)} %bitcast.218), calls=%async_computation.3 | async-start | bytes 8388608
  239.2 2.5 slice-start.4
  242.6 9.3 %slice-start.7 = ((s8[6291456]{0:T(1024)(128)(4,1)}), s8[4194304]{0:T(1024)(128)(4,1)S(1)}, s32[]{:S(2)}) async-start(s8[6291456]{0:T(1024)(128)(4,1)} %bitcast.226), calls=%async_computation.7 | async-start | bytes 8388608
  246.5 5.3 slice-start.8
  251.8 8.6 %copy-start.18 = (bf16[256,3072]{1,0:T(8,128)(2,1)}, bf16[256,3072]{1,0:T(8,128)(2,1)S(1)}, u32[]{:S(2)}) copy-start(bf16[256,3072]{1,0:T(8,128)(2,1)S(1)} %get-tuple-element.57) | copy-start | bytes 4718596
  251.8 9.0 %copy-start.20 = (bf16[256,3072]{1,0:T(8,128)(2,1)}, bf16[256,3072]{1,0:T(8,128)(2,1)S(1)}, u32[]{:S(2)}) copy-start(bf16[256,3072]{1,0:T(8,128)(2,1)S(1)} %get-tuple-element.58) | copy-start | bytes 4718596
  257.9 36.6 %copy-start.2 = (f32[256,1152]{1,0:T(8,128)}, f32[256,1152]{1,0:T(8,128)S(1)}, u32[]{:S(2)}) copy-start(f32[256,1152]{1,0:T(8,128)S(1)} %convert_add_fusion) | copy-start | bytes 3538948
  275.6 6.0 %copy-start.19 = (bf16[256,3072]{1,0:T(8,128)(2,1)S(1)}, bf16[256,3072]{1,0:T(8,128)(2,1)}, u32[]{:S(2)}) copy-start(bf16[256,3072]{1,0:T(8,128)(2,1)} %copy-done.18) | copy-start | bytes 4718596
  281.6 4.5 copy-start.31
  281.6 4.6 copy-start.33
  286.2 2.3 copy-start.38
  288.4 5.2 copy-start.5
  443.0 4.7 copy-start.41
  443.1 5.4 copy-start.34
  444.1 4.9 copy-start.28
  463.4 4.0 copy-start.29
  464.7 2.8 copy-start.10
  464.7 2.8 copy-start.11
  464.7 2.8 copy-start.42
  464.7 2.8 copy-start.43
  470.8 3.9 copy-start
  470.9 3.9 copy-start.1
  470.9 3.9 copy-start.7
  470.9 4.1 copy-start.8
  470.9 4.4 copy-start.9
  475.3 3.2 copy-start.35
  475.3 2.7 copy-start.24
  478.0 2.4 copy-start.26
  491.1 47.8 %copy-start.3 = (f32[256,1152]{1,0:T(8,128)S(1)}, f32[256,1152]{1,0:T(8,128)}, u32[]{:S(2)}) copy-start(f32[256,1152]{1,0:T(8,128)} %copy-done.2) | copy-start | bytes 3538948
  491.1 47.8 %copy-start.45 = (s32[1152]{0:T(1024)S(1)}, s32[1152]{0:T(1024)}, u32[]{:S(2)}) copy-start(s32[1152]{0:T(1024)} %copy-done.44) | copy-start | bytes 13828
  491.1 47.8 %copy-start.46 = (f32[256]{0:T(256)S(1)}, f32[256]{0:T(256)}, u32[]{:S(2)}) copy-start(f32[256]{0:T(256)} %get-tuple-element.81) | copy-start | bytes 3076
  542.6 7.5 %copy-start.40 = (f32[96,1152]{1,0:T(8,128)S(1)}, f32[96,1152]{1,0:T(8,128)}, u32[]{:S(2)}) copy-start(f32[96,1152]{1,0:T(8,128)} %get-tuple-element.113) | copy-start | bytes 1327108
  (12 other events, 18.6 us)

commit v3 on v2

--- a/solution.py
+++ b/solution.py
@@ -654,7 +654,7 @@
 
 def stage_step(items, stages, t):
     for n in range(stages):
-        if 0 <= t - n < len(items):
+        if 0 <= t - n < len(items) and items[t - n] is not None:
             items[t - n].stage(n)
 
 
@@ -839,43 +839,13 @@
                 c.wait_send()
 
 
-def scatter_all(parts, cuts, collective_id):
-    zn = lax.axis_size("ctx") // 2
-    n = len(parts)
-    work = [
-        (a, piece) for a in range(n) for piece in pieces_of(*parts[a].shape[4:], *cuts[a])
-    ]
-    scratch = []
-    for a, (r0, nr, c0, nc) in work:
-        scratch += Scatter.scratch(zn, nr, nc)
-
-    def kernel(*refs):
-        ins, outs, bufs, (send, recv) = refs[:n], refs[n : 2 * n], refs[2 * n : -2], refs[-2:]
-        greet(zn)
-        items = []
-        for i, (a, (r0, nr, c0, nc)) in enumerate(work):
-            part = ins[a].at[:, :, :, :, pl.ds(r0, nr), pl.ds(c0, nc)]
-            out = outs[a].at[pl.ds(r0, nr), pl.ds(c0, nc)]
-            items.append(Scatter(part, out, bufs[5 * i : 5 * i + 5], send.at[i], recv.at[i], zn))
-        run_stages(items, 5)
-
-    return pl.pallas_call(
-        kernel,
-        out_shape=[jax.ShapeDtypeStruct(p.shape[4:], jnp.float32) for p in parts],
-        in_specs=[pl.BlockSpec(memory_space=pl.ANY)] * n,
-        out_specs=[pl.BlockSpec(memory_space=pltpu.VMEM)] * n,
-        scratch_shapes=scratch
-        + [
-            pltpu.SemaphoreType.DMA((len(work), Scatter.SEMS)),
-            pltpu.SemaphoreType.DMA((len(work), Scatter.SEMS)),
-        ],
-        compiler_params=pltpu.CompilerParams(
-            collective_id=collective_id, has_side_effects=True, vmem_limit_bytes=VMEM_LIMIT
-        ),
-    )(*parts)
-
-
 NT = (((1,), (1,)), ((), ()))
+
+
+def nt(a, b):
+    return lax.dot_general(a, b, NT, preferred_element_type=jnp.float32)
+
+
 PER = QUERY_HEADS // KEY_VALUE_HEADS
 HALF_GROUPS = KEY_VALUE_HEADS // 2
 HALF_HEADS = QUERY_HEADS // 2
@@ -1129,32 +1099,155 @@
     )(q, kv, *arrays)
 
 
-def scatter_attend(do, qh, kvg, oh, lse, parts, cuts, collective_id):
+class Share:
+    def __init__(self, src, own, other, local, send, recv, split):
+        z, y, x, k = place()
+        mine = src.at[:, :, :, k] if split else src
+        theirs = src.at[:, :, :, 1 - k] if split else src
+        self.load = None if mine is own else pltpu.make_async_copy(mine, own, local)
+        self.swap = remote(theirs, other, send, recv, device(z, y, x, 1 - k))
+        self.waited = False
+
+    def start(self):
+        if self.load is not None:
+            self.load.start()
+        self.swap.start()
+
+    def ready(self):
+        if not self.waited:
+            if self.load is not None:
+                self.load.wait()
+            self.swap.wait_recv()
+            self.waited = True
+
+    def sent(self):
+        self.swap.wait_send()
+
+
+class Sum:
+    SEMS = 8
+
+    def __init__(self, make, held, bufs, out, send, recv, zn):
+        z, y, x, k = self.at = place()
+        self.make, self.held, self.out, self.zn = make, held, out, zn
+        hz = zn // 2
+        xn, yn = device(z, y, 1 - x, k), device(z, 1 - y, x, k)
+        self.corners, self.colsums, self.ends = corners, colsums, ends = bufs
+        self.to_corner = [
+            remote(held.at[pl.ds(0, hz), 1 - y, 1 - x], corners.at[0], send.at[0], recv.at[0], yn),
+            remote(held.at[pl.ds(hz, hz), 1 - y, 1 - x], corners.at[1], send.at[1], recv.at[1], xn),
+        ]
+        self.to_col = [
+            remote(held.at[:, y, 1 - x], colsums.at[0], send.at[2], recv.at[2], xn),
+            remote(held.at[:, 1 - y, x], colsums.at[1], send.at[3], recv.at[3], yn),
+        ]
+        self.along = []
+        for j in range(1, zn):
+            zz = lax.rem(z + j, zn)
+            self.along.append(
+                remote(held.at[zz, y, x], ends.at[j - 1], send.at[3 + j], recv.at[3 + j], device(zz, y, x, k))
+            )
+
+    @staticmethod
+    def scratch(zn, nr, nc):
+        b = jnp.bfloat16
+        return [
+            pltpu.VMEM((2, zn // 2, nr, nc), b),
+            pltpu.VMEM((2, zn, nr, nc), b),
+            pltpu.VMEM((zn - 1, nr, nc), b),
+        ]
+
+    def stage(self, n):
+        z, y, x, k = self.at
+        zn, hz, held = self.zn, self.zn // 2, self.held
+        f32, b16 = jnp.float32, jnp.bfloat16
+        if n == 0:
+            self.make(held)
+            for c in self.to_corner:
+                c.start()
+        elif n == 1:
+            for c in self.to_corner:
+                c.wait_recv()
+            for i in range(hz):
+                held[i, y, 1 - x] = held[i, y, 1 - x] + self.corners[0, i]
+                held[hz + i, 1 - y, x] = held[hz + i, 1 - y, x] + self.corners[1, i]
+            for c in self.to_col:
+                c.start()
+        elif n == 2:
+            for c in self.to_col:
+                c.wait_recv()
+            for i in range(zn):
+                held[i, y, x] = (
+                    held[i, y, x].astype(f32)
+                    + self.colsums[0, i].astype(f32)
+                    + self.colsums[1, i].astype(f32)
+                ).astype(b16)
+            for c in self.along:
+                c.start()
+        elif n == 3:
+            for c in self.along:
+                c.wait_recv()
+            total = held[z, y, x].astype(f32)
+            for j in range(zn - 1):
+                total = total + self.ends[j].astype(f32)
+            self.out[...] = total
+            for c in self.to_corner + self.to_col + self.along:
+                c.wait_send()
+
+
+def scatter_attend(do, qh, kvg, oh, lse, tables, lefts, rests, rights, plan, collective_id):
     cn, wn = lax.axis_size("ctx"), lax.axis_size("ws")
     zn = cn // 2
     mbs, q_rows, tokens = do.shape
     rows = tokens // 2
     mine = q_rows // 2
-    n = len(parts)
+    all_rows = mbs * tokens
     f32, b16 = jnp.float32, jnp.bfloat16
-    work = [(a, piece) for a in range(n) for piece in pieces_of(*parts[a].shape[4:], *cuts[a])]
-    scratch = []
-    for a, (r0, nr, c0, nc) in work:
-        scratch += Scatter.scratch(zn, nr, nc)
     groups = range(HALF_GROUPS)
     scale = HEAD_SIZE**-0.5
+    ff = rights[2].shape[1]
+    width = rights[0].shape[1]
+    qkv_w = q_rows + 2 * KV_LANES
+    act_rows = lefts[0].shape[4]
+    ra = lefts[1].shape[4]
+    rest_w, qkv_rest_w = plan
+    n_down = act_rows // ra
+    half_ff = ff // 2
+    sizes = (
+        [(ra, width)] * n_down
+        + [(ra, half_ff)] * 4
+        + [(ra, width), (16, rest_w), (ra, 2 * KV_LANES), (ra, q_rows), (16, qkv_rest_w)]
+    )
+    max_cols = max(s[1] for s in sizes)
+    ring = 4
+    scratch = []
+    for nr, nc in sizes:
+        scratch += Sum.scratch(zn, nr, nc)
+    n_items = len(sizes)
+    ins_all = [*lefts, *rests, *rights]
+    n_in = len(ins_all)
+    split = [True] * len(lefts) + [False] * (n_in - len(lefts))
+    half = lambda a, s: (a.shape[:3] + a.shape[4:]) if s else a.shape
+    shares = []
+    for a, s in zip(ins_all, split):
+        shares += [pltpu.VMEM(half(a, s), b16), pltpu.VMEM(half(a, s), b16)]
+    outs_shape = [
+        (act_rows, width), (ra, ff), (ra, ff), (ra, width), (16, rest_w), (ra, qkv_w), (16, qkv_rest_w)
+    ]
+    n_out = len(outs_shape)
 
     def kernel(*refs):
-        do_ref, qh, kvg, oh, lse_ref = refs[:5]
-        ins = refs[5 : 5 + n]
-        dq_out, dkv_out = refs[5 + n : 7 + n]
-        outs = refs[7 + n : 7 + 2 * n]
-        rest = refs[7 + 2 * n :]
+        do_ref, qh, kvg, oh_ref, lse_ref, tab = refs[:6]
+        ins = refs[6 : 6 + n_in]
+        gq = refs[6 + n_in]
+        outs = refs[7 + n_in : 7 + n_in + n_out]
+        rest = refs[7 + n_in + n_out :]
         bufs, rest = rest[: len(scratch)], rest[len(scratch) :]
-        gh, qt, dot_, qr, dor, kt, delta, dq, dkv, give, kb, send, recv, xs, xr, ks, kr = (
-            rest[:10] + (rest[10:14],) + rest[14:]
-        )
-        dqh = gh
+        pairs, rest = rest[: len(shares)], rest[len(shares) :]
+        (held, gq_other, dkv_in, oh, gh, qt, dot_, kt, delta, dq, dkv, give) = rest[:12]
+        kb = rest[12:16]
+        send, recv, ps, pr, pl_, xs, xr, ks, kr = rest[16:]
+        dqh, dq_in = gh, oh
         greet(zn)
         z, y, x, k = place()
         w = 2 * x + k
@@ -1163,15 +1256,114 @@
             return ref.at[zz // 2, pl.ds(pl.multiple_of(lax.rem(zz, 2) * mine, 16), mine), :]
 
         gx = Exchange(lambda zz: heads_of(do_ref, zz), lambda zz: gh.at[zz], xs.at[0], xr.at[0], zn)
-        dx = Exchange(lambda zz: dqh.at[zz], lambda zz: heads_of(dq_out, zz), xs.at[1], xr.at[1], zn)
-        kvx = Scatter(None, dkv_out, tuple(kb) + (None,), ks, kr, zn, give)
+        dx = Exchange(lambda zz: dqh.at[zz], lambda zz: dq_in.at[zz], xs.at[1], xr.at[1], zn)
+        kvx = Scatter(None, dkv_in, tuple(kb) + (None,), ks, kr, zn, give)
+        share = [
+            Share(ins[i], pairs[2 * i], pairs[2 * i + 1], pl_.at[i], ps.at[i], pr.at[i], split[i])
+            for i in range(n_in)
+        ]
+        gq_share = Share(gq, gq, gq_other, None, ps.at[n_in], pr.at[n_in], False)
+        own = lambda i: pairs[2 * i]
+        other = lambda i: pairs[2 * i + 1]
+        ACT, H2, OT, HN, H2B, OTB, HNB, GY, GB, GG, GU = range(n_in)
+
+        def product(left, right, lo, row0, needs):
+            def make(dst):
+                for i in needs:
+                    share[i].ready()
+                nr, nc = dst.shape[3:]
+                lefts2 = [
+                    r[:, :, :, row0 : row0 + nr, :].reshape(zn * 4 * nr, all_rows)
+                    for r in (own(left), other(left))
+                ]
+                step = 3 * WIDE
+
+                def cols(i, _):
+                    at = pl.multiple_of(i * step, WIDE)
+                    t = jnp.dot(lefts2[0], right[0][:, pl.ds(lo + at, step)], preferred_element_type=f32)
+                    t = t + jnp.dot(lefts2[1], right[1][:, pl.ds(lo + at, step)], preferred_element_type=f32)
+                    dst[:, :, :, :, pl.ds(at, step)] = t.astype(b16).reshape(zn, 2, 2, nr, step)
+                    return 0
+
+                lax.fori_loop(0, nc // step, cols, 0)
+
+            return make
+
+        def both(i):
+            return (own(i), other(i))
+
+        def fold4(quarters):
+            row = lax.rem(lax.broadcasted_iota(jnp.int32, quarters[0].shape, 0), 8)
+            here = k == 0
+
+            def put(a, b):
+                n = a.shape[0]
+                low = jnp.where(here, a, pltpu.roll(a, n - 4, 0))
+                high = jnp.where(here, pltpu.roll(b, 4, 0), b)
+                t = jnp.where(row < 4, low, high)
+                return t.reshape(zn * 4, 8, t.shape[1])
+
+            t = jnp.concatenate([put(*quarters[:2]), put(*quarters[2:])], axis=1)
+            return t.astype(b16).reshape(zn, 2, 2, 16, t.shape[2])
+
+        def rest_product(dst):
+            step = 3 * WIDE
+            for i in (H2B, OTB, GB, GG, GU):
+                share[i].ready()
+            columns = []
+            for left, right, n in ((OTB, GB, width), (H2B, GG, ff), (H2B, GU, ff)):
+                columns += [(left, right, c) for c in range(0, n, step)]
+            per = rest_w // step
+
+            def one(entry):
+                if entry is None:
+                    return jnp.zeros((own(H2B).shape[0], step), f32)
+                left, right, c = entry
+                return jnp.dot(own(left)[...], own(right)[:, c : c + step], preferred_element_type=f32) + jnp.dot(
+                    other(left)[...], other(right)[:, c : c + step], preferred_element_type=f32
+                )
+
+            for c in range(per):
+                quarters = []
+                for q in range(4):
+                    at = q * per + c
+                    quarters.append(one(columns[at] if at < len(columns) else None))
+                dst[:, :, :, :, c * step : (c + 1) * step] = fold4(quarters)
+
+        def qkv_rest_product(dst):
+            for i in (HNB,):
+                share[i].ready()
+            gq_share.ready()
+            quarters = []
+            for q in range(4):
+                lo, hi = q * qkv_rest_w, min((q + 1) * qkv_rest_w, qkv_w)
+                t = jnp.dot(own(HNB)[...], gq[:, lo:hi], preferred_element_type=f32) + jnp.dot(
+                    other(HNB)[...], gq_other[:, lo:hi], preferred_element_type=f32
+                )
+                if hi - lo < qkv_rest_w:
+                    t = jnp.concatenate([t, jnp.zeros((t.shape[0], qkv_rest_w - hi + lo), f32)], axis=1)
+                quarters.append(t)
+            dst[...] = fold4(quarters)
+
+        gq_both = (gq, gq_other)
+        makes = [product(ACT, both(GY), 0, ra * i, (ACT, GY)) for i in range(n_down)]
+        makes += [product(H2, both(g), lo, 0, (H2, g)) for g in (GG, GU) for lo in (0, half_ff)]
+        makes += [product(OT, both(GB), 0, 0, (OT, GB)), rest_product]
+        makes += [product(HN, gq_both, 0, 0, (HN,)), product(HN, gq_both, 2 * KV_LANES, 0, (HN,)), qkv_rest_product]
+        targets = [outs[0].at[pl.ds(ra * i, ra), :] for i in range(n_down)]
+        targets += [outs[g].at[:, pl.ds(lo, half_ff)] for g in (1, 2) for lo in (0, half_ff)]
+        targets += [outs[3], outs[4], outs[5].at[:, pl.ds(0, 2 * KV_LANES)], outs[5].at[:, pl.ds(2 * KV_LANES, q_rows)], outs[6]]
         items = []
-        for i, (a, (r0, nr, c0, nc)) in enumerate(work):
-            part = ins[a].at[:, :, :, :, pl.ds(r0, nr), pl.ds(c0, nc)]
-            out = outs[a].at[pl.ds(r0, nr), pl.ds(c0, nc)]
-            items.append(Scatter(part, out, bufs[5 * i : 5 * i + 5], send.at[i], recv.at[i], zn))
+        for i, (nr, nc) in enumerate(sizes):
+            slot = held.at[i % ring, :, :, :, pl.ds(0, nr), pl.ds(0, nc)]
+            items.append(
+                Sum(makes[i], slot, bufs[3 * i : 3 * i + 3], targets[i], send.at[i], recv.at[i], zn)
+            )
+        load_o = pltpu.make_async_copy(oh_ref, oh, pl_.at[n_in])
+        load_o.start()
         gx.start()
-        stage_step(items, 5, 0)
+        for i in (ACT, GY, H2, GG, GU, OT, GB, H2B, OTB, HN, HNB):
+            share[i].start()
         dq[...] = jnp.zeros(dq.shape, f32)
 
         def clear(i, _):
@@ -1179,6 +1371,7 @@
             return 0
 
         lax.fori_loop(0, zn, clear, 0)
+        stage_step(items, 4, 0)
 
         def turn(j, block):
             flat = {b: turned(block(b)) for b in sorted({key_slot(g)[0] for g in groups})}
@@ -1187,19 +1380,18 @@
                 kt[j, g] = flat[b][side * HEAD_SIZE : (side + 1) * HEAD_SIZE]
 
         by_span(turn, kvg, cn, rows)
-        stage_step(items, 5, 1)
+        stage_step(items, 4, 1)
         gx.arrived()
-        for half in range(2):
+        load_o.wait()
+        for half_ in range(2):
             for zp in range(2):
-                p = pair_index(half, zp)
+                p = pair_index(half_, zp)
                 for g in groups:
-                    g_tile = pair_tile(gh, g, half, zp)
-                    o_tile = pair_tile(oh, g, half, zp)
+                    g_tile = pair_tile(gh, g, half_, zp)
+                    o_tile = pair_tile(oh, g, half_, zp)
                     delta[g, p] = jnp.sum(g_tile * o_tile, axis=0, keepdims=True)
-                    set_padded(qt, g, p, pair_tile(qh, g, half, zp), key_slot(g)[1])
+                    set_padded(qt, g, p, pair_tile(qh, g, half_, zp), key_slot(g)[1])
                     set_padded(dot_, g, p, g_tile, value_slot(g)[1])
-                    qr[g, p] = turned(qt[g, p])
-                    dor[g, p] = turned(dot_[g, p])
 
         def step(t, _):
             p, j, zz, yy, late, edge = walk(t, y, cn)
@@ -1219,8 +1411,8 @@
                     e = jnp.exp(s - lse_ref[g, p])
                     dp = jnp.dot(blocks[value_slot(g)[0]], dot_[g, p], preferred_element_type=f32)
                     ds = (e * (dp - delta[g, p])).astype(b16)
-                    put(value_slot(g)[0], jnp.dot(e.astype(b16), dor[g, p], preferred_element_type=f32))
-                    put(key_slot(g)[0], jnp.dot(ds, qr[g, p], preferred_element_type=f32))
+                    put(value_slot(g)[0], nt(e.astype(b16), dot_[g, p]))
+                    put(key_slot(g)[0], nt(ds, qt[g, p]))
                     dq[g, p] += jnp.dot(kt[j, g], ds, preferred_element_type=f32)
                 for b, v in enumerate(sums):
                     dkv[zz, yy, :, :, pl.ds(late, rows), WIDE * b : WIDE * b + WIDE] += v.reshape(
@@ -1231,12 +1423,48 @@
             pl.when(jnp.logical_not(edge))(lambda: run(False))
             return 0
 
-        last = len(items) + 4
+        def rope_back():
+            low_lanes = lax.broadcasted_iota(jnp.int32, (tokens, WIDE), 1) < HEAD_SIZE
+            quarter = HEAD_SIZE // 2
+
+            def back(t, kind):
+                if kind == "still":
+                    return t
+                cos, low, high = tab[0], tab[1], tab[2]
+                r = t * cos - pltpu.roll(t, WIDE - quarter, 1) * low - pltpu.roll(t, quarter, 1) * high
+                return r if kind == "turn" else jnp.where(low_lanes, r, t)
+
+            def heads_block(mb, at):
+                n = max(0, min(WIDE, mine - at))
+                parts = []
+                if n:
+                    parts.append(dq_in[2 * mb, at : at + n, :].astype(f32))
+                if n < WIDE:
+                    lo = at + n - mine
+                    parts.append(dq_in[2 * mb + 1, lo : lo + WIDE - n, :].astype(f32))
+                return parts[0] if len(parts) == 1 else jnp.concatenate(parts, axis=0)
+
+            kinds = ["turn", "mixed", "still"]
+            for mb in range(mbs):
+                at = slice(mb * tokens, (mb + 1) * tokens)
+                for hh in range(2):
+                    for b in range(KV_LANES // WIDE):
+                        t = dkv_in[2 * mb + hh, :, WIDE * b : WIDE * b + WIDE].astype(f32)
+                        lo = hh * KV_LANES + WIDE * b
+                        gq[at, lo : lo + WIDE] = back(t, kinds[b]).astype(b16)
+                for b in range(q_rows // WIDE):
+                    t = heads_block(mb, WIDE * b).T
+                    lo = 2 * KV_LANES + WIDE * b
+                    gq[at, lo : lo + WIDE] = back(t, "turn").astype(b16)
+
+        first = n_items - 3
+        order = items[:first] + [None, None] + items[first:]
         t = 0
+        per_step = -(-STEPS // (first - 3))
         kv_stage = 0
-        for s in range(2, last):
-            upto = min(STEPS, 6 * (s - 1))
-            if t < upto:
+        for s in range(2, len(order) + 3):
+            if t < STEPS:
+                upto = min(STEPS, t + per_step)
                 lax.fori_loop(t, upto, step, 0)
                 t = upto
                 if t == STEPS:
@@ -1250,42 +1478,49 @@
 
                     lax.fori_loop(0, zn, pack, 0)
                     kvx.stage(0)
+                    kv_stage = 1
                     unpair(lambda g, p: dq[g, p] * scale, dqh)
                     dx.start()
-                    kv_stage = 1
-            elif t == STEPS and kv_stage < 5:
+            elif kv_stage < 4 and s <= first + 1:
                 kvx.stage(kv_stage)
                 kv_stage += 1
-            stage_step(items, 5, s)
-        while kv_stage < 5:
-            kvx.stage(kv_stage)
-            kv_stage += 1
-        dx.arrived()
+            if s == first + 2:
+                while kv_stage < 5:
+                    kvx.stage(kv_stage)
+                    kv_stage += 1
+                dx.arrived()
+                rope_back()
+                gq_share.start()
+                gq_share.ready()
+            stage_step(order, 4, s)
         dx.sent()
         gx.sent()
+        gq_share.sent()
+        for i in share:
+            i.sent()
 
     stat = (HALF_GROUPS, 4, 1, PER * WIDE)
     block = (zn, mine, tokens)
     tile = (HALF_GROUPS, 4, WIDE, PER * WIDE)
-    tile_t = (HALF_GROUPS, 4, PER * WIDE, WIDE)
     any_ = pl.BlockSpec(memory_space=pl.ANY)
     vmem = pl.BlockSpec(memory_space=pltpu.VMEM)
+    dma = pltpu.SemaphoreType.DMA
     return pl.pallas_call(
         kernel,
-        out_shape=[
-            jax.ShapeDtypeStruct(do.shape, b16),
-            jax.ShapeDtypeStruct((zn, tokens, KV_LANES), b16),
-        ]
-        + [jax.ShapeDtypeStruct(p.shape[4:], f32) for p in parts],
-        in_specs=[any_, vmem, vmem, vmem, vmem] + [any_] * n,
-        out_specs=[any_, any_] + [vmem] * n,
+        out_shape=[jax.ShapeDtypeStruct((all_rows, qkv_w), b16)]
+        + [jax.ShapeDtypeStruct(s, f32) for s in outs_shape],
+        in_specs=[any_, vmem, vmem, any_, vmem, vmem] + [any_] * n_in,
+        out_specs=[vmem] * (1 + n_out),
         scratch_shapes=scratch
+        + shares
         + [
+            pltpu.VMEM((ring, zn, 2, 2, ra, max_cols), b16),
+            pltpu.VMEM((all_rows, qkv_w), b16),
+            pltpu.VMEM((zn, tokens, KV_LANES), b16),
+            pltpu.VMEM(block, b16),
             pltpu.VMEM(block, b16),
             pltpu.VMEM(tile, b16),
             pltpu.VMEM(tile, b16),
-            pltpu.VMEM(tile_t, b16),
-            pltpu.VMEM(tile_t, b16),
             pltpu.VMEM((2 * cn, HALF_GROUPS, HEAD_SIZE, wn * rows), b16),
             pltpu.VMEM(stat, f32),
             pltpu.VMEM((HALF_GROUPS, 4, HEAD_SIZE, PER * WIDE), f32),
@@ -1294,17 +1529,83 @@
         ]
         + Scatter.scratch(zn, tokens, KV_LANES)[:4]
         + [
-            pltpu.SemaphoreType.DMA((len(work), Scatter.SEMS)),
-            pltpu.SemaphoreType.DMA((len(work), Scatter.SEMS)),
-            pltpu.SemaphoreType.DMA((2, zn)),
-            pltpu.SemaphoreType.DMA((2, zn)),
-            pltpu.SemaphoreType.DMA((Scatter.SEMS,)),
-            pltpu.SemaphoreType.DMA((Scatter.SEMS,)),
+            dma((n_items, Sum.SEMS)),
+            dma((n_items, Sum.SEMS)),
+            dma((n_in + 1,)),
+            dma((n_in + 1,)),
+            dma((n_in + 1,)),
+            dma((2, zn)),
+            dma((2, zn)),
+            dma((Scatter.SEMS,)),
+            dma((Scatter.SEMS,)),
         ],
         compiler_params=pltpu.CompilerParams(
             collective_id=collective_id, has_side_effects=True, vmem_limit_bytes=VMEM_LIMIT
         ),
-    )(do, qh, kvg, oh, lse, *parts)
+    )(do, qh, kvg, oh, lse, tables, *ins_all)
+
+
+def finish(gq, weights, rest, x, inv, gain, gx1, gain_sums, order, collective_id):
+    zn = lax.axis_size("ctx") // 2
+    f32, b16 = jnp.float32, jnp.bfloat16
+    wa = weights.shape[0]
+    width = x.shape[1]
+
+    def kernel(gq_ref, w_ref, r_ref, x_ref, inv_ref, gain_ref, gx1_ref, sums_ref, order_ref, out, total, ghn, low, got, send, recv):
+        greet(zn)
+        z, y, x_, k = place()
+        ghn[:, :wa] = lax.dot_general(gq_ref[...], w_ref[...], NT, preferred_element_type=f32)
+        ghn[:, wa:] = lax.dot_general(gq_ref[...], r_ref[...], NT, preferred_element_type=f32)
+        xf = x_ref[...].astype(f32)
+        inv_ = inv_ref[...]
+        grad = ghn[...]
+        total[...] = jnp.zeros(total.shape, f32)
+        total[0:1, :] = jnp.sum(grad * xf * inv_, axis=0, keepdims=True)
+        total[1:2, :] = sums_ref[...]
+        moves = [
+            remote(total, got.at[0], send.at[0], recv.at[0], device(z, y, x_, 1 - k)),
+            remote(total, got.at[1], send.at[1], recv.at[1], device(z, y, 1 - x_, k)),
+            remote(total, got.at[2], send.at[2], recv.at[2], device(z, 1 - y, x_, k)),
+        ]
+        moves[0].start()
+        weighted = grad * gain_ref[...]
+        inner = jnp.mean(weighted * xf, axis=-1, keepdims=True)
+        row = inv_ * weighted - xf * (inv_ * inv_ * inv_) * inner
+        low[...] = (gx1_ref[...] + row).astype(b16)
+        for i in range(3):
+            moves[i].wait()
+            total[...] = total[...] + got[i]
+            if i < 2:
+                moves[i + 1].start()
+        ends = []
+        for j in range(1, zn):
+            ends.append(remote(total, got.at[2 + j], send.at[2 + j], recv.at[2 + j], device(lax.rem(z + j, zn), y, x_, k)))
+            ends[-1].start()
+        out[...] = lax.dot_general(low[...], order_ref[...], NT, preferred_element_type=f32).astype(b16)
+        for c in ends:
+            c.wait()
+        t = total[...]
+        for j in range(1, zn):
+            t = t + got[2 + j]
+        total[...] = t
+
+    vmem = pl.BlockSpec(memory_space=pltpu.VMEM)
+    return pl.pallas_call(
+        kernel,
+        out_shape=[jax.ShapeDtypeStruct(x.shape, b16), jax.ShapeDtypeStruct((8, width), f32)],
+        in_specs=[vmem] * 9,
+        out_specs=[vmem] * 2,
+        scratch_shapes=[
+            pltpu.VMEM(x.shape, f32),
+            pltpu.VMEM(x.shape, b16),
+            pltpu.VMEM((2 + zn, 8, width), f32),
+            pltpu.SemaphoreType.DMA((2 + zn,)),
+            pltpu.SemaphoreType.DMA((2 + zn,)),
+        ],
+        compiler_params=pltpu.CompilerParams(
+            collective_id=collective_id, has_side_effects=True, vmem_limit_bytes=VMEM_LIMIT
+        ),
+    )(gq, weights, rest, x, inv, gain, gx1, gain_sums, order)
 
 
 def rotate_lanes(t, cos, low, high):
@@ -1424,6 +1725,7 @@
     c, w = lax.axis_index("ctx"), lax.axis_index("ws")
     places = query_places(c, w, tokens, cn, wn)
     cos, low, high = (jnp.tile(t, (mbs, 1)) for t in lane_tables(places))
+    q_at = 2 * hid
     x = x_low.astype(f32)
     hn, inv1 = normalize(x, gain1)
     hn = hn.astype(b16)
@@ -1464,45 +1766,30 @@
     gattn = from_order(mm_back(gb, out_a, out_b).astype(b16))
     gb_plain = from_order(gb)
     gy_plain = cotangent.reshape(rows, width)
-
-    def sums(h, g):
-        first, rest = outer_sum(h[:, :wa], g), outer_sum(h[:, wa:], g)
-        return first.astype(b16).reshape(zn, 2, 2, 2, ra, -1), rest.astype(b16)
-
-    def fold_sums(parts):
-        t = jnp.concatenate(parts, axis=1)
-        return (
-            t.reshape(dn, rb, fold, -1).transpose(0, 2, 1, 3).reshape(zn, 2, 2, 2, 16, -1)
-        )
-
-    d_out_a, d_out_b = sums(o_p, gb_plain)
-    d_gate_a, d_gate_b = sums(h2, g_gate)
-    d_up_a, d_up_b = sums(h2, g_up)
-    d_down = outer_sum(act, gy_plain).astype(b16).reshape(zn, 2, 2, 2, -1, width)
-    d_b2 = fold_sums([d_out_b, d_gate_b, d_up_b, jnp.zeros((dn * rb, pad2), b16)])
-
-    dq, dkv, r_out, r_gate, r_up, r_down, r_b2 = scatter_attend(
+    left = lambda t: t.T.reshape(zn, 2, 2, 2, -1, rows)
+    wide = 2 * HEAD_SIZE
+    head_tables = jnp.stack([t[:tokens, q_at : q_at + wide] for t in (cos, low, high)])
+    gq, r_down, r_gate, r_up, r_out, r_b2, r_qkv, r_b1 = scatter_attend(
         gattn.reshape(mbs, tokens, q_width).transpose(0, 2, 1),
         qh,
         kvg,
         oh,
         lse,
-        [d_out_a, d_gate_a, d_up_a, d_down, d_b2],
-        [(1, 1), (1, 2), (1, 2), (2, 1), (1, 1)],
+        head_tables,
+        [left(act), left(h2[:, :wa]), left(o_p[:, :wa]), left(hn[:, :wa])],
+        [h2[:, wa:].T, o_p[:, wa:].T, hn[:, wa:].T],
+        [gy_plain, gb_plain, g_gate, g_up],
+        ((rest_w + pad2) // fold, (qkv_w + pad1) // fold),
         3,
     )
-    dkv = dkv.reshape(mbs, 2, tokens, hid).transpose(0, 2, 1, 3).reshape(rows, 2 * hid)
-    dq = dq.transpose(0, 2, 1).reshape(rows, q_width)
-    g_qkv = rotate_lanes(jnp.concatenate([dkv, dq], axis=1).astype(f32), cos, -low, -high).astype(b16)
-    ghn = mm_back(g_qkv, qkv_a, qkv_b)
-    first, gain1_sum = normalize_back(x, inv1, gain1, ghn)
-    input_grad = from_order((gx1 + first).astype(b16))
-    d_qkv_a, d_qkv_b = sums(hn, g_qkv)
-    by_owner = lambda t: jnp.concatenate([t[:wa].reshape(dn, ra), t[wa:].reshape(dn, rb)], axis=1)
-    gain_sums = jnp.stack([by_owner(gain1_sum), by_owner(gain2_sum)], axis=1).astype(b16)
-    gain_sums = jnp.pad(gain_sums, ((0, 0), (0, rb - 2), (0, pad1 - own))).reshape(dn * rb, pad1)
-    d_b1 = fold_sums([d_qkv_b, gain_sums])
-    r_qkv, r_b1 = scatter_all([d_qkv_a, d_b1], [(1, 1), (1, 1)], 4)
+    input_grad, gain_sums = finish(
+        gq, qkv_a, qkv_b, x_low, inv1, gain1[None], gx1, gain2_sum[None], order, 4
+    )
+    device_at = c * wn + w
+
+    def own_gain(t):
+        first = lax.dynamic_slice(t, (device_at * ra,), (ra,))
+        return jnp.concatenate([first, lax.dynamic_slice(t, (wa + device_at * rb,), (rb,))])
 
     def own_rows(t):
         return t.reshape(fold, rb, -1).transpose(1, 0, 2).reshape(rb, -1)
@@ -1513,12 +1800,12 @@
     return (
         out.reshape(inputs.shape),
         input_grad.reshape(inputs.shape),
-        e1[0, qkv_w : qkv_w + own],
+        own_gain(gain_sums[0]),
         d_qkv[:, 2 * hid :],
         jnp.concatenate([d_qkv[:, :half_hid], d_qkv[:, hid : hid + half_hid]], axis=1),
         jnp.concatenate([d_qkv[:, half_hid:hid], d_qkv[:, hid + half_hid : 2 * hid]], axis=1),
         whole(r_out, e2[:, :width]),
-        e1[1, qkv_w : qkv_w + own],
+        own_gain(gain_sums[1]),
         whole(r_gate, e2[:, width : width + ff]),
         whole(r_up, e2[:, width + ff : width + 2 * ff]),
         r_down,

time: 560 us -> 506 us (0.904)
  matrix products: 73.6 us -> 45.7 us
  local copies, waits for them, and re-layouts: 79.6 us -> 62.8 us
  other arithmetic: 27.1 us -> 18.3 us
    dot_general x9 -> x0, matrix products: 23.5 us -> none  [outer_sum(): jnp.einsum('ri,rj->ij', left, right, preferred_element_type=jnp.float32)]
    reshape x10 -> x0, local copies, waits for them, and re-layouts: 19.3 us -> none  [the longest x6 18.9 us: fold_sums(): t.reshape(dn, rb, fold, -1).transpose(0, 2, 1, 3)]
    concatenate x5 -> x0, local copies, waits for them, and re-layouts: 8.88 us -> none  [the longest x2 4.46 us: rotate_lanes(): jnp.roll(t, -quarter, axis=-1) * low]
    dot_general x4 -> x3, matrix products: 13.8 us -> 12.4 us  [from_order(): lax.dot_general(t, order, NT, preferred_element_type=f32).astype(t.dtype)]
    unnamed x134 -> x98, local copies, waits for them, and re-layouts: 17 us -> 18.3 us
    dot_general x9 -> x7, matrix products: 15.5 us -> 14.4 us  [back_product(): jnp.einsum('rj,ij->ri', gradient, weight, preferred_element_type=jnp.floa...]
where the time goes in v3:
time: 506 us; the launch traced here: 499 us
  Pallas kernels  370 us (73%)
  local copies, waits for them, and re-layouts  62.8 us (12%)
  matrix products  45.7 us (9%)
  other arithmetic  18.3 us (4%)
    pallas_call x1, Pallas kernels, scatter_attend(): pl.pallas_call(kernel, out_shape=[jax.ShapeDtypeStruct((all_rows, qkv_w),...  168 us
    pallas_call x1, Pallas kernels, gather_attend(): pl.pallas_call(kernel, out_shape=[jax.ShapeDtypeStruct(q.shape, b16), jax...  144 us
    pallas_call x1, Pallas kernels, gather_all(): pl.pallas_call(kernel, out_shape=[jax.ShapeDtypeStruct((zn, 2, 2, 2, rows...  37.5 us
    pallas_call x1, Pallas kernels, finish(): pl.pallas_call(kernel, out_shape=[jax.ShapeDtypeStruct(x.shape, b16), jax...  20 us
    unnamed x98, local copies, waits for them, and re-layouts  18.3 us
    dot_general x8, matrix products, matrix_multiply(): return jnp.dot(left, right, preferred_element_type=jnp.float32)  14.9 us
    dot_general x7, matrix products, back_product(): jnp.einsum('rj,ij->ri', gradient, weight, preferred_element_type=jnp.floa...  14.4 us
    dot_general x3, matrix products, from_order(): lax.dot_general(t, order, NT, preferred_element_type=f32).astype(t.dtype)  12.4 us

profile of v3, /device:TPU:0, one launch (start us, length us, event | category | flops | bytes accessed | tf_op | source)
XLA Modules:
  0.0 498.6 jit_solution(2624828704570587957)
XLA Ops:
  0.6 0.9 fusion.122
  1.6 1.1 concatenate.105.refs_0_
  4.1 37.5 %shard_map.194 = (bf16[4,2,2,2,32,1920]{5,4,3,2,1,0:T(8,128)(2,1)}, bf16[4,2,2,2,16,512]{5,4,3,2,1,0:T(8,128)(2,1)}) custom-call(bf16[36,1920]{1,0:T(8,128)(2,1)} %copy-done.26, bf16[16,512]{1,0:T(8,128)(2,1)} %reshape.325.refs_1_), custom_call_target="tpu_custom_call" | custom-call | tf_op jit(solution)/shard_map/pallas_call | solution.py:721
  41.6 1.2 reshape.326
  43.6 2.4 fusion.6
  46.4 1.3 fusion.49
  48.2 2.6 fusion.118
  53.7 0.9 constant_dynamic-update-slice_fusion
  54.6 1.5 copy.39
  58.8 0.9 constant_dynamic-update-slice_fusion.3
  59.7 2.5 copy.40
  65.7 2.5 copy.41
  68.2 3.3 fusion.24
  71.5 1.3 copy-done.12
  72.9 1.1 copy.42
  74.0 1.9 slice.326
  78.0 144.4 %shard_map.195 = (bf16[2,1152,128]{2,1,0:T(8,128)(2,1)}, bf16[4,576,128]{2,1,0:T(8,128)(2,1)}, bf16[4,2,2,2,128,384]{5,4,3,2,1,0:T(8,128)(2,1)}, bf16[4,576,128]...) custom-call(bf16[2,1152,128]{2,1,0:T(8,128)(2,1)} %bitcast.144, ...), custom_call_target="tpu_custom_call" | custom-call | tf_op jit(solution)/shard_map/pallas_call | solution.py:1064
  222.4 3.2 reshape.336
  226.4 1.5 copy.63
  228.2 1.6 fusion.18
  230.8 1.4 multiply_reduce_fusion.2
  232.7 5.0 fusion.53
  237.8 1.8 fusion.51
  240.4 2.2 fusion.47
  242.6 3.6 multiply_convert_fusion.1
  246.2 1.8 copy-done.17
  248.0 0.9 fusion.7
  248.9 1.6 copy.51
  250.5 5.2 %fusion.124 = f32[256,1024]{1,0:T(8,128)S(1)} fusion(bf16[256,3072]{1,0:T(8,128)(2,1)} %get-tuple-element.57.refs_15_, bf16[1024,3072]{1,0:T(8,128)(2,1)} %bitcast.189), kind=kOutput, calls=%fused_computation.221 | convolution fusion | flops 1610612736 | bytes 8912896 | tf_op jit(solution)/shard_map/rj,ij->ri/dot_general | solution.py:41
  257.1 4.6 fusion.125
  264.1 1.2 copy-done.3
  265.4 0.9 convolution_convert_fusion
  266.6 1.3 fusion.20
  267.9 1.1 copy.50
  268.9 2.1 fusion.21.refs_14_
  271.9 2.0 copy.52
  274.7 2.0 slice.228
  276.6 1.5 slice_bitcast_fusion.5.refs_11_
  278.4 1.0 copy-done.5
  280.4 1.0 copy.53
  282.1 168.0 %shard_map.196 = (bf16[256,1920]{1,0:T(8,128)(2,1)}, f32[96,1152]{1,0:T(8,128)}, f32[32,3072]{1,0:T(8,128)}, f32[32,3072]{1,0:T(8,128)}, f32[32,1152]{1,0:T(8,12...) custom-call(bf16[2,1152,128]{2,1,0:T(8,128)(2,1)} %bitcast.145, ...), custom_call_target="tpu_custom_call" | custom-call | tf_op jit(solution)/shard_map/pallas_call | solution.py:1508
  450.2 1.1 reshape.350
  451.2 1.8 pad_maximum_fusion.1
  453.0 1.8 pad_maximum_fusion
  456.3 1.8 slice.218.r_ref
  459.8 2.6 fusion.order_ref
  462.4 20.0 %shard_map.197 = (bf16[256,1152]{1,0:T(8,128)(2,1)}, f32[8,1152]{1,0:T(8,128)}) custom-call(bf16[256,1920]{1,0:T(8,128)(2,1)} %get-tuple-element.45.gq_ref, bf16[1024,1920]{1,0:T(8,128)(2,1)} %bitcast.138, bf16[128,1920]{1,0:T(8,128)(2,1)} %slice.218.r_ref, bf16[256,1152]{1,0:T(8,128)(2,1)} %slice.210.x_ref, f32[256,1]{1,0:T(8,128)} %copy.56.inv_ref, ...), custom_call_target="tpu_custom_call" | custom-call | tf_op jit(solution)/shard_map/pallas_call | solution.py:1593
  487.5 9.0 %fusion.19 = bf16[256,1152]{1,0:T(8,128)(2,1)} fusion(s32[1152]{0:T(1024)S(1)} %fusion.83, f32[256,1152]{1,0:T(8,128)S(1)} %get-tuple-element.82, bf16[3072,1152]{1,0:T(8,128)(2,1)} %bitcast.180, f32[256,3072]{1,0:T(8,128)} %copy-done.1, f32[256,3072]{1,0:T(8,128)} %copy-done.17), kind=kOutput, calls=%fused_computation.32 | convolution fusion | flops 2498347008 | bytes 15143424 | tf_op jit(solution)/shard_map/dot_general | solution.py:1669
  (186 shorter events, 34.8 us)
Async XLA Ops:
  1.5 42.0 %copy-start.29 = (bf16[2,128,1152]{2,1,0:T(8,128)(2,1)S(1)}, bf16[2,128,1152]{2,1,0:T(8,128)(2,1)}, u32[]{:S(2)}) copy-start(bf16[2,128,1152]{2,1,0:T(8,128)(2,1)} %param.21) | copy-start | bytes 1769476
  1.5 42.0 %copy-start.33 = (bf16[2,128,1152]{2,1,0:T(8,128)(2,1)S(1)}, bf16[2,128,1152]{2,1,0:T(8,128)(2,1)}, u32[]{:S(2)}) copy-start(bf16[2,128,1152]{2,1,0:T(8,128)(2,1)} %param.11) | copy-start | bytes 1769476
  1.6 42.0 %copy-start.34 = (bf16[96,1152]{1,0:T(8,128)(2,1)S(1)}, bf16[96,1152]{1,0:T(8,128)(2,1)}, u32[]{:S(2)}) copy-start(bf16[96,1152]{1,0:T(8,128)(2,1)} %param.20) | copy-start | bytes 663556
  1.6 42.0 %copy-start.35 = (bf16[36,1152]{1,0:T(8,128)(2,1)S(1)}, bf16[36,1152]{1,0:T(8,128)(2,1)}, u32[]{:S(2)}) copy-start(bf16[36,1152]{1,0:T(8,128)(2,1)} %param.16) | copy-start | bytes 248836
  2.7 1.4 copy-start.26
  43.1 4.6 copy-start.15
  43.6 2.9 copy-start.16
  46.0 1.7 copy-start.8
  46.4 1.3 copy-start.20
  56.1 12.1 %copy-start.4 = (f32[128,1920]{1,0:T(8,128)}, f32[128,1920]{1,0:T(8,128)S(1)}, u32[]{:S(2)}) copy-start(f32[128,1920]{1,0:T(8,128)S(1)} %copy.39) | copy-start | bytes 2949124
  71.5 1.3 copy-start.12
  72.8 3.1 copy-start.9
  72.8 3.8 slice-start
  72.8 3.8 slice-start.1
  72.8 3.8 slice-start.2
  226.4 1.5 copy-start.28
  228.2 1.7 copy-start.2
  229.8 1.0 copy-start.22
  232.5 5.2 %slice-start.5 = ((s8[6291456]{0:T(1024)(128)(4,1)}), s8[4194304]{0:T(1024)(128)(4,1)S(1)}, s32[]{:S(2)}) async-start(s8[6291456]{0:T(1024)(128)(4,1)} %bitcast.185), calls=%async_computation.5 | async-start | bytes 8388608
  232.7 9.9 %copy-start.18 = (bf16[256,1152]{1,0:T(8,128)(2,1)}, bf16[256,1152]{1,0:T(8,128)(2,1)S(1)}, u32[]{:S(2)}) copy-start(bf16[256,1152]{1,0:T(8,128)(2,1)S(1)} %multiply_convert_fusion.4) | copy-start | bytes 1769476
  232.7 5.0 %slice-start.6 = ((s8[6291456]{0:T(1024)(128)(4,1)}), s8[2097152]{0:T(1024)(128)(4,1)S(1)}, s32[]{:S(2)}) async-start(s8[6291456]{0:T(1024)(128)(4,1)} %bitcast.185), calls=%async_computation.6 | async-start | bytes 4194304
  232.7 7.4 %slice-start.3 = ((s8[7077888]{0:T(1024)(128)(4,1)}), s8[4194304]{0:T(1024)(128)(4,1)S(1)}, s32[]{:S(2)}) async-start(s8[7077888]{0:T(1024)(128)(4,1)} %bitcast.181), calls=%async_computation.3 | async-start | bytes 8388608
  237.7 1.8 copy-start.13
  237.8 2.6 slice-start.4
  240.1 6.1 %copy-start.1 = (f32[256,3072]{1,0:T(8,128)}, f32[256,3072]{1,0:T(8,128)S(1)}, u32[]{:S(2)}) copy-start(f32[256,3072]{1,0:T(8,128)S(1)} %convolution_add_fusion) | copy-start | bytes 9437188
  246.2 1.8 copy-start.17
  250.5 5.2 %copy-start.14 = (bf16[16,8,4,1920]{3,1,2,0:T(8,128)(2,1)S(1)}, bf16[16,8,4,1920]{3,1,2,0:T(8,128)(2,1)}, u32[]{:S(2)}) copy-start(bf16[16,8,4,1920]{3,1,2,0:T(8,128)(2,1)} %copy.63) | copy-start | bytes 5898244
  250.5 5.2 %copy-start.24 = (bf16[256,3072]{1,0:T(8,128)(2,1)S(1)}, bf16[256,3072]{1,0:T(8,128)(2,1)}, u32[]{:S(2)}) copy-start(bf16[256,3072]{1,0:T(8,128)(2,1)} %get-tuple-element.57.refs_15_) | copy-start | bytes 4718596
  255.7 1.4 copy-start.25
  262.3 1.4 copy-start.10
  263.7 1.7 copy-start.3
  265.4 3.6 copy-start
  268.9 2.1 copy-start.19
  271.0 7.1 %copy-start.6 = (f32[128,1920]{1,0:T(8,128)S(1)}, f32[128,1920]{1,0:T(8,128)}, u32[]{:S(2)}) copy-start(f32[128,1920]{1,0:T(8,128)} %copy.40) | copy-start | bytes 2949124
  274.7 3.6 copy-start.7
  278.2 1.2 copy-start.5
  278.4 1.9 copy-start.21
  450.1 8.8 %copy-start.11 = (bf16[644,1152]{1,0:T(8,128)(2,1)S(1)}, bf16[644,1152]{1,0:T(8,128)(2,1)}, u32[]{:S(2)}) copy-start(bf16[644,1152]{1,0:T(8,128)(2,1)} %copy-done.8) | copy-start | bytes 4451332
  462.4 21.6 %copy-start.31 = (f32[32,1152]{1,0:T(8,128)S(1)}, f32[32,1152]{1,0:T(8,128)}, u32[]{:S(2)}) copy-start(f32[32,1152]{1,0:T(8,128)} %get-tuple-element.50) | copy-start | bytes 442372
  462.4 22.3 %copy-start.32 = (f32[16,512]{1,0:T(8,128)S(1)}, f32[16,512]{1,0:T(8,128)}, u32[]{:S(2)}) copy-start(f32[16,512]{1,0:T(8,128)} %get-tuple-element.49) | copy-start | bytes 98308
  462.4 22.3 %copy-start.23 = (f32[32,1920]{1,0:T(8,128)S(1)}, f32[32,1920]{1,0:T(8,128)}, u32[]{:S(2)}) copy-start(f32[32,1920]{1,0:T(8,128)} %get-tuple-element.48) | copy-start | bytes 737284
  487.5 9.0 %copy-start.27 = (bf16[256,1152]{1,0:T(8,128)(2,1)S(1)}, bf16[256,1152]{1,0:T(8,128)(2,1)}, u32[]{:S(2)}) copy-start(bf16[256,1152]{1,0:T(8,128)(2,1)} %get-tuple-element.46) | copy-start | bytes 1769476
  487.5 9.9 %copy-start.30 = (f32[96,1152]{1,0:T(8,128)S(1)}, f32[96,1152]{1,0:T(8,128)}, u32[]{:S(2)}) copy-start(f32[96,1152]{1,0:T(8,128)} %get-tuple-element.109) | copy-start | bytes 1327108

commit v4 on v3

--- a/solution.py
+++ b/solution.py
@@ -701,41 +701,6 @@
             c.wait_send()
 
 
-def gather_all(arrays, rows_used, cuts, collective_id):
-    zn = lax.axis_size("ctx") // 2
-    n = len(arrays)
-    work = [
-        (a, piece)
-        for a in range(n)
-        for piece in pieces_of(rows_used[a], arrays[a].shape[1], *cuts[a])
-    ]
-
-    def kernel(*refs):
-        ins, outs, (send, recv) = refs[:n], refs[n : 2 * n], refs[2 * n :]
-        greet(zn)
-        items = []
-        for i, (a, (r0, nr, c0, nc)) in enumerate(work):
-            items.append(gather_item(ins[a], outs[a], r0, nr, c0, nc, send.at[i], recv.at[i], zn))
-        run_stages(items, 5)
-
-    return pl.pallas_call(
-        kernel,
-        out_shape=[
-            jax.ShapeDtypeStruct((zn, 2, 2, 2, rows_used[a], arrays[a].shape[1]), arrays[a].dtype)
-            for a in range(n)
-        ],
-        in_specs=[pl.BlockSpec(memory_space=pl.ANY)] * n,
-        out_specs=[pl.BlockSpec(memory_space=pl.ANY)] * n,
-        scratch_shapes=[
-            pltpu.SemaphoreType.DMA((len(work), Gather.SEMS)),
-            pltpu.SemaphoreType.DMA((len(work), Gather.SEMS)),
-        ],
-        compiler_params=pltpu.CompilerParams(
-            collective_id=collective_id, has_side_effects=True, vmem_limit_bytes=VMEM_LIMIT
-        ),
-    )(*arrays)
-
-
 class Scatter:
     SEMS = 10
 
@@ -947,49 +912,142 @@
     lax.fori_loop(0, 2 * cn, one, 0)
 
 
-def gather_attend(q, kv, arrays, used, cuts, collective_id):
+def transposed(t):
+    return jnp.concatenate([t[:, i : i + WIDE].T for i in range(0, t.shape[1], WIDE)], axis=0)
+
+
+def unfold_rows(src, dst, rb):
+    n = src.shape[0] // 16
+    fold = 16 // rb
+    cols = src.shape[1]
+    shape = (n * rb, n * 16)
+    row = lax.broadcasted_iota(jnp.int32, shape, 0)
+    at = 16 * (row // rb) + lax.rem(row, rb)
+    col = lax.broadcasted_iota(jnp.int32, shape, 1)
+    for q in range(fold):
+        pick = jnp.where(col == at + rb * q, 1.0, 0.0).astype(jnp.bfloat16)
+        t = jnp.dot(pick, src[...], preferred_element_type=jnp.float32)
+        dst[:, q * cols : (q + 1) * cols] = t.astype(dst.dtype)
+
+
+def gather_attend(x, tables, qkv, fold1, arrays, used, cuts, collective_id):
     cn, wn = lax.axis_size("ctx"), lax.axis_size("ws")
     zn = cn // 2
-    mbs, q_rows, tokens = q.shape
+    dn = cn * wn
+    tokens = tables.shape[1]
+    all_rows, width = x.shape
+    mbs = all_rows // tokens
+    qkv_w = qkv.shape[1]
+    q_rows = qkv_w - 2 * KV_LANES
     rows = tokens // 2
     mine = q_rows // 2
+    f32, b16 = jnp.float32, jnp.bfloat16
+    ra = qkv.shape[0] // 16 * 16
+    rb = qkv.shape[0] - ra
+    wa = dn * ra
+    wide1 = fold1.shape[1] * (16 // rb)
     n = len(arrays)
-    f32, b16 = jnp.float32, jnp.bfloat16
     work = [(a, piece) for a in range(n) for piece in pieces_of(used[a], arrays[a].shape[1], *cuts[a])]
     groups = range(HALF_GROUPS)
+    n_first = 3
 
     def kernel(*refs):
-        q_ref, kv_ref = refs[:2]
-        ins = refs[2 : 2 + n]
-        o_out, q_out, kv_out, oh_out, lse_out = refs[2 + n : 7 + n]
-        outs = refs[7 + n : 7 + 2 * n]
-        qh, kvg, oh, qpad, vt, m_s, l_s, acc, send, recv, xs, xr, ks, kr, save = refs[7 + 2 * n :]
+        x_ref, tab, qkv_ref, fold_ref = refs[:4]
+        ins = refs[4 : 4 + n]
+        at = 4 + n
+        o_out, q_out, kv_out, oh_out, lse_out, w_out, wb_out, hn_out, hnb_out, inv_out, gains_out = refs[at : at + 11]
+        at += 11
+        outs = refs[at : at + n]
+        at += n
+        (wq, f1, wide, hn, q_s, kv_s, qh, kvg, oh, qpad, vt, m_s, l_s, acc, send, recv, xs, xr, ks, kr, save) = refs[at:]
         greet(zn)
-        z, y, x, k = place()
-        w = 2 * x + k
+        z, y, x_, k = place()
+        w = 2 * x_ + k
 
         def lanes_of(zz):
-            return kv_ref.at[zz // 2, :, pl.ds(pl.multiple_of(lax.rem(zz, 2) * KV_LANES, WIDE), KV_LANES)]
+            return kv_s.at[zz // 2, :, pl.ds(pl.multiple_of(lax.rem(zz, 2) * KV_LANES, WIDE), KV_LANES)]
 
         def heads_of(ref, zz):
             return ref.at[zz // 2, pl.ds(pl.multiple_of(lax.rem(zz, 2) * mine, 16), mine), :]
 
         items = [
-            gather_item(ins[a], outs[a], r0, nr, c0, nc, send.at[i], recv.at[i], zn)
+            gather_item(fold_ref, f1, 0, 16, 0, fold1.shape[1], send.at[0], recv.at[0], zn),
+            gather_item(qkv_ref, wq, 0, ra, 0, 2 * KV_LANES, send.at[1], recv.at[1], zn),
+            gather_item(qkv_ref, wq, 0, ra, 2 * KV_LANES, q_rows, send.at[2], recv.at[2], zn),
+        ]
+        items += [
+            gather_item(ins[a], outs[a], r0, nr, c0, nc, send.at[n_first + i], recv.at[n_first + i], zn)
             for i, (a, (r0, nr, c0, nc)) in enumerate(work)
         ]
         kvx = Gather(lanes_of, kvg, ks, kr, zn)
-        qx = Exchange(lambda zz: heads_of(q_ref, zz), lambda zz: qh.at[zz], xs.at[0], xr.at[0], zn)
+        qx = Exchange(lambda zz: heads_of(q_s, zz), lambda zz: qh.at[zz], xs.at[0], xr.at[0], zn)
         ox = Exchange(lambda zz: oh.at[zz], lambda zz: heads_of(o_out, zz), xs.at[1], xr.at[1], zn)
-        kvx.stage(0)
-        qx.start()
-        stage_step(items, 5, 0)
+        for s in range(n_first + 1):
+            stage_step(items, 5, s)
+        xf = x_ref[...].astype(f32)
+        inv = lax.rsqrt(jnp.mean(xf * xf, axis=-1, keepdims=True) + EPSILON)
+        inv_out[...] = inv
         m_s[...] = jnp.full(m_s.shape, NEG, f32)
         l_s[...] = jnp.zeros(l_s.shape, f32)
         acc[...] = jnp.zeros(acc.shape, f32)
+        stage_step(items, 5, n_first + 1)
+        unfold_rows(f1[...].reshape(dn * 16, fold1.shape[1]), wide, rb)
+        lane = lax.broadcasted_iota(jnp.int32, (WIDE, width), 1)
+        local = jnp.where(lane < wa, lax.rem(lane, ra), ra + lax.rem(lane - wa, rb))
+        spread = jnp.where(lax.broadcasted_iota(jnp.int32, (WIDE, width), 0) == local, 1.0, 0.0).astype(b16)
+        lines = jnp.dot(wide[:, wide1 - WIDE :], spread, preferred_element_type=f32)
+        lane = lax.broadcasted_iota(jnp.int32, lines.shape, 1)
+        owner = jnp.where(lane < wa, lane // ra, (lane - wa) // rb)
+        line = lax.broadcasted_iota(jnp.int32, lines.shape, 0)
+        for i in range(2):
+            gains_out[i : i + 1, :] = jnp.sum(jnp.where(line == rb * owner + i, lines, 0.0), axis=0, keepdims=True)
+        normed = xf * inv * gains_out[0:1, :]
+        hn[...] = normed.astype(b16)
+        hn_out[...] = transposed(normed[:, :wa]).astype(b16)
+        hnb_out[...] = transposed(normed[:, wa:]).astype(b16)
+        stage_step(items, 5, n_first + 2)
+
+        low_lanes = lax.broadcasted_iota(jnp.int32, (tokens, WIDE), 1) < HEAD_SIZE
+        quarter = HEAD_SIZE // 2
+
+        def turned_heads(t, kind):
+            if kind == "still":
+                return t
+            cos, low, high = tab[0], tab[1], tab[2]
+            r = t * cos + pltpu.roll(t, WIDE - quarter, 1) * low + pltpu.roll(t, quarter, 1) * high
+            return r if kind == "turn" else jnp.where(low_lanes, r, t)
+
+        def project(c):
+            cols = slice(c * KV_LANES, (c + 1) * KV_LANES)
+            t = jnp.dot(hn[:, :wa], wq[:, :, :, :, :, cols].reshape(wa, KV_LANES), preferred_element_type=f32)
+            t = t + jnp.dot(hn[:, wa:], wide[:, cols], preferred_element_type=f32)
+            kinds = ["turn", "mixed", "still"] if c < 2 else ["turn"] * 3
+            for mb in range(mbs):
+                for b in range(3):
+                    r = turned_heads(t[mb * tokens : (mb + 1) * tokens, WIDE * b : WIDE * b + WIDE], kinds[b])
+                    at = c * KV_LANES + WIDE * b
+                    if c < 2:
+                        kv_s[mb, :, at : at + WIDE] = r.astype(b16)
+                    else:
+                        at -= 2 * KV_LANES
+                        q_s[mb, at : at + WIDE, :] = (r * HEAD_SIZE**-0.5).T.astype(b16)
+
+        project(0)
+        project(1)
+        kvx.stage(0)
+        stage_step(items, 5, n_first + 3)
+        for c in range(2, qkv_w // KV_LANES):
+            project(c)
+        qx.start()
+        saves = [
+            pltpu.make_async_copy(wq, w_out, save.at[3]),
+            pltpu.make_async_copy(wide.at[:, pl.ds(0, qkv_w)], wb_out, save.at[4]),
+        ]
+        for s in saves:
+            s.start()
         kvx.stage(1)
         kvx.stage(2)
-        stage_step(items, 5, 1)
+        stage_step(items, 5, n_first + 4)
         kvx.stage(3)
         qx.arrived()
         for half in range(2):
@@ -1005,11 +1063,11 @@
                 vt[j, g] = flat[b][side * HEAD_SIZE : (side + 1) * HEAD_SIZE]
 
         by_span(turn, kvg, cn, rows)
-        saves = [
+        saves += [
             pltpu.make_async_copy(qh, q_out, save.at[0]),
             pltpu.make_async_copy(kvg, kv_out, save.at[1]),
         ]
-        for s in saves:
+        for s in saves[2:]:
             s.start()
 
         def step(t, _):
@@ -1039,8 +1097,10 @@
 
         last = len(items) + 4
         t = 0
-        for s in range(2, last):
-            upto = min(STEPS, 5 * (s - 1))
+        start = n_first + 5
+        per_step = -(-STEPS // (last - start - 2))
+        for s in range(start, last):
+            upto = min(STEPS, t + per_step)
             if t < upto:
                 lax.fori_loop(t, upto, step, 0)
                 t = upto
@@ -1061,22 +1121,34 @@
     block = (zn, mine, tokens)
     kv_shape = (zn, 2, 2, 2, tokens, KV_LANES)
     any_ = pl.BlockSpec(memory_space=pl.ANY)
+    vmem = pl.BlockSpec(memory_space=pltpu.VMEM)
+    sds = jax.ShapeDtypeStruct
+    dma = pltpu.SemaphoreType.DMA
     return pl.pallas_call(
         kernel,
         out_shape=[
-            jax.ShapeDtypeStruct(q.shape, b16),
-            jax.ShapeDtypeStruct(block, b16),
-            jax.ShapeDtypeStruct(kv_shape, b16),
-            jax.ShapeDtypeStruct(block, b16),
-            jax.ShapeDtypeStruct(stat, f32),
+            sds((mbs, q_rows, tokens), b16),
+            sds(block, b16),
+            sds(kv_shape, b16),
+            sds(block, b16),
+            sds(stat, f32),
+            sds((zn, 2, 2, 2, ra, qkv_w), b16),
+            sds((dn * rb, qkv_w), b16),
+            sds((wa, all_rows), b16),
+            sds((width - wa, all_rows), b16),
+            sds((all_rows, 1), f32),
+            sds((2, width), f32),
         ]
-        + [
-            jax.ShapeDtypeStruct((zn, 2, 2, 2, used[a], arrays[a].shape[1]), arrays[a].dtype)
-            for a in range(n)
-        ],
-        in_specs=[any_] * (2 + n),
-        out_specs=[any_] * 4 + [pl.BlockSpec(memory_space=pltpu.VMEM)] + [any_] * n,
+        + [sds((zn, 2, 2, 2, used[a], arrays[a].shape[1]), arrays[a].dtype) for a in range(n)],
+        in_specs=[vmem] * 2 + [any_] * (2 + n),
+        out_specs=[any_] * 4 + [vmem] + [any_] * 2 + [vmem] * 4 + [any_] * n,
         scratch_shapes=[
+            pltpu.VMEM((zn, 2, 2, 2, ra, qkv_w), b16),
+            pltpu.VMEM((zn, 2, 2, 2, 16, fold1.shape[1]), b16),
+            pltpu.VMEM((dn * rb, wide1), b16),
+            pltpu.VMEM((all_rows, width), b16),
+            pltpu.VMEM((mbs, q_rows, tokens), b16),
+            pltpu.VMEM((mbs, tokens, 2 * KV_LANES), b16),
             pltpu.VMEM(block, b16),
             pltpu.VMEM(kv_shape, b16),
             pltpu.VMEM(block, b16),
@@ -1085,18 +1157,18 @@
             pltpu.VMEM(stat, f32),
             pltpu.VMEM(stat, f32),
             pltpu.VMEM((HALF_GROUPS, 4, HEAD_SIZE, PER * WIDE), f32),
-            pltpu.SemaphoreType.DMA((len(work), Gather.SEMS)),
-            pltpu.SemaphoreType.DMA((len(work), Gather.SEMS)),
-            pltpu.SemaphoreType.DMA((2, zn)),
-            pltpu.SemaphoreType.DMA((2, zn)),
-            pltpu.SemaphoreType.DMA((Gather.SEMS,)),
-            pltpu.SemaphoreType.DMA((Gather.SEMS,)),
-            pltpu.SemaphoreType.DMA((3,)),
+            dma((n_first + len(work), Gather.SEMS)),
+            dma((n_first + len(work), Gather.SEMS)),
+            dma((2, zn)),
+            dma((2, zn)),
+            dma((Gather.SEMS,)),
+            dma((Gather.SEMS,)),
+            dma((5,)),
         ],
         compiler_params=pltpu.CompilerParams(
             collective_id=collective_id, has_side_effects=True, vmem_limit_bytes=VMEM_LIMIT
         ),
-    )(q, kv, *arrays)
+    )(x, tables, qkv, fold1, *arrays)
 
 
 class Share:
@@ -1608,9 +1680,137 @@
     )(gq, weights, rest, x, inv, gain, gx1, gain_sums, order)
 
 
-def rotate_lanes(t, cos, low, high):
-    quarter = HEAD_SIZE // 2
-    return t * cos + jnp.roll(t, -quarter, axis=-1) * low + jnp.roll(t, quarter, axis=-1) * high
+def ffn(o_t, x, gy, gain, order_t, out_a, gate_a, up_a, down, rest):
+    f32, b16 = jnp.float32, jnp.bfloat16
+    mbs, width, tokens = o_t.shape
+    rows = mbs * tokens
+    ff = gate_a.shape[1]
+    wa = out_a.shape[0]
+    wb = width - wa
+    rb = wb * 16 // rest.shape[0]
+    chunk = 4 * WIDE
+
+    def kernel(o_ref, x_ref, gy_ref, gain_ref, order_hbm, out_hbm, gate_hbm, up_hbm, down_hbm, rest_hbm,
+               y_ref, gx1_ref, gb_ref, gg_ref, gu_ref, act_ref, h2_ref, h2b_ref, op_ref, opb_ref, go_ref, gain_sum,
+               order_s, out_s, gate_s, up_s, down_s, rest_s, wide, x1, h2, acc, gh, sems):
+        loads = [
+            pltpu.make_async_copy(src, dst, sems.at[i])
+            for i, (src, dst) in enumerate(
+                [(order_hbm, order_s), (rest_hbm, rest_s), (out_hbm, out_s), (gate_hbm, gate_s), (up_hbm, up_s), (down_hbm, down_s)]
+            )
+        ]
+        for c in loads:
+            c.start()
+        loads[0].wait()
+        for mb in range(mbs):
+            at = slice(mb * tokens, (mb + 1) * tokens)
+            t = jnp.dot(order_s[...], o_ref[mb], preferred_element_type=f32)
+            op_ref[:, at] = t[:wa].astype(b16)
+            opb_ref[:, at] = t[wa:].astype(b16)
+            h2[at, :] = transposed_rows(t).astype(b16)
+        loads[1].wait()
+        unfold_rows(rest_s, wide, rb)
+        loads[2].wait()
+        x1[...] = (
+            x_ref[...].astype(f32)
+            + jnp.dot(h2[:, :wa], out_s[...], preferred_element_type=f32)
+            + jnp.dot(h2[:, wa:], wide[:, :width], preferred_element_type=f32)
+        )
+        u = x1[...]
+        inv = lax.rsqrt(jnp.mean(u * u, axis=-1, keepdims=True) + EPSILON)
+        hidden = u * inv * gain_ref[...]
+        h2[...] = hidden.astype(b16)
+        h2_ref[...] = transposed(hidden[:, :wa]).astype(b16)
+        h2b_ref[...] = transposed(hidden[:, wa:]).astype(b16)
+        acc[...] = jnp.zeros(acc.shape, f32)
+        gh[...] = jnp.zeros(gh.shape, f32)
+        for c in loads[3:]:
+            c.wait()
+
+        def one(i, _):
+            at = pl.multiple_of(i * chunk, WIDE)
+            cols = pl.ds(at, chunk)
+            gcols, ucols = pl.ds(width + at, chunk), pl.ds(width + ff + at, chunk)
+            ha, hb = h2[:, :wa], h2[:, wa:]
+            gate = jnp.dot(ha, gate_s[:, cols], preferred_element_type=f32) + jnp.dot(
+                hb, wide[:, gcols], preferred_element_type=f32
+            )
+            up = jnp.dot(ha, up_s[:, cols], preferred_element_type=f32) + jnp.dot(
+                hb, wide[:, ucols], preferred_element_type=f32
+            )
+            ga = nt(gy_ref[...], down_s[cols, :])
+            sig = jax.nn.sigmoid(gate)
+            silu = gate * sig
+            act = silu * up
+            g_gate = (ga * up * sig * (1.0 + gate * (1.0 - sig))).astype(b16)
+            g_up = (ga * silu).astype(b16)
+            gg_ref[:, cols] = g_gate
+            gu_ref[:, cols] = g_up
+            act_ref[cols, :] = transposed(act).astype(b16)
+            acc[...] += jnp.dot(act.astype(b16), down_s[cols, :], preferred_element_type=f32)
+            gh[:, :wa] += nt(g_gate, gate_s[:, cols]) + nt(g_up, up_s[:, cols])
+            gh[:, wa:] += nt(g_gate, wide[:, gcols]) + nt(g_up, wide[:, ucols])
+            return 0
+
+        lax.fori_loop(0, ff // chunk, one, 0)
+        y = (x1[...] + acc[...]).astype(b16)
+        y_ref[...] = jnp.dot(y, order_s[...], preferred_element_type=f32).astype(b16)
+        u = x1[...]
+        inv = lax.rsqrt(jnp.mean(u * u, axis=-1, keepdims=True) + EPSILON)
+        grad = gh[...]
+        gain_sum[...] = jnp.sum(grad * u * inv, axis=0, keepdims=True)
+        weighted = grad * gain_ref[...]
+        inner = jnp.mean(weighted * u, axis=-1, keepdims=True)
+        gx1 = inv * weighted - u * (inv * inv * inv) * inner + gy_ref[...].astype(f32)
+        gx1_ref[...] = gx1
+        gb = gx1.astype(b16)
+        gb_ref[...] = jnp.dot(gb, order_s[...], preferred_element_type=f32).astype(b16)
+        h2[:, :wa] = nt(gb, out_s[...]).astype(b16)
+        h2[:, wa:] = nt(gb, wide[:, :width]).astype(b16)
+        go = jnp.dot(h2[...], order_s[...], preferred_element_type=f32)
+        for mb in range(mbs):
+            go_ref[mb] = transposed(go[mb * tokens : (mb + 1) * tokens]).astype(b16)
+
+    def transposed_rows(t):
+        return jnp.concatenate([t[i : i + WIDE].T for i in range(0, t.shape[0], WIDE)], axis=1)
+
+    any_ = pl.BlockSpec(memory_space=pl.ANY)
+    vmem = pl.BlockSpec(memory_space=pltpu.VMEM)
+    sds = jax.ShapeDtypeStruct
+    return pl.pallas_call(
+        kernel,
+        out_shape=[
+            sds((rows, width), b16),
+            sds((rows, width), f32),
+            sds((rows, width), b16),
+            sds((rows, ff), b16),
+            sds((rows, ff), b16),
+            sds((ff, rows), b16),
+            sds((wa, rows), b16),
+            sds((wb, rows), b16),
+            sds((wa, rows), b16),
+            sds((wb, rows), b16),
+            sds(o_t.shape, b16),
+            sds((1, width), f32),
+        ],
+        in_specs=[vmem] * 4 + [any_] * 6,
+        out_specs=[vmem] * 12,
+        scratch_shapes=[
+            pltpu.VMEM(order_t.shape, b16),
+            pltpu.VMEM(out_a.shape, b16),
+            pltpu.VMEM(gate_a.shape, b16),
+            pltpu.VMEM(up_a.shape, b16),
+            pltpu.VMEM(down.shape, b16),
+            pltpu.VMEM(rest.shape, b16),
+            pltpu.VMEM((wb, 16 // rb * rest.shape[1]), b16),
+            pltpu.VMEM((rows, width), f32),
+            pltpu.VMEM((rows, width), b16),
+            pltpu.VMEM((rows, width), f32),
+            pltpu.VMEM((rows, width), f32),
+            pltpu.SemaphoreType.DMA((6,)),
+        ],
+        compiler_params=pltpu.CompilerParams(vmem_limit_bytes=VMEM_LIMIT),
+    )(o_t, x, gy, gain, order_t, out_a, gate_a, up_a, down, rest)
 
 
 def lane_tables(positions):
@@ -1619,14 +1819,8 @@
     angles = positions.astype(jnp.float32)[:, None] * frequency[None, :]
     cos, sin = jnp.cos(angles), jnp.sin(angles)
     none = jnp.zeros_like(sin)
-
-    def full(a, b, still):
-        head = jnp.concatenate([a, b], axis=1)
-        keys = jnp.tile(head, (1, HALF_GROUPS))
-        still = jnp.full_like(keys, still)
-        return jnp.concatenate([keys, still, keys, still, jnp.tile(head, (1, QUERY_HEADS))], axis=1)
-
-    return full(cos, cos, 1.0), full(-sin, none, 0.0), full(none, sin, 0.0)
+    full = lambda a, b: jnp.concatenate([a, b, a, b], axis=1)
+    return jnp.stack([full(cos, cos), full(-sin, none), full(none, sin)])
 
 
 def fast_device(
@@ -1703,87 +1897,41 @@
             jnp.concatenate([out_p[ra:], gate_weight[ra:], up_weight[ra:]], axis=1), ((0, 0), (0, pad2))
         )
     )
-    qkv_a, b1g = gather_all([qkv, b1], [ra, 16], [(1, 1), (1, 1)], 1)
-
-    def unfolded(t):
-        cols = t.shape[-1]
-        return t.reshape(dn, fold, rb, cols).transpose(0, 2, 1, 3).reshape(dn * rb, fold * cols)
-
     flat = lambda t: t.reshape(-1, t.shape[-1])
-    qkv_a, b1u = flat(qkv_a), unfolded(b1g)
-    qkv_b = b1u[:, :qkv_w]
-    gains_all = b1u[:, qkv_w : qkv_w + own].reshape(dn, rb, own)
-    in_order = lambda t: jnp.concatenate([t[:, :ra].reshape(-1), t[:, ra:].reshape(-1)]).astype(f32)
-    gain1, gain2 = in_order(gains_all[:, 0]), in_order(gains_all[:, 1])
-
-    def mm(h, a, b):
-        return matrix_multiply(h[:, :wa], a) + matrix_multiply(h[:, wa:], b)
-
-    def mm_back(g, a, b):
-        return jnp.concatenate([back_product(g, a), back_product(g, b)], axis=1)
-
     c, w = lax.axis_index("ctx"), lax.axis_index("ws")
-    places = query_places(c, w, tokens, cn, wn)
-    cos, low, high = (jnp.tile(t, (mbs, 1)) for t in lane_tables(places))
-    q_at = 2 * hid
-    x = x_low.astype(f32)
-    hn, inv1 = normalize(x, gain1)
-    hn = hn.astype(b16)
-    proj = rotate_lanes(mm(hn, qkv_a, qkv_b), cos, low, high)
-    kv = proj[:, : 2 * hid].astype(b16).reshape(mbs, tokens, 2 * hid)
-    q = (proj[:, 2 * hid :] * HEAD_SIZE**-0.5).astype(b16)
-    q = q.reshape(mbs, tokens, q_width).transpose(0, 2, 1)
-    o_t, qh, kvg, oh, lse, out_a, gate_a, up_a, down_a, b2g = gather_attend(
-        q,
-        kv,
+    tables = lane_tables(query_places(c, w, tokens, cn, wn))
+    (o_t, qh, kvg, oh, lse, qkv_a, qkv_b, hn_t, hn_bt, inv1, gains, out_a, gate_a, up_a, down_a, b2g) = gather_attend(
+        x_low,
+        tables,
+        qkv,
+        b1,
         [out_p, gate_weight, up_weight, down_p, b2],
         [ra, ra, ra, down_p.shape[0], 16],
         [(1, 1), (1, 2), (1, 2), (2, 1), (1, 1)],
         2,
     )
-    out_a, gate_a, up_a, down_w = map(flat, (out_a, gate_a, up_a, down_a))
-    b2u = unfolded(b2g)
-    out_b = b2u[:, :width]
-    gate_b, up_b = b2u[:, width : width + ff], b2u[:, width + ff : width + 2 * ff]
-    o_p = to_order(o_t.transpose(0, 2, 1).reshape(rows, q_width))
-    x1 = x + mm(o_p, out_a, out_b)
-    h2, inv2 = normalize(x1, gain2)
-    h2 = h2.astype(b16)
-    gate = mm(h2, gate_a, gate_b)
-    up = mm(h2, up_a, up_b)
-    sig = jax.nn.sigmoid(gate)
-    silu = gate * sig
-    act = (silu * up).astype(b16)
-    out = from_order((x1 + matrix_multiply(act, down_w)).astype(b16))
-    gy = gy_low.astype(f32)
-    ga = back_product(gy_low, down_w)
-    g_gate = (ga * up * sig * (1.0 + gate * (1.0 - sig))).astype(b16)
-    g_up = (ga * silu).astype(b16)
-    gh2 = mm_back(g_gate, gate_a, gate_b) + mm_back(g_up, up_a, up_b)
-    mid, gain2_sum = normalize_back(x1, inv2, gain2, gh2)
-    gx1 = mid + gy
-    gb = gx1.astype(b16)
-    gattn = from_order(mm_back(gb, out_a, out_b).astype(b16))
-    gb_plain = from_order(gb)
+    qkv_a, out_a, gate_a, up_a, down_w = map(flat, (qkv_a, out_a, gate_a, up_a, down_a))
+    gain1, gain2 = gains[:1], gains[1:]
+    out, gx1, gb_plain, g_gate, g_up, act_t, h2_t, h2_bt, o_pt, o_pbt, go_t, gain2_sum = ffn(
+        o_t, x_low, gy_low, gain2, order.T, out_a, gate_a, up_a, down_w, flat(b2g)
+    )
     gy_plain = cotangent.reshape(rows, width)
-    left = lambda t: t.T.reshape(zn, 2, 2, 2, -1, rows)
-    wide = 2 * HEAD_SIZE
-    head_tables = jnp.stack([t[:tokens, q_at : q_at + wide] for t in (cos, low, high)])
+    left = lambda t: t.reshape(zn, 2, 2, 2, -1, rows)
     gq, r_down, r_gate, r_up, r_out, r_b2, r_qkv, r_b1 = scatter_attend(
-        gattn.reshape(mbs, tokens, q_width).transpose(0, 2, 1),
+        go_t,
         qh,
         kvg,
         oh,
         lse,
-        head_tables,
-        [left(act), left(h2[:, :wa]), left(o_p[:, :wa]), left(hn[:, :wa])],
-        [h2[:, wa:].T, o_p[:, wa:].T, hn[:, wa:].T],
+        tables,
+        [left(act_t), left(h2_t), left(o_pt), left(hn_t)],
+        [h2_bt, o_pbt, hn_bt],
         [gy_plain, gb_plain, g_gate, g_up],
         ((rest_w + pad2) // fold, (qkv_w + pad1) // fold),
         3,
     )
     input_grad, gain_sums = finish(
-        gq, qkv_a, qkv_b, x_low, inv1, gain1[None], gx1, gain2_sum[None], order, 4
+        gq, qkv_a, qkv_b, x_low, inv1, gain1, gx1, gain2_sum, order, 4
     )
     device_at = c * wn + w
 

time: 506 us -> 407 us (0.80)
  local copies, waits for them, and re-layouts: 62.8 us -> 9.91 us
  matrix products: 45.7 us -> 3.8 us
  other arithmetic: 18.3 us -> 10.6 us
  Pallas kernels: 370 us -> 376 us
    dot_general x18 -> x0, matrix products: 41.7 us -> none  [the longest x8 14.9 us: matrix_multiply(): return jnp.dot(left, right, preferred_element_type=jnp.float32)]
    unnamed x98 -> x20, local copies, waits for them, and re-layouts: 18.3 us -> 1.62 us
    concatenate x14 -> x0, local copies, waits for them, and re-layouts: 9.76 us -> none  [the longest x6 9.16 us: full(): jnp.concatenate([keys, still, keys, still, jnp.tile(head, (1, QUERY_HEADS...]
    reshape x6 -> x0, local copies, waits for them, and re-layouts: 7.52 us -> none  [the longest x4 5.4 us: unfolded(): t.reshape(dn, fold, rb, cols).transpose(0, 2, 1, 3)]
    transpose x10 -> x0, local copies, waits for them, and re-layouts: 7.23 us -> none  [the longest x4 3.96 us: fast_device(): left = lambda t: t.T.reshape(zn, 2, 2, 2, -1, rows)]
    slice x9 -> x1, local copies, waits for them, and re-layouts: 8.58 us -> 1.38 us  [fast_device(): gain1, gain2 = (gains[:1], gains[1:])]
where the time goes in v4:
time: 407 us; the launch traced here: 402 us
  Pallas kernels  376 us (92%)
  other arithmetic  10.6 us (3%)
  local copies, waits for them, and re-layouts  9.91 us (2%)
    pallas_call x1, Pallas kernels, scatter_attend(): pl.pallas_call(kernel, out_shape=[jax.ShapeDtypeStruct((all_rows, qkv_w),...  169 us
    pallas_call x1, Pallas kernels, gather_attend(): pl.pallas_call(kernel, out_shape=[sds((mbs, q_rows, tokens), b16), sds(bl...  157 us
    pallas_call x1, Pallas kernels, ffn(): pl.pallas_call(kernel, out_shape=[sds((rows, width), b16), sds((rows, wid...  29.6 us
    pallas_call x1, Pallas kernels, finish(): pl.pallas_call(kernel, out_shape=[jax.ShapeDtypeStruct(x.shape, b16), jax...  20.1 us

profile of v4, /device:TPU:0, one launch (start us, length us, event | category | flops | bytes accessed | tf_op | source)
XLA Modules:
  0.0 401.7 jit_solution(11703904462874633297)
XLA Ops:
  0.7 0.7 fusion.48
  1.4 0.9 fusion.62
  2.3 1.0 concatenate.49.refs_2_
  3.3 0.0 copy-start.1
  3.3 0.6 reshape.173.refs_3_
  3.9 0.3 multiply_cosine_fusion
  4.3 0.2 maximum_bitcast_fusion.1
  4.5 0.7 pad_maximum_fusion.2.refs_1_.refs_5_
  5.2 3.8 fusion.3
  9.0 0.0 copy-done.1
  9.0 0.0 slice-done
  9.0 0.0 slice-done.1
  9.1 0.6 reshape.175.refs_8_
  9.7 0.6 slice.103.refs_4_
  10.4 0.7 slice.104.refs_7_
  11.1 1.1 fusion.59
  12.2 3.1 fusion
  15.3 157.0 %shard_map.194 = (bf16[2,1152,128]{2,1,0:T(8,128)(2,1)}, bf16[4,576,128]{2,1,0:T(8,128)(2,1)}, bf16[4,2,2,2,128,384]{5,4,3,2,1,0:T(8,128)(2,1)}, bf16[4,576,128]...) custom-call(bf16[256,1152]{1,0:T(8,128)(2,1)} %get-tuple-element.88., ...), custom_call_target="tpu_custom_call" | custom-call | tf_op jit(solution)/shard_map/pallas_call | solution.py:1127
  172.3 1.4 fusion.64
  173.7 29.6 %shard_map.195 = (bf16[256,1152]{1,0:T(8,128)(2,1)}, f32[256,1152]{1,0:T(8,128)}, bf16[256,1152]{1,0:T(8,128)(2,1)}, bf16[256,3072]{1,0:T(8,128)(2,1)}, bf16[256...) custom-call(bf16[2,1152,128]{2,1,0:T(8,128)(2,1)} %get-tuple-element, ...), custom_call_target="tpu_custom_call" | custom-call | tf_op jit(solution)/shard_map/pallas_call | solution.py:1780
  203.3 169.2 %shard_map.196 = (bf16[256,1920]{1,0:T(8,128)(2,1)}, f32[96,1152]{1,0:T(8,128)}, f32[32,3072]{1,0:T(8,128)}, f32[32,3072]{1,0:T(8,128)}, f32[32,1152]{1,0:T(8,12...) custom-call(bf16[2,1152,128]{2,1,0:T(8,128)(2,1)} %get-tuple-element.57.refs_0_, ...), custom_call_target="tpu_custom_call" | custom-call | tf_op jit(solution)/shard_map/pallas_call | solution.py:1580
  372.5 0.0 copy-start.8
  372.6 0.0 copy-start.7
  372.6 0.0 copy-start.6
  372.6 0.0 copy-start.5
  372.6 0.0 copy-start.4
  372.6 20.1 %shard_map.197 = (bf16[256,1152]{1,0:T(8,128)(2,1)}, f32[8,1152]{1,0:T(8,128)}) custom-call(bf16[256,1920]{1,0:T(8,128)(2,1)} %get-tuple-element.72.gq_ref, bf16[1024,1920]{1,0:T(8,128)(2,1)} %bitcast.45, bf16[128,1920]{1,0:T(8,128)(2,1)} %get-tuple-element.74.r_ref, bf16[256,1152]{1,0:T(8,128)(2,1)} %get-tuple-element.88.refs_0_.x_ref, ...), custom_call_target="tpu_custom_call" | custom-call | tf_op jit(solution)/shard_map/pallas_call | solution.py:1665
  392.7 0.0 copy-start
  392.8 0.0 copy-start.2
  392.8 0.9 fusion.61
  393.6 0.1 fusion.54
  393.7 0.1 fusion.53
  393.8 0.6 pad_maximum_fusion.7
  394.4 0.1 fusion.51
  394.4 0.1 fusion.52
  394.5 0.6 pad_maximum_fusion.6
  395.2 0.0 copy-done.6
  395.2 0.7 pad_maximum_fusion.3
  395.9 0.0 copy-done.5
  395.9 0.8 pad_maximum_fusion.1
  396.7 0.8 pad_maximum_fusion
  397.6 0.1 fusion.19
  397.6 0.6 fusion.18
  398.3 0.7 fusion.12
  399.0 0.7 pad_maximum_fusion.4
  399.7 0.8 copy.26
  400.5 0.0 copy-done.3
  400.5 0.8 copy.27
  (21 shorter events, 0.2 us)
Async XLA Ops:
  3.3 5.7 %copy-start.1 = (bf16[36,1920]{1,0:T(8,128)(2,1)}, bf16[36,1920]{1,0:T(8,128)(2,1)S(1)}, u32[]{:S(2)}) copy-start(bf16[36,1920]{1,0:T(8,128)(2,1)S(1)} %concatenate.49.refs_2_) | copy-start | bytes 414724
  5.2 3.8 slice-start
  5.2 3.8 slice-start.1
  372.5 22.6 %copy-start.8 = (f32[16,512]{1,0:T(8,128)S(1)}, f32[16,512]{1,0:T(8,128)}, u32[]{:S(2)}) copy-start(f32[16,512]{1,0:T(8,128)} %get-tuple-element.81) | copy-start | bytes 98308
  372.6 22.6 %copy-start.7 = (f32[16,1920]{1,0:T(8,128)S(1)}, f32[16,1920]{1,0:T(8,128)}, u32[]{:S(2)}) copy-start(f32[16,1920]{1,0:T(8,128)} %get-tuple-element.83) | copy-start | bytes 368644
  372.6 22.7 %copy-start.6 = (f32[32,1152]{1,0:T(8,128)S(1)}, f32[32,1152]{1,0:T(8,128)}, u32[]{:S(2)}) copy-start(f32[32,1152]{1,0:T(8,128)} %get-tuple-element.82) | copy-start | bytes 442372
  372.6 23.4 %copy-start.5 = (f32[32,3072]{1,0:T(8,128)S(1)}, f32[32,3072]{1,0:T(8,128)}, u32[]{:S(2)}) copy-start(f32[32,3072]{1,0:T(8,128)} %get-tuple-element.85) | copy-start | bytes 1179652
  372.6 24.2 %copy-start.4 = (f32[32,3072]{1,0:T(8,128)S(1)}, f32[32,3072]{1,0:T(8,128)}, u32[]{:S(2)}) copy-start(f32[32,3072]{1,0:T(8,128)} %get-tuple-element.84) | copy-start | bytes 1179652
  392.7 4.8 %copy-start = (f32[32,1920]{1,0:T(8,128)S(1)}, f32[32,1920]{1,0:T(8,128)}, u32[]{:S(2)}) copy-start(f32[32,1920]{1,0:T(8,128)} %get-tuple-element.80) | copy-start | bytes 737284
  392.8 6.9 %copy-start.2 = (bf16[256,1152]{1,0:T(8,128)(2,1)S(1)}, bf16[256,1152]{1,0:T(8,128)(2,1)}, u32[]{:S(2)}) copy-start(bf16[256,1152]{1,0:T(8,128)(2,1)} %get-tuple-element.78) | copy-start | bytes 1769476
  395.1 5.4 %copy-start.3 = (f32[96,1152]{1,0:T(8,128)S(1)}, f32[96,1152]{1,0:T(8,128)}, u32[]{:S(2)}) copy-start(f32[96,1152]{1,0:T(8,128)} %get-tuple-element.133) | copy-start | bytes 1327108

commit v5 on v4

--- a/solution.py
+++ b/solution.py
@@ -652,15 +652,28 @@
                 c.wait_send()
 
 
-def stage_step(items, stages, t):
-    for n in range(stages):
-        if 0 <= t - n < len(items) and items[t - n] is not None:
+def stage_step(items, stages, t, between=None):
+    for n in stages:
+        if 0 <= t - n < len(items):
             items[t - n].stage(n)
-
-
-def run_stages(items, stages):
-    for t in range(len(items) + stages - 1):
-        stage_step(items, stages, t)
+            if between is not None:
+                between()
+
+
+GATHER_STAGES = (0, 1, 2, 3, 4)
+SUM_STAGES = (0, 1, 2, 3)
+
+
+def portions(step, total, parts):
+    done = [0]
+
+    def call(all_=False):
+        upto = total if all_ else min(total, done[0] + -(-total // parts))
+        if upto > done[0]:
+            lax.fori_loop(done[0], upto, step, 0)
+            done[0] = upto
+
+    return call
 
 
 def pieces_of(rows, cols, nrow, ncol):
@@ -879,6 +892,7 @@
 
 
 STEPS = 38
+FORWARD_PARTS = 20
 
 
 def visible(p, j, y, w, cn, wn, rows):
@@ -983,14 +997,14 @@
         qx = Exchange(lambda zz: heads_of(q_s, zz), lambda zz: qh.at[zz], xs.at[0], xr.at[0], zn)
         ox = Exchange(lambda zz: oh.at[zz], lambda zz: heads_of(o_out, zz), xs.at[1], xr.at[1], zn)
         for s in range(n_first + 1):
-            stage_step(items, 5, s)
+            stage_step(items, GATHER_STAGES, s)
         xf = x_ref[...].astype(f32)
         inv = lax.rsqrt(jnp.mean(xf * xf, axis=-1, keepdims=True) + EPSILON)
         inv_out[...] = inv
         m_s[...] = jnp.full(m_s.shape, NEG, f32)
         l_s[...] = jnp.zeros(l_s.shape, f32)
         acc[...] = jnp.zeros(acc.shape, f32)
-        stage_step(items, 5, n_first + 1)
+        stage_step(items, GATHER_STAGES, n_first + 1)
         unfold_rows(f1[...].reshape(dn * 16, fold1.shape[1]), wide, rb)
         lane = lax.broadcasted_iota(jnp.int32, (WIDE, width), 1)
         local = jnp.where(lane < wa, lax.rem(lane, ra), ra + lax.rem(lane - wa, rb))
@@ -1005,7 +1019,7 @@
         hn[...] = normed.astype(b16)
         hn_out[...] = transposed(normed[:, :wa]).astype(b16)
         hnb_out[...] = transposed(normed[:, wa:]).astype(b16)
-        stage_step(items, 5, n_first + 2)
+        stage_step(items, GATHER_STAGES, n_first + 2)
 
         low_lanes = lax.broadcasted_iota(jnp.int32, (tokens, WIDE), 1) < HEAD_SIZE
         quarter = HEAD_SIZE // 2
@@ -1035,7 +1049,7 @@
         project(0)
         project(1)
         kvx.stage(0)
-        stage_step(items, 5, n_first + 3)
+        stage_step(items, GATHER_STAGES, n_first + 3)
         for c in range(2, qkv_w // KV_LANES):
             project(c)
         qx.start()
@@ -1047,7 +1061,7 @@
             s.start()
         kvx.stage(1)
         kvx.stage(2)
-        stage_step(items, 5, n_first + 4)
+        stage_step(items, GATHER_STAGES, n_first + 4)
         kvx.stage(3)
         qx.arrived()
         for half in range(2):
@@ -1096,21 +1110,17 @@
             return 0
 
         last = len(items) + 4
-        t = 0
         start = n_first + 5
-        per_step = -(-STEPS // (last - start - 2))
+        attend = portions(step, STEPS, FORWARD_PARTS)
         for s in range(start, last):
-            upto = min(STEPS, t + per_step)
-            if t < upto:
-                lax.fori_loop(t, upto, step, 0)
-                t = upto
-                if t == STEPS:
-                    unpair(lambda g, p: acc[g, p] / l_s[g, p], oh)
-                    ox.start()
-                    saves.append(pltpu.make_async_copy(oh, oh_out, save.at[2]))
-                    saves[-1].start()
-                    lse_out[...] = m_s[...] + jnp.log(l_s[...])
-            stage_step(items, 5, s)
+            stage_step(items, GATHER_STAGES, s, attend if s < last - 2 else None)
+            if s == last - 3:
+                attend(True)
+                unpair(lambda g, p: acc[g, p] / l_s[g, p], oh)
+                ox.start()
+                saves.append(pltpu.make_async_copy(oh, oh_out, save.at[2]))
+                saves[-1].start()
+                lse_out[...] = m_s[...] + jnp.log(l_s[...])
         ox.arrived()
         ox.sent()
         qx.sent()
@@ -1267,7 +1277,11 @@
                 c.wait_send()
 
 
-def scatter_attend(do, qh, kvg, oh, lse, tables, lefts, rests, rights, plan, collective_id):
+ORDER = (0, 1, 2, 3, 4, 5, 6, 7, 8, 9, 10, 11, 12)
+BACK_SPAN, BACK_PARTS = 3, 10
+
+
+def scatter_attend(do, qh, kvg, oh, lse, tables, lefts, rests, rights, plan, last, collective_id):
     cn, wn = lax.axis_size("ctx"), lax.axis_size("ws")
     zn = cn // 2
     mbs, q_rows, tokens = do.shape
@@ -1287,7 +1301,8 @@
     half_ff = ff // 2
     sizes = (
         [(ra, width)] * n_down
-        + [(ra, half_ff)] * 4
+        + [(ra, half_ff)] * 3
+        + [(ra, half_ff // 2)] * 2
         + [(ra, width), (16, rest_w), (ra, 2 * KV_LANES), (ra, q_rows), (16, qkv_rest_w)]
     )
     max_cols = max(s[1] for s in sizes)
@@ -1307,18 +1322,22 @@
         (act_rows, width), (ra, ff), (ra, ff), (ra, width), (16, rest_w), (ra, qkv_w), (16, qkv_rest_w)
     ]
     n_out = len(outs_shape)
+    n_last = len(last)
 
     def kernel(*refs):
-        do_ref, qh, kvg, oh_ref, lse_ref, tab = refs[:6]
+        do_ref, qh_ref, kvg_ref, oh_ref, lse_ref, tab = refs[:6]
         ins = refs[6 : 6 + n_in]
-        gq = refs[6 + n_in]
-        outs = refs[7 + n_in : 7 + n_in + n_out]
-        rest = refs[7 + n_in + n_out :]
+        at = 6 + n_in
+        w_ref, r_ref, x_ref, inv_ref, gain_ref, gx1_ref, gain2_ref, order_ref = refs[at : at + n_last]
+        at += n_last
+        outs = refs[at : at + n_out]
+        input_grad, total = refs[at + n_out : at + n_out + 2]
+        rest = refs[at + n_out + 2 :]
         bufs, rest = rest[: len(scratch)], rest[len(scratch) :]
         pairs, rest = rest[: len(shares)], rest[len(shares) :]
-        (held, gq_other, dkv_in, oh, gh, qt, dot_, kt, delta, dq, dkv, give) = rest[:12]
-        kb = rest[12:16]
-        send, recv, ps, pr, pl_, xs, xr, ks, kr = rest[16:]
+        (held, gq, gq_other, dkv_in, oh, gh, give, got) = rest[:8]
+        kb = rest[8:12]
+        send, recv, ps, pr, pl_, xs, xr, ks, kr, gs, gr, loads = rest[12:]
         dqh, dq_in = gh, oh
         greet(zn)
         z, y, x, k = place()
@@ -1419,15 +1438,17 @@
 
         gq_both = (gq, gq_other)
         makes = [product(ACT, both(GY), 0, ra * i, (ACT, GY)) for i in range(n_down)]
-        makes += [product(H2, both(g), lo, 0, (H2, g)) for g in (GG, GU) for lo in (0, half_ff)]
+        ffn_parts = [(GG, 0, half_ff), (GG, half_ff, half_ff), (GU, 0, half_ff)]
+        ffn_parts += [(GU, half_ff, half_ff // 2), (GU, half_ff + half_ff // 2, half_ff // 2)]
+        makes += [product(H2, both(g), lo, 0, (H2, g)) for g, lo, _ in ffn_parts]
         makes += [product(OT, both(GB), 0, 0, (OT, GB)), rest_product]
         makes += [product(HN, gq_both, 0, 0, (HN,)), product(HN, gq_both, 2 * KV_LANES, 0, (HN,)), qkv_rest_product]
         targets = [outs[0].at[pl.ds(ra * i, ra), :] for i in range(n_down)]
-        targets += [outs[g].at[:, pl.ds(lo, half_ff)] for g in (1, 2) for lo in (0, half_ff)]
+        targets += [outs[1 if g == GG else 2].at[:, pl.ds(lo, n)] for g, lo, n in ffn_parts]
         targets += [outs[3], outs[4], outs[5].at[:, pl.ds(0, 2 * KV_LANES)], outs[5].at[:, pl.ds(2 * KV_LANES, q_rows)], outs[6]]
         items = []
         for i, (nr, nc) in enumerate(sizes):
-            slot = held.at[i % ring, :, :, :, pl.ds(0, nr), pl.ds(0, nc)]
+            slot = held.at[ORDER.index(i) % ring, :, :, :, pl.ds(0, nr), pl.ds(0, nc)]
             items.append(
                 Sum(makes[i], slot, bufs[3 * i : 3 * i + 3], targets[i], send.at[i], recv.at[i], zn)
             )
@@ -1436,64 +1457,105 @@
         gx.start()
         for i in (ACT, GY, H2, GG, GU, OT, GB, H2B, OTB, HN, HNB):
             share[i].start()
-        dq[...] = jnp.zeros(dq.shape, f32)
-
-        def clear(i, _):
-            dkv[i] = jnp.zeros(dkv.shape[1:], f32)
-            return 0
-
-        lax.fori_loop(0, zn, clear, 0)
-        stage_step(items, 4, 0)
-
-        def turn(j, block):
-            flat = {b: turned(block(b)) for b in sorted({key_slot(g)[0] for g in groups})}
-            for g in groups:
-                b, side = key_slot(g)
-                kt[j, g] = flat[b][side * HEAD_SIZE : (side + 1) * HEAD_SIZE]
-
-        by_span(turn, kvg, cn, rows)
-        stage_step(items, 4, 1)
-        gx.arrived()
-        load_o.wait()
-        for half_ in range(2):
-            for zp in range(2):
-                p = pair_index(half_, zp)
+        order = [items[i] for i in ORDER]
+        at_qkv = ORDER.index(n_items - 3)
+        n_back = BACK_SPAN
+        stage_step(order, SUM_STAGES, 0)
+
+        def attention_back(kvg, qh, qt, dot_, kt, delta, dq, dkv):
+            load_kv = pltpu.make_async_copy(kvg_ref, kvg, loads.at[0])
+            load_q = pltpu.make_async_copy(qh_ref, qh, loads.at[1])
+            load_kv.start()
+            load_q.start()
+            dq[...] = jnp.zeros(dq.shape, f32)
+
+            def clear(i, _):
+                dkv[i] = jnp.zeros(dkv.shape[1:], f32)
+                return 0
+
+            lax.fori_loop(0, zn, clear, 0)
+            def turn(j, block):
+                flat = {b: turned(block(b)) for b in sorted({key_slot(g)[0] for g in groups})}
                 for g in groups:
-                    g_tile = pair_tile(gh, g, half_, zp)
-                    o_tile = pair_tile(oh, g, half_, zp)
-                    delta[g, p] = jnp.sum(g_tile * o_tile, axis=0, keepdims=True)
-                    set_padded(qt, g, p, pair_tile(qh, g, half_, zp), key_slot(g)[1])
-                    set_padded(dot_, g, p, g_tile, value_slot(g)[1])
-
-        def step(t, _):
-            p, j, zz, yy, late, edge = walk(t, y, cn)
-
-            def run(masked):
-                seen = visible(p, j, y, w, cn, wn, rows) if masked else None
-                blocks = [key_block(kvg, zz, yy, late, rows, b) for b in range(KV_LANES // WIDE)]
-                sums = [None] * len(blocks)
-
-                def put(b, v):
-                    sums[b] = v if sums[b] is None else sums[b] + v
-
-                for g in groups:
-                    s = jnp.dot(blocks[key_slot(g)[0]], qt[g, p], preferred_element_type=f32)
-                    if masked:
-                        s = jnp.where(seen, s, NEG)
-                    e = jnp.exp(s - lse_ref[g, p])
-                    dp = jnp.dot(blocks[value_slot(g)[0]], dot_[g, p], preferred_element_type=f32)
-                    ds = (e * (dp - delta[g, p])).astype(b16)
-                    put(value_slot(g)[0], nt(e.astype(b16), dot_[g, p]))
-                    put(key_slot(g)[0], nt(ds, qt[g, p]))
-                    dq[g, p] += jnp.dot(kt[j, g], ds, preferred_element_type=f32)
-                for b, v in enumerate(sums):
-                    dkv[zz, yy, :, :, pl.ds(late, rows), WIDE * b : WIDE * b + WIDE] += v.reshape(
-                        2, 2, rows, WIDE
-                    )
-
-            pl.when(edge)(lambda: run(True))
-            pl.when(jnp.logical_not(edge))(lambda: run(False))
-            return 0
+                    b, side = key_slot(g)
+                    kt[j, g] = flat[b][side * HEAD_SIZE : (side + 1) * HEAD_SIZE]
+
+            load_kv.wait()
+            by_span(turn, kvg, cn, rows)
+            stage_step(order, SUM_STAGES, 1)
+            gx.arrived()
+            load_o.wait()
+            load_q.wait()
+            for half_ in range(2):
+                for zp in range(2):
+                    p = pair_index(half_, zp)
+                    for g in groups:
+                        g_tile = pair_tile(gh, g, half_, zp)
+                        o_tile = pair_tile(oh, g, half_, zp)
+                        delta[g, p] = jnp.sum(g_tile * o_tile, axis=0, keepdims=True)
+                        set_padded(qt, g, p, pair_tile(qh, g, half_, zp), key_slot(g)[1])
+                        set_padded(dot_, g, p, g_tile, value_slot(g)[1])
+
+            def step(t, _):
+                p, j, zz, yy, late, edge = walk(t, y, cn)
+
+                def run(masked):
+                    seen = visible(p, j, y, w, cn, wn, rows) if masked else None
+                    blocks = [key_block(kvg, zz, yy, late, rows, b) for b in range(KV_LANES // WIDE)]
+                    sums = [None] * len(blocks)
+
+                    def put(b, v):
+                        sums[b] = v if sums[b] is None else sums[b] + v
+
+                    for g in groups:
+                        s = jnp.dot(blocks[key_slot(g)[0]], qt[g, p], preferred_element_type=f32)
+                        if masked:
+                            s = jnp.where(seen, s, NEG)
+                        e = jnp.exp(s - lse_ref[g, p])
+                        dp = jnp.dot(blocks[value_slot(g)[0]], dot_[g, p], preferred_element_type=f32)
+                        ds = (e * (dp - delta[g, p])).astype(b16)
+                        put(value_slot(g)[0], nt(e.astype(b16), dot_[g, p]))
+                        put(key_slot(g)[0], nt(ds, qt[g, p]))
+                        dq[g, p] += jnp.dot(kt[j, g], ds, preferred_element_type=f32)
+                    for b, v in enumerate(sums):
+                        dkv[zz, yy, :, :, pl.ds(late, rows), WIDE * b : WIDE * b + WIDE] += v.reshape(
+                            2, 2, rows, WIDE
+                        )
+
+                pl.when(edge)(lambda: run(True))
+                pl.when(jnp.logical_not(edge))(lambda: run(False))
+                return 0
+
+            attend = portions(step, STEPS, BACK_PARTS)
+            for s in range(2, 2 + n_back):
+                stage_step(order, SUM_STAGES, s, attend)
+            attend(True)
+
+            def pack(i, _):
+                for yy in range(2):
+                    for xx in range(2):
+                        kb[0][i, yy, xx] = dkv[i, yy, xx, k].astype(b16)
+                        give[i, yy, xx] = dkv[i, yy, xx, 1 - k].astype(b16)
+                return 0
+
+            lax.fori_loop(0, zn, pack, 0)
+            kvx.stage(0)
+            unpair(lambda g, p: dq[g, p] * scale, dqh)
+            dx.start()
+
+        stat = (HALF_GROUPS, 4, 1, PER * WIDE)
+        tile = (HALF_GROUPS, 4, WIDE, PER * WIDE)
+        pl.run_scoped(
+            attention_back,
+            pltpu.VMEM(kvg_ref.shape, b16),
+            pltpu.VMEM(qh_ref.shape, b16),
+            pltpu.VMEM(tile, b16),
+            pltpu.VMEM(tile, b16),
+            pltpu.VMEM((2 * cn, HALF_GROUPS, HEAD_SIZE, wn * rows), b16),
+            pltpu.VMEM(stat, f32),
+            pltpu.VMEM((HALF_GROUPS, 4, HEAD_SIZE, PER * WIDE), f32),
+            pltpu.VMEM((zn, 2, 2, 2, tokens, KV_LANES), f32),
+        )
 
         def rope_back():
             low_lanes = lax.broadcasted_iota(jnp.int32, (tokens, WIDE), 1) < HEAD_SIZE
@@ -1529,75 +1591,113 @@
                     lo = 2 * KV_LANES + WIDE * b
                     gq[at, lo : lo + WIDE] = back(t, "turn").astype(b16)
 
-        first = n_items - 3
-        order = items[:first] + [None, None] + items[first:]
-        t = 0
-        per_step = -(-STEPS // (first - 3))
-        kv_stage = 0
-        for s in range(2, len(order) + 3):
-            if t < STEPS:
-                upto = min(STEPS, t + per_step)
-                lax.fori_loop(t, upto, step, 0)
-                t = upto
-                if t == STEPS:
-
-                    def pack(i, _):
-                        for yy in range(2):
-                            for xx in range(2):
-                                kb[0][i, yy, xx] = dkv[i, yy, xx, k].astype(b16)
-                                give[i, yy, xx] = dkv[i, yy, xx, 1 - k].astype(b16)
-                        return 0
-
-                    lax.fori_loop(0, zn, pack, 0)
-                    kvx.stage(0)
-                    kv_stage = 1
-                    unpair(lambda g, p: dq[g, p] * scale, dqh)
-                    dx.start()
-            elif kv_stage < 4 and s <= first + 1:
-                kvx.stage(kv_stage)
-                kv_stage += 1
-            if s == first + 2:
-                while kv_stage < 5:
+        def gains_and_input(w_s, r_s, order_s, x_s, gx_s, ghn, low):
+            moves = [
+                pltpu.make_async_copy(src, dst, loads.at[i])
+                for i, (src, dst) in enumerate(
+                    [(w_ref, w_s), (r_ref, r_s), (order_ref, order_s), (x_ref, x_s), (gx1_ref, gx_s)]
+                )
+            ]
+            for c in moves:
+                c.start()
+            wa = w_s.shape[0]
+            chips = [device(z, y, x, 1 - k), device(z, y, 1 - x, k), device(z, 1 - y, x, k)]
+            steps = [remote(total, got.at[i], gs.at[i], gr.at[i], chips[i]) for i in range(3)]
+            ends = [
+                remote(total, got.at[2 + j], gs.at[2 + j], gr.at[2 + j], device(lax.rem(z + j, zn), y, x, k))
+                for j in range(1, zn)
+            ]
+
+            def first():
+                for c in moves:
+                    c.wait()
+                ghn[:, :wa] = nt(gq[...], w_s[...])
+                ghn[:, wa:] = nt(gq[...], r_s[...])
+
+            def second():
+                xf, inv, grad = x_s[...].astype(f32), inv_ref[...], ghn[...]
+                total[...] = jnp.zeros(total.shape, f32)
+                total[0:1, :] = jnp.sum(grad * xf * inv, axis=0, keepdims=True)
+                total[1:2, :] = gain2_ref[...]
+                steps[0].start()
+                weighted = grad * gain_ref[...]
+                inner = jnp.mean(weighted * xf, axis=-1, keepdims=True)
+                low[...] = (gx_s[...] + inv * weighted - xf * (inv * inv * inv) * inner).astype(b16)
+
+            def add(i):
+                steps[i].wait()
+                total[...] = total[...] + got[i]
+                for c in [steps[i + 1]] if i < 2 else ends:
+                    c.start()
+
+            def third():
+                input_grad[...] = jnp.dot(low[...], order_s[...], preferred_element_type=f32).astype(b16)
+
+            jobs = [first, second, lambda: (add(0), third()), lambda: add(1), lambda: add(2)]
+            kv_stage = 1
+            for s in range(2 + n_back, len(order) + 3):
+                if s == at_qkv:
+                    while kv_stage < 5:
+                        kvx.stage(kv_stage)
+                        kv_stage += 1
+                    dx.arrived()
+                    rope_back()
+                    gq_share.start()
+                    gq_share.ready()
+                stage_step(order, SUM_STAGES, s)
+                if kv_stage < 4:
                     kvx.stage(kv_stage)
                     kv_stage += 1
-                dx.arrived()
-                rope_back()
-                gq_share.start()
-                gq_share.ready()
-            stage_step(order, 4, s)
+                if s >= at_qkv and jobs:
+                    jobs.pop(0)()
+            for job in jobs:
+                job()
+            for c in ends:
+                c.wait()
+            t = total[...]
+            for j in range(1, zn):
+                t = t + got[2 + j]
+            total[...] = t
+
+        pl.run_scoped(
+            gains_and_input,
+            pltpu.VMEM(w_ref.shape, b16),
+            pltpu.VMEM(r_ref.shape, b16),
+            pltpu.VMEM(order_ref.shape, b16),
+            pltpu.VMEM(x_ref.shape, b16),
+            pltpu.VMEM(gx1_ref.shape, f32),
+            pltpu.VMEM(gx1_ref.shape, f32),
+            pltpu.VMEM(x_ref.shape, b16),
+        )
         dx.sent()
         gx.sent()
         gq_share.sent()
         for i in share:
             i.sent()
 
-    stat = (HALF_GROUPS, 4, 1, PER * WIDE)
     block = (zn, mine, tokens)
-    tile = (HALF_GROUPS, 4, WIDE, PER * WIDE)
     any_ = pl.BlockSpec(memory_space=pl.ANY)
     vmem = pl.BlockSpec(memory_space=pltpu.VMEM)
     dma = pltpu.SemaphoreType.DMA
     return pl.pallas_call(
         kernel,
-        out_shape=[jax.ShapeDtypeStruct((all_rows, qkv_w), b16)]
-        + [jax.ShapeDtypeStruct(s, f32) for s in outs_shape],
-        in_specs=[any_, vmem, vmem, any_, vmem, vmem] + [any_] * n_in,
-        out_specs=[vmem] * (1 + n_out),
+        out_shape=[jax.ShapeDtypeStruct(s, f32) for s in outs_shape]
+        + [jax.ShapeDtypeStruct((all_rows, width), b16), jax.ShapeDtypeStruct((8, width), f32)],
+        in_specs=[any_, any_, any_, any_, vmem, vmem]
+        + [any_] * n_in
+        + [any_, any_, any_, vmem, vmem, any_, vmem, any_],
+        out_specs=[vmem] * (n_out + 2),
         scratch_shapes=scratch
         + shares
         + [
             pltpu.VMEM((ring, zn, 2, 2, ra, max_cols), b16),
             pltpu.VMEM((all_rows, qkv_w), b16),
+            pltpu.VMEM((all_rows, qkv_w), b16),
             pltpu.VMEM((zn, tokens, KV_LANES), b16),
             pltpu.VMEM(block, b16),
             pltpu.VMEM(block, b16),
-            pltpu.VMEM(tile, b16),
-            pltpu.VMEM(tile, b16),
-            pltpu.VMEM((2 * cn, HALF_GROUPS, HEAD_SIZE, wn * rows), b16),
-            pltpu.VMEM(stat, f32),
-            pltpu.VMEM((HALF_GROUPS, 4, HEAD_SIZE, PER * WIDE), f32),
-            pltpu.VMEM((zn, 2, 2, 2, tokens, KV_LANES), f32),
             pltpu.VMEM((zn, 2, 2, tokens, KV_LANES), b16),
+            pltpu.VMEM((2 + zn, 8, width), f32),
         ]
         + Scatter.scratch(zn, tokens, KV_LANES)[:4]
         + [
@@ -1610,74 +1710,14 @@
             dma((2, zn)),
             dma((Scatter.SEMS,)),
             dma((Scatter.SEMS,)),
+            dma((2 + zn,)),
+            dma((2 + zn,)),
+            dma((5,)),
         ],
         compiler_params=pltpu.CompilerParams(
             collective_id=collective_id, has_side_effects=True, vmem_limit_bytes=VMEM_LIMIT
         ),
-    )(do, qh, kvg, oh, lse, tables, *ins_all)
-
-
-def finish(gq, weights, rest, x, inv, gain, gx1, gain_sums, order, collective_id):
-    zn = lax.axis_size("ctx") // 2
-    f32, b16 = jnp.float32, jnp.bfloat16
-    wa = weights.shape[0]
-    width = x.shape[1]
-
-    def kernel(gq_ref, w_ref, r_ref, x_ref, inv_ref, gain_ref, gx1_ref, sums_ref, order_ref, out, total, ghn, low, got, send, recv):
-        greet(zn)
-        z, y, x_, k = place()
-        ghn[:, :wa] = lax.dot_general(gq_ref[...], w_ref[...], NT, preferred_element_type=f32)
-        ghn[:, wa:] = lax.dot_general(gq_ref[...], r_ref[...], NT, preferred_element_type=f32)
-        xf = x_ref[...].astype(f32)
-        inv_ = inv_ref[...]
-        grad = ghn[...]
-        total[...] = jnp.zeros(total.shape, f32)
-        total[0:1, :] = jnp.sum(grad * xf * inv_, axis=0, keepdims=True)
-        total[1:2, :] = sums_ref[...]
-        moves = [
-            remote(total, got.at[0], send.at[0], recv.at[0], device(z, y, x_, 1 - k)),
-            remote(total, got.at[1], send.at[1], recv.at[1], device(z, y, 1 - x_, k)),
-            remote(total, got.at[2], send.at[2], recv.at[2], device(z, 1 - y, x_, k)),
-        ]
-        moves[0].start()
-        weighted = grad * gain_ref[...]
-        inner = jnp.mean(weighted * xf, axis=-1, keepdims=True)
-        row = inv_ * weighted - xf * (inv_ * inv_ * inv_) * inner
-        low[...] = (gx1_ref[...] + row).astype(b16)
-        for i in range(3):
-            moves[i].wait()
-            total[...] = total[...] + got[i]
-            if i < 2:
-                moves[i + 1].start()
-        ends = []
-        for j in range(1, zn):
-            ends.append(remote(total, got.at[2 + j], send.at[2 + j], recv.at[2 + j], device(lax.rem(z + j, zn), y, x_, k)))
-            ends[-1].start()
-        out[...] = lax.dot_general(low[...], order_ref[...], NT, preferred_element_type=f32).astype(b16)
-        for c in ends:
-            c.wait()
-        t = total[...]
-        for j in range(1, zn):
-            t = t + got[2 + j]
-        total[...] = t
-
-    vmem = pl.BlockSpec(memory_space=pltpu.VMEM)
-    return pl.pallas_call(
-        kernel,
-        out_shape=[jax.ShapeDtypeStruct(x.shape, b16), jax.ShapeDtypeStruct((8, width), f32)],
-        in_specs=[vmem] * 9,
-        out_specs=[vmem] * 2,
-        scratch_shapes=[
-            pltpu.VMEM(x.shape, f32),
-            pltpu.VMEM(x.shape, b16),
-            pltpu.VMEM((2 + zn, 8, width), f32),
-            pltpu.SemaphoreType.DMA((2 + zn,)),
-            pltpu.SemaphoreType.DMA((2 + zn,)),
-        ],
-        compiler_params=pltpu.CompilerParams(
-            collective_id=collective_id, has_side_effects=True, vmem_limit_bytes=VMEM_LIMIT
-        ),
-    )(gq, weights, rest, x, inv, gain, gx1, gain_sums, order)
+    )(do, qh, kvg, oh, lse, tables, *ins_all, *last)
 
 
 def ffn(o_t, x, gy, gain, order_t, out_a, gate_a, up_a, down, rest):
@@ -1912,12 +1952,13 @@
     )
     qkv_a, out_a, gate_a, up_a, down_w = map(flat, (qkv_a, out_a, gate_a, up_a, down_a))
     gain1, gain2 = gains[:1], gains[1:]
+    order_t = order.T
     out, gx1, gb_plain, g_gate, g_up, act_t, h2_t, h2_bt, o_pt, o_pbt, go_t, gain2_sum = ffn(
-        o_t, x_low, gy_low, gain2, order.T, out_a, gate_a, up_a, down_w, flat(b2g)
+        o_t, x_low, gy_low, gain2, order_t, out_a, gate_a, up_a, down_w, flat(b2g)
     )
     gy_plain = cotangent.reshape(rows, width)
     left = lambda t: t.reshape(zn, 2, 2, 2, -1, rows)
-    gq, r_down, r_gate, r_up, r_out, r_b2, r_qkv, r_b1 = scatter_attend(
+    r_down, r_gate, r_up, r_out, r_b2, r_qkv, r_b1, input_grad, gain_sums = scatter_attend(
         go_t,
         qh,
         kvg,
@@ -1928,10 +1969,8 @@
         [h2_bt, o_pbt, hn_bt],
         [gy_plain, gb_plain, g_gate, g_up],
         ((rest_w + pad2) // fold, (qkv_w + pad1) // fold),
+        [qkv_a, qkv_b, x_low, inv1, gain1, gx1, gain2_sum, order_t],
         3,
-    )
-    input_grad, gain_sums = finish(
-        gq, qkv_a, qkv_b, x_low, inv1, gain1, gx1, gain2_sum, order, 4
     )
     device_at = c * wn + w
 

time: 407 us -> 388 us (0.953)
  Pallas kernels: 376 us -> 354 us
    pallas_call x2 -> x1, Pallas kernels: 189 us -> 170 us  [scatter_attend(): pl.pallas_call(kernel, out_shape=[jax.ShapeDtypeStruct(s, f32) for s in o...]
where the time goes in v5:
time: 388 us; the launch traced here: 383 us
  Pallas kernels  354 us (91%)
  other arithmetic  12.5 us (3%)
  local copies, waits for them, and re-layouts  11.6 us (3%)
    pallas_call x1, Pallas kernels, scatter_attend(): pl.pallas_call(kernel, out_shape=[jax.ShapeDtypeStruct(s, f32) for s in o...  170 us
    pallas_call x1, Pallas kernels, gather_attend(): pl.pallas_call(kernel, out_shape=[sds((mbs, q_rows, tokens), b16), sds(bl...  155 us
    pallas_call x1, Pallas kernels, ffn(): pl.pallas_call(kernel, out_shape=[sds((rows, width), b16), sds((rows, wid...  29.8 us

profile of v5, /device:TPU:0, one launch (start us, length us, event | category | flops | bytes accessed | tf_op | source)
XLA Modules:
  0.0 383.0 jit_solution(17245171034951546614)
XLA Ops:
  0.7 0.7 fusion.47
  1.4 0.9 fusion.61
  2.3 1.0 concatenate.49.refs_2_
  3.3 0.0 copy-start.1
  3.3 0.6 reshape.173.refs_3_
  3.9 0.3 multiply_cosine_fusion
  4.3 0.2 maximum_bitcast_fusion.1
  4.5 0.7 pad_maximum_fusion.2.refs_1_.refs_5_
  5.2 0.0 slice-start
  5.2 0.0 slice-start.1
  5.2 3.8 fusion.2
  9.0 0.0 copy-done.1
  9.0 0.0 slice-done
  9.0 0.0 slice-done.1
  9.1 0.6 reshape.175.refs_8_
  9.7 0.6 slice.103.refs_4_
  10.4 0.7 slice.104.refs_7_
  11.1 1.1 fusion.58
  12.2 2.0 fusion.1.order_hbm.refs_24_
  14.3 154.8 %shard_map.194 = (bf16[2,1152,128]{2,1,0:T(8,128)(2,1)}, bf16[4,576,128]{2,1,0:T(8,128)(2,1)}, bf16[4,2,2,2,128,384]{5,4,3,2,1,0:T(8,128)(2,1)}, bf16[4,576,128]...) custom-call(bf16[256,1152]{1,0:T(8,128)(2,1)} %get-tuple-element.86., ...), custom_call_target="tpu_custom_call" | custom-call | tf_op jit(solution)/shard_map/pallas_call | solution.py:1137
  169.0 1.4 fusion.63
  170.4 29.8 %shard_map.195 = (bf16[256,1152]{1,0:T(8,128)(2,1)}, f32[256,1152]{1,0:T(8,128)}, bf16[256,1152]{1,0:T(8,128)(2,1)}, bf16[256,3072]{1,0:T(8,128)(2,1)}, bf16[256...) custom-call(bf16[2,1152,128]{2,1,0:T(8,128)(2,1)} %get-tuple-element, ...), custom_call_target="tpu_custom_call" | custom-call | tf_op jit(solution)/shard_map/pallas_call | solution.py:1820
  200.2 169.6 %shard_map.196 = (f32[96,1152]{1,0:T(8,128)}, f32[32,3072]{1,0:T(8,128)}, f32[32,3072]{1,0:T(8,128)}, f32[32,1152]{1,0:T(8,128)}, f32[16,1920]{1,0:T(8,128)}, /*...) custom-call(bf16[2,1152,128]{2,1,0:T(8,128)(2,1)} %get-tuple-element.56.refs_0_, ...), custom_call_target="tpu_custom_call" | custom-call | tf_op jit(solution)/shard_map/pallas_call | solution.py:1682
  369.7 0.0 copy-start
  369.8 0.0 copy-start.2
  369.8 0.9 fusion.60
  370.6 0.1 fusion.53
  370.7 0.1 fusion.52
  370.8 0.6 pad_maximum_fusion.7
  371.4 0.1 fusion.50
  371.4 0.1 fusion.51
  371.5 0.6 pad_maximum_fusion.6
  372.1 0.8 reshape.188
  372.9 0.0 copy-start.3
  372.9 1.0 reshape.190
  373.9 1.6 pad_maximum_fusion.3
  375.5 1.8 pad_maximum_fusion.1
  377.3 1.8 pad_maximum_fusion
  379.1 0.0 copy-done
  379.1 0.1 fusion.18
  379.2 0.6 fusion.17
  379.8 0.7 fusion.11
  380.5 0.7 pad_maximum_fusion.4
  381.2 0.0 copy-done.2
  381.2 0.8 copy.26
  382.1 0.0 copy-done.3
  382.1 0.8 copy.27
  (11 shorter events, 0.1 us)
Async XLA Ops:
  3.3 5.7 %copy-start.1 = (bf16[36,1920]{1,0:T(8,128)(2,1)}, bf16[36,1920]{1,0:T(8,128)(2,1)S(1)}, u32[]{:S(2)}) copy-start(bf16[36,1920]{1,0:T(8,128)(2,1)S(1)} %concatenate.49.refs_2_) | copy-start | bytes 414724
  5.2 3.8 %slice-start = ((bf16[36,3072]{1,0:T(8,128)(2,1)}), bf16[4,3072]{1,0:T(4,128)(2,1)S(1)}, s32[]{:S(2)}) async-start(bf16[36,3072]{1,0:T(8,128)(2,1)} %refs_5_.1), calls=%async_computation | async-start | bytes 49152 | tf_op jit(solution)/shard_map/slice | solution.py:1937
  5.2 3.8 %slice-start.1 = ((bf16[36,3072]{1,0:T(8,128)(2,1)}), bf16[4,3072]{1,0:T(4,128)(2,1)S(1)}, s32[]{:S(2)}) async-start(bf16[36,3072]{1,0:T(8,128)(2,1)} %refs_6_.1), calls=%async_computation.1 | async-start | bytes 49152 | tf_op jit(solution)/shard_map/slice | solution.py:1937
  369.7 9.4 %copy-start = (f32[32,1920]{1,0:T(8,128)S(1)}, f32[32,1920]{1,0:T(8,128)}, u32[]{:S(2)}) copy-start(f32[32,1920]{1,0:T(8,128)} %get-tuple-element.78) | copy-start | bytes 737284
  369.8 11.5 %copy-start.2 = (bf16[256,1152]{1,0:T(8,128)(2,1)S(1)}, bf16[256,1152]{1,0:T(8,128)(2,1)}, u32[]{:S(2)}) copy-start(bf16[256,1152]{1,0:T(8,128)(2,1)} %get-tuple-element.76) | copy-start | bytes 1769476
  372.9 9.2 %copy-start.3 = (f32[96,1152]{1,0:T(8,128)S(1)}, f32[96,1152]{1,0:T(8,128)}, u32[]{:S(2)}) copy-start(f32[96,1152]{1,0:T(8,128)} %get-tuple-element.129) | copy-start | bytes 1327108

commit v6 on v5

--- a/solution.py
+++ b/solution.py
@@ -652,15 +652,19 @@
                 c.wait_send()
 
 
-def stage_step(items, stages, t, between=None):
-    for n in stages:
-        if 0 <= t - n < len(items):
-            items[t - n].stage(n)
+def stage_step(items, offsets, t, between=None):
+    for n, offset in enumerate(offsets):
+        if 0 <= t - offset < len(items):
+            if items[t - offset] is not None:
+                items[t - offset].stage(n)
             if between is not None:
                 between()
 
 
+FIRST_STAGES = (0, 1, 2, 3, 4)
 GATHER_STAGES = (0, 1, 2, 3, 4)
+GATHER_FROM = 3
+GATHER_CUTS = [(1, 1), (1, 2), (1, 2), (2, 1), (1, 1)]
 SUM_STAGES = (0, 1, 2, 3)
 
 
@@ -892,7 +896,7 @@
 
 
 STEPS = 38
-FORWARD_PARTS = 20
+FORWARD_PARTS, FORWARD_LEFT = 20, 3
 
 
 def visible(p, j, y, w, cn, wn, rows):
@@ -944,7 +948,7 @@
         dst[:, q * cols : (q + 1) * cols] = t.astype(dst.dtype)
 
 
-def gather_attend(x, tables, qkv, fold1, arrays, used, cuts, collective_id):
+def gather_attend(x, gy, tables, qkv, fold1, weights, cuts, collective_id):
     cn, wn = lax.axis_size("ctx"), lax.axis_size("ws")
     zn = cn // 2
     dn = cn * wn
@@ -960,20 +964,28 @@
     rb = qkv.shape[0] - ra
     wa = dn * ra
     wide1 = fold1.shape[1] * (16 // rb)
-    n = len(arrays)
-    work = [(a, piece) for a in range(n) for piece in pieces_of(used[a], arrays[a].shape[1], *cuts[a])]
+    own = ra + rb
+    ff = weights[1].shape[1]
+    step_cols = 3 * WIDE
+    rest_w = -(-(width + 2 * ff) // (4 * step_cols)) * step_cols
+    shapes = [(ra, width), (ra, ff), (ra, ff), weights[3].shape, (16, rest_w)]
+    n = len(shapes)
+    work = [(a, piece) for a in range(n) for piece in pieces_of(*shapes[a], *cuts[a])]
     groups = range(HALF_GROUPS)
     n_first = 3
 
     def kernel(*refs):
-        x_ref, tab, qkv_ref, fold_ref = refs[:4]
-        ins = refs[4 : 4 + n]
-        at = 4 + n
+        x_raw, gy_raw, tab, qkv_ref, fold_ref, out_raw, gate_raw, up_raw, down_raw = refs[:9]
+        at = 9
+        x_ref, gy_out, order_out = refs[at : at + 3]
+        at += 3
         o_out, q_out, kv_out, oh_out, lse_out, w_out, wb_out, hn_out, hnb_out, inv_out, gains_out = refs[at : at + 11]
         at += 11
         outs = refs[at : at + n]
         at += n
-        (wq, f1, wide, hn, q_s, kv_s, qh, kvg, oh, qpad, vt, m_s, l_s, acc, send, recv, xs, xr, ks, kr, save) = refs[at:]
+        (order, out_s, down_s, rest_s, wq, f1, wide, hn, q_s, kv_s, qh, kvg, oh, qpad, vt, m_s, l_s, acc) = refs[at : at + 18]
+        send, recv, xs, xr, ks, kr, save = refs[at + 18 :]
+        ins = [out_s, gate_raw, up_raw, down_s, rest_s]
         greet(zn)
         z, y, x_, k = place()
         w = 2 * x_ + k
@@ -989,22 +1001,56 @@
             gather_item(qkv_ref, wq, 0, ra, 0, 2 * KV_LANES, send.at[1], recv.at[1], zn),
             gather_item(qkv_ref, wq, 0, ra, 2 * KV_LANES, q_rows, send.at[2], recv.at[2], zn),
         ]
-        items += [
+        later = [
             gather_item(ins[a], outs[a], r0, nr, c0, nc, send.at[n_first + i], recv.at[n_first + i], zn)
             for i, (a, (r0, nr, c0, nc)) in enumerate(work)
         ]
         kvx = Gather(lanes_of, kvg, ks, kr, zn)
         qx = Exchange(lambda zz: heads_of(q_s, zz), lambda zz: qh.at[zz], xs.at[0], xr.at[0], zn)
         ox = Exchange(lambda zz: oh.at[zz], lambda zz: heads_of(o_out, zz), xs.at[1], xr.at[1], zn)
-        for s in range(n_first + 1):
-            stage_step(items, GATHER_STAGES, s)
+
+        def advance(s, between=None):
+            stage_step(items, FIRST_STAGES, s)
+            stage_step(later, GATHER_STAGES, s - GATHER_FROM, between)
+
+        advance(0)
+        for r in range(0, width, WIDE):
+            new = r + lax.broadcasted_iota(jnp.int32, (WIDE, width), 0)
+            old = jnp.where(
+                new < wa, own * (new // ra) + lax.rem(new, ra), own * ((new - wa) // rb) + ra + lax.rem(new - wa, rb)
+            )
+            col = lax.broadcasted_iota(jnp.int32, (WIDE, width), 1)
+            order[r : r + WIDE, :] = jnp.where(col == old, 1.0, 0.0).astype(b16)
+        advance(1)
+        out_s[...] = nt(out_raw[...], order[...]).astype(b16)
+        down_s[...] = nt(down_raw[...], order[...]).astype(b16)
+        columns = []
+        for ref, cols in ((out_s, width), (gate_raw, ff), (up_raw, ff)):
+            columns += [(ref, c) for c in range(0, cols, step_cols)]
+        per = rest_w // step_cols
+        row = lax.broadcasted_iota(jnp.int32, (16, own), 0)
+        src = lax.broadcasted_iota(jnp.int32, (16, own), 1)
+        for c in range(per):
+            total = jnp.zeros((16, step_cols), f32)
+            for q in range(16 // rb):
+                if q * per + c < len(columns):
+                    ref, lo = columns[q * per + c]
+                    pick = jnp.where((row // rb == q) & (src == ra + lax.rem(row, rb)), 1.0, 0.0).astype(b16)
+                    total = total + jnp.dot(pick, ref[:, lo : lo + step_cols], preferred_element_type=f32)
+            rest_s[:, c * step_cols : (c + 1) * step_cols] = total.astype(b16)
+        advance(2)
+        x_ref[...] = nt(x_raw[...], order[...]).astype(b16)
+        advance(3)
+        gy_out[...] = nt(gy_raw[...], order[...]).astype(b16)
+        save_order = pltpu.make_async_copy(order, order_out, save.at[5])
+        save_order.start()
         xf = x_ref[...].astype(f32)
         inv = lax.rsqrt(jnp.mean(xf * xf, axis=-1, keepdims=True) + EPSILON)
         inv_out[...] = inv
         m_s[...] = jnp.full(m_s.shape, NEG, f32)
         l_s[...] = jnp.zeros(l_s.shape, f32)
         acc[...] = jnp.zeros(acc.shape, f32)
-        stage_step(items, GATHER_STAGES, n_first + 1)
+        advance(n_first + 1)
         unfold_rows(f1[...].reshape(dn * 16, fold1.shape[1]), wide, rb)
         lane = lax.broadcasted_iota(jnp.int32, (WIDE, width), 1)
         local = jnp.where(lane < wa, lax.rem(lane, ra), ra + lax.rem(lane - wa, rb))
@@ -1019,7 +1065,7 @@
         hn[...] = normed.astype(b16)
         hn_out[...] = transposed(normed[:, :wa]).astype(b16)
         hnb_out[...] = transposed(normed[:, wa:]).astype(b16)
-        stage_step(items, GATHER_STAGES, n_first + 2)
+        advance(n_first + 2)
 
         low_lanes = lax.broadcasted_iota(jnp.int32, (tokens, WIDE), 1) < HEAD_SIZE
         quarter = HEAD_SIZE // 2
@@ -1049,10 +1095,11 @@
         project(0)
         project(1)
         kvx.stage(0)
-        stage_step(items, GATHER_STAGES, n_first + 3)
+        advance(n_first + 3)
         for c in range(2, qkv_w // KV_LANES):
             project(c)
         qx.start()
+        save_order.wait()
         saves = [
             pltpu.make_async_copy(wq, w_out, save.at[3]),
             pltpu.make_async_copy(wide.at[:, pl.ds(0, qkv_w)], wb_out, save.at[4]),
@@ -1061,7 +1108,7 @@
             s.start()
         kvx.stage(1)
         kvx.stage(2)
-        stage_step(items, GATHER_STAGES, n_first + 4)
+        advance(n_first + 4)
         kvx.stage(3)
         qx.arrived()
         for half in range(2):
@@ -1109,12 +1156,12 @@
             pl.when(jnp.logical_not(edge))(lambda: run(False))
             return 0
 
-        last = len(items) + 4
+        last = GATHER_FROM + len(later) + GATHER_STAGES[-1]
         start = n_first + 5
         attend = portions(step, STEPS, FORWARD_PARTS)
         for s in range(start, last):
-            stage_step(items, GATHER_STAGES, s, attend if s < last - 2 else None)
-            if s == last - 3:
+            advance(s, attend if s <= last - FORWARD_LEFT else None)
+            if s == last - FORWARD_LEFT:
                 attend(True)
                 unpair(lambda g, p: acc[g, p] / l_s[g, p], oh)
                 ox.start()
@@ -1137,6 +1184,9 @@
     return pl.pallas_call(
         kernel,
         out_shape=[
+            sds(x.shape, b16),
+            sds(x.shape, b16),
+            sds((width, width), b16),
             sds((mbs, q_rows, tokens), b16),
             sds(block, b16),
             sds(kv_shape, b16),
@@ -1149,10 +1199,14 @@
             sds((all_rows, 1), f32),
             sds((2, width), f32),
         ]
-        + [sds((zn, 2, 2, 2, used[a], arrays[a].shape[1]), arrays[a].dtype) for a in range(n)],
-        in_specs=[vmem] * 2 + [any_] * (2 + n),
-        out_specs=[any_] * 4 + [vmem] + [any_] * 2 + [vmem] * 4 + [any_] * n,
+        + [sds((zn, 2, 2, 2, *shapes[a]), b16) for a in range(n)],
+        in_specs=[vmem] * 3 + [any_] * 2 + [vmem] * 4,
+        out_specs=[vmem] * 2 + [any_] + [any_] * 4 + [vmem] + [any_] * 2 + [vmem] * 4 + [any_] * n,
         scratch_shapes=[
+            pltpu.VMEM((width, width), b16),
+            pltpu.VMEM(weights[0].shape, b16),
+            pltpu.VMEM(weights[3].shape, b16),
+            pltpu.VMEM((16, rest_w), b16),
             pltpu.VMEM((zn, 2, 2, 2, ra, qkv_w), b16),
             pltpu.VMEM((zn, 2, 2, 2, 16, fold1.shape[1]), b16),
             pltpu.VMEM((dn * rb, wide1), b16),
@@ -1173,12 +1227,12 @@
             dma((2, zn)),
             dma((Gather.SEMS,)),
             dma((Gather.SEMS,)),
-            dma((5,)),
+            dma((6,)),
         ],
         compiler_params=pltpu.CompilerParams(
             collective_id=collective_id, has_side_effects=True, vmem_limit_bytes=VMEM_LIMIT
         ),
-    )(x, tables, qkv, fold1, *arrays)
+    )(x, gy, tables, qkv, fold1, *weights)
 
 
 class Share:
@@ -1277,7 +1331,8 @@
                 c.wait_send()
 
 
-ORDER = (0, 1, 2, 3, 4, 5, 6, 7, 8, 9, 10, 11, 12)
+FFN_CUTS = 2
+ORDER = (0, 1, 2, 3, 4, 5, 6, 7, 8, 9, 10, 11)
 BACK_SPAN, BACK_PARTS = 3, 10
 
 
@@ -1298,15 +1353,13 @@
     ra = lefts[1].shape[4]
     rest_w, qkv_rest_w = plan
     n_down = act_rows // ra
-    half_ff = ff // 2
     sizes = (
         [(ra, width)] * n_down
-        + [(ra, half_ff)] * 3
-        + [(ra, half_ff // 2)] * 2
+        + [(ra, ff // FFN_CUTS)] * (2 * FFN_CUTS)
         + [(ra, width), (16, rest_w), (ra, 2 * KV_LANES), (ra, q_rows), (16, qkv_rest_w)]
     )
     max_cols = max(s[1] for s in sizes)
-    ring = 4
+    ring = SUM_STAGES[-1] + 1
     scratch = []
     for nr, nc in sizes:
         scratch += Sum.scratch(zn, nr, nc)
@@ -1438,8 +1491,7 @@
 
         gq_both = (gq, gq_other)
         makes = [product(ACT, both(GY), 0, ra * i, (ACT, GY)) for i in range(n_down)]
-        ffn_parts = [(GG, 0, half_ff), (GG, half_ff, half_ff), (GU, 0, half_ff)]
-        ffn_parts += [(GU, half_ff, half_ff // 2), (GU, half_ff + half_ff // 2, half_ff // 2)]
+        ffn_parts = [(g, i * (ff // FFN_CUTS), ff // FFN_CUTS) for g in (GG, GU) for i in range(FFN_CUTS)]
         makes += [product(H2, both(g), lo, 0, (H2, g)) for g, lo, _ in ffn_parts]
         makes += [product(OT, both(GB), 0, 0, (OT, GB)), rest_product]
         makes += [product(HN, gq_both, 0, 0, (HN,)), product(HN, gq_both, 2 * KV_LANES, 0, (HN,)), qkv_rest_product]
@@ -1457,7 +1509,7 @@
         gx.start()
         for i in (ACT, GY, H2, GG, GU, OT, GB, H2B, OTB, HN, HNB):
             share[i].start()
-        order = [items[i] for i in ORDER]
+        order = [None if i is None else items[i] for i in ORDER]
         at_qkv = ORDER.index(n_items - 3)
         n_back = BACK_SPAN
         stage_step(order, SUM_STAGES, 0)
@@ -1620,7 +1672,7 @@
                 total[0:1, :] = jnp.sum(grad * xf * inv, axis=0, keepdims=True)
                 total[1:2, :] = gain2_ref[...]
                 steps[0].start()
-                weighted = grad * gain_ref[...]
+                weighted = grad * gain_ref[0:1, :]
                 inner = jnp.mean(weighted * xf, axis=-1, keepdims=True)
                 low[...] = (gx_s[...] + inv * weighted - xf * (inv * inv * inv) * inner).astype(b16)
 
@@ -1635,7 +1687,7 @@
 
             jobs = [first, second, lambda: (add(0), third()), lambda: add(1), lambda: add(2)]
             kv_stage = 1
-            for s in range(2 + n_back, len(order) + 3):
+            for s in range(2 + n_back, len(order) + SUM_STAGES[-1]):
                 if s == at_qkv:
                     while kv_stage < 5:
                         kvx.stage(kv_stage)
@@ -1758,7 +1810,7 @@
         )
         u = x1[...]
         inv = lax.rsqrt(jnp.mean(u * u, axis=-1, keepdims=True) + EPSILON)
-        hidden = u * inv * gain_ref[...]
+        hidden = u * inv * gain_ref[1:2, :]
         h2[...] = hidden.astype(b16)
         h2_ref[...] = transposed(hidden[:, :wa]).astype(b16)
         h2b_ref[...] = transposed(hidden[:, wa:]).astype(b16)
@@ -1799,7 +1851,7 @@
         inv = lax.rsqrt(jnp.mean(u * u, axis=-1, keepdims=True) + EPSILON)
         grad = gh[...]
         gain_sum[...] = jnp.sum(grad * u * inv, axis=0, keepdims=True)
-        weighted = grad * gain_ref[...]
+        weighted = grad * gain_ref[1:2, :]
         inner = jnp.mean(weighted * u, axis=-1, keepdims=True)
         gx1 = inv * weighted - u * (inv * inv * inv) * inner + gy_ref[...].astype(f32)
         gx1_ref[...] = gx1
@@ -1890,18 +1942,6 @@
     rows = mbs * tokens
     wa = dn * ra
 
-    new = jnp.arange(width)
-    old = jnp.where(
-        new < wa, own * (new // ra) + new % ra, own * ((new - wa) // rb) + ra + (new - wa) % rb
-    )
-    order = (jnp.arange(width)[:, None] == old[None, :]).astype(b16)
-
-    def to_order(t):
-        return jnp.dot(t, order, preferred_element_type=f32).astype(t.dtype)
-
-    def from_order(t):
-        return lax.dot_general(t, order, NT, preferred_element_type=f32).astype(t.dtype)
-
     fold = 16 // rb
 
     def folded(t):
@@ -1911,13 +1951,6 @@
     pad1 = -qkv_w % (fold * WIDE)
     rest_w = width + 2 * ff
     pad2 = -rest_w % (fold * WIDE)
-    moved = to_order(
-        jnp.concatenate(
-            [inputs.reshape(rows, width), cotangent.reshape(rows, width), out_weight, down_weight]
-        )
-    )
-    x_low, gy_low = moved[:rows], moved[rows : 2 * rows]
-    out_p, down_p = moved[2 * rows : 2 * rows + own], moved[2 * rows + own :]
     half_hid = hid // 2
     qkv = jnp.concatenate(
         [
@@ -1932,29 +1965,22 @@
     gains = jnp.stack([attn_gain, ffn_gain])
     gains = jnp.pad(gains, ((0, rb - 2), (0, pad1 - own)))
     b1 = folded(jnp.concatenate([qkv[ra:], gains], axis=1))
-    b2 = folded(
-        jnp.pad(
-            jnp.concatenate([out_p[ra:], gate_weight[ra:], up_weight[ra:]], axis=1), ((0, 0), (0, pad2))
-        )
-    )
     flat = lambda t: t.reshape(-1, t.shape[-1])
     c, w = lax.axis_index("ctx"), lax.axis_index("ws")
     tables = lane_tables(query_places(c, w, tokens, cn, wn))
-    (o_t, qh, kvg, oh, lse, qkv_a, qkv_b, hn_t, hn_bt, inv1, gains, out_a, gate_a, up_a, down_a, b2g) = gather_attend(
-        x_low,
+    (x_low, gy_low, order_t, o_t, qh, kvg, oh, lse, qkv_a, qkv_b, hn_t, hn_bt, inv1, gains, out_a, gate_a, up_a, down_a, b2g) = gather_attend(
+        inputs.reshape(rows, width),
+        cotangent.reshape(rows, width),
         tables,
         qkv,
         b1,
-        [out_p, gate_weight, up_weight, down_p, b2],
-        [ra, ra, ra, down_p.shape[0], 16],
-        [(1, 1), (1, 2), (1, 2), (2, 1), (1, 1)],
+        [out_weight, gate_weight, up_weight, down_weight],
+        GATHER_CUTS,
         2,
     )
     qkv_a, out_a, gate_a, up_a, down_w = map(flat, (qkv_a, out_a, gate_a, up_a, down_a))
-    gain1, gain2 = gains[:1], gains[1:]
-    order_t = order.T
     out, gx1, gb_plain, g_gate, g_up, act_t, h2_t, h2_bt, o_pt, o_pbt, go_t, gain2_sum = ffn(
-        o_t, x_low, gy_low, gain2, order_t, out_a, gate_a, up_a, down_w, flat(b2g)
+        o_t, x_low, gy_low, gains, order_t, out_a, gate_a, up_a, down_w, flat(b2g)
     )
     gy_plain = cotangent.reshape(rows, width)
     left = lambda t: t.reshape(zn, 2, 2, 2, -1, rows)
@@ -1969,7 +1995,7 @@
         [h2_bt, o_pbt, hn_bt],
         [gy_plain, gb_plain, g_gate, g_up],
         ((rest_w + pad2) // fold, (qkv_w + pad1) // fold),
-        [qkv_a, qkv_b, x_low, inv1, gain1, gx1, gain2_sum, order_t],
+        [qkv_a, qkv_b, x_low, inv1, gains, gx1, gain2_sum, order_t],
         3,
     )
     device_at = c * wn + w

time: 388 us -> 382 us (0.985)
  Pallas kernels: 354 us -> 359 us
  local copies, waits for them, and re-layouts: 11.6 us -> 7.07 us
    slice x9 -> x0, local copies, waits for them, and re-layouts: 3.91 us -> none  [the longest x2 1.38 us: fast_device(): out_p, down_p = (moved[2 * rows:2 * rows + own], moved[2 * rows + own:])]
where the time goes in v6:
time: 382 us; the launch traced here: 378 us
  Pallas kernels  359 us (94%)
  other arithmetic  10.4 us (3%)
  local copies, waits for them, and re-layouts  7.07 us (2%)
    pallas_call x1, Pallas kernels, scatter_attend(): pl.pallas_call(kernel, out_shape=[jax.ShapeDtypeStruct(s, f32) for s in o...  172 us
    pallas_call x1, Pallas kernels, gather_attend(): pl.pallas_call(kernel, out_shape=[sds(x.shape, b16), sds(x.shape, b16), s...  157 us
    pallas_call x1, Pallas kernels, ffn(): pl.pallas_call(kernel, out_shape=[sds((rows, width), b16), sds((rows, wid...  29.8 us

profile of v6, /device:TPU:0, one launch (start us, length us, event | category | flops | bytes accessed | tf_op | source)
XLA Modules:
  0.0 377.9 jit_solution(16625299721546380294)
XLA Ops:
  0.7 0.7 fusion.10
  1.4 0.9 fusion.22
  2.3 1.0 concatenate.42.refs_3_
  3.3 0.0 copy-start.1
  3.3 0.6 reshape.111.refs_4_
  3.9 0.3 multiply_cosine_fusion
  4.3 0.2 maximum_bitcast_fusion.1
  4.5 0.7 pad_maximum_fusion.2.refs_2_.refs_5_
  5.2 0.0 copy-done.1
  5.2 157.3 %shard_map.194 = (bf16[256,1152]{1,0:T(8,128)(2,1)}, bf16[256,1152]{1,0:T(8,128)(2,1)}, bf16[1152,1152]{1,0:T(8,128)(2,1)}, bf16[2,1152,128]{2,1,0:T(8,128)(2,1)...) custom-call(bf16[256,1152]{1,0:T(8,128)(2,1)} %bitcast.49, ...), custom_call_target="tpu_custom_call" | custom-call | tf_op jit(solution)/shard_map/pallas_call | solution.py:1184
  162.5 29.8 %shard_map.195 = (bf16[256,1152]{1,0:T(8,128)(2,1)}, f32[256,1152]{1,0:T(8,128)}, bf16[256,1152]{1,0:T(8,128)(2,1)}, bf16[256,3072]{1,0:T(8,128)(2,1)}, bf16[256...) custom-call(bf16[2,1152,128]{2,1,0:T(8,128)(2,1)} %get-tuple-element, ...), custom_call_target="tpu_custom_call" | custom-call | tf_op jit(solution)/shard_map/pallas_call | solution.py:1872
  192.3 172.3 %shard_map.196 = (f32[96,1152]{1,0:T(8,128)}, f32[32,3072]{1,0:T(8,128)}, f32[32,3072]{1,0:T(8,128)}, f32[32,1152]{1,0:T(8,128)}, f32[16,1920]{1,0:T(8,128)}, /*...) custom-call(bf16[2,1152,128]{2,1,0:T(8,128)(2,1)} %get-tuple-element.62.refs_0_, ...), custom_call_target="tpu_custom_call" | custom-call | tf_op jit(solution)/shard_map/pallas_call | solution.py:1734
  364.6 0.0 copy-start
  364.7 0.0 copy-start.2
  364.7 0.9 fusion.21
  365.5 0.1 fusion.16
  365.6 0.1 fusion.15
  365.7 0.6 pad_maximum_fusion.7
  366.3 0.1 fusion.13
  366.3 0.1 fusion.14
  366.4 0.6 pad_maximum_fusion.6
  367.0 0.8 reshape.124
  367.8 0.0 copy-start.3
  367.8 1.0 reshape.126
  368.8 1.6 pad_maximum_fusion.3
  370.4 1.8 pad_maximum_fusion.1
  372.2 1.8 pad_maximum_fusion
  374.0 0.0 copy-done
  374.0 0.1 fusion.2
  374.1 0.6 fusion.1
  374.8 0.7 fusion
  375.4 0.7 pad_maximum_fusion.4
  376.1 0.0 copy-done.2
  376.1 0.8 copy.25
  377.0 0.0 copy-done.3
  377.0 0.8 copy.26
  (8 shorter events, 0.1 us)
Async XLA Ops:
  3.3 1.9 copy-start.1
  364.6 9.4 %copy-start = (f32[32,1920]{1,0:T(8,128)S(1)}, f32[32,1920]{1,0:T(8,128)}, u32[]{:S(2)}) copy-start(f32[32,1920]{1,0:T(8,128)} %get-tuple-element.84) | copy-start | bytes 737284
  364.7 11.5 %copy-start.2 = (bf16[256,1152]{1,0:T(8,128)(2,1)S(1)}, bf16[256,1152]{1,0:T(8,128)(2,1)}, u32[]{:S(2)}) copy-start(bf16[256,1152]{1,0:T(8,128)(2,1)} %get-tuple-element.82) | copy-start | bytes 1769476
  367.8 9.2 %copy-start.3 = (f32[96,1152]{1,0:T(8,128)S(1)}, f32[96,1152]{1,0:T(8,128)}, u32[]{:S(2)}) copy-start(f32[96,1152]{1,0:T(8,128)} %get-tuple-element.131) | copy-start | bytes 1327108

commit v7 on v6

--- a/solution.py
+++ b/solution.py
@@ -556,7 +556,7 @@
 MESH = pl.DeviceIdType.MESH
 NEG = -1e30
 WIDE = 128
-VMEM_LIMIT = 61 * 1024 * 1024
+VMEM_LIMIT = 62 * 1024 * 1024
 
 
 def fits_fast(mesh):
@@ -878,10 +878,40 @@
                 dst[2 * zp + 1, lo : lo + HEAD_SIZE, :] = odd.astype(dst.dtype)
 
 
+GROUP_LANES = 3 * WIDE
+
+
 def set_padded(dst, g, p, tile, side):
     tile = tile.astype(dst.dtype)
-    dst[g, p, side * HEAD_SIZE : (side + 1) * HEAD_SIZE, :] = tile
-    dst[g, p, (1 - side) * HEAD_SIZE : (2 - side) * HEAD_SIZE, :] = jnp.zeros_like(tile)
+    cols = slice(g * GROUP_LANES, (g + 1) * GROUP_LANES)
+    dst[p, side * HEAD_SIZE : (side + 1) * HEAD_SIZE, cols] = tile
+    dst[p, (1 - side) * HEAD_SIZE : (2 - side) * HEAD_SIZE, cols] = jnp.zeros_like(tile)
+
+
+def by_block(slot):
+    runs = []
+    for g in range(HALF_GROUPS):
+        if runs and runs[-1][0] == slot(g)[0]:
+            runs[-1][2] += 1
+        else:
+            runs.append([slot(g)[0], g, 1])
+    return runs
+
+
+def group_scores(block, right, p, slot):
+    out = []
+    for b, g, n in by_block(slot):
+        t = jnp.dot(block(b), right[p, :, g * GROUP_LANES : (g + n) * GROUP_LANES], preferred_element_type=jnp.float32)
+        out += [t[:, i * GROUP_LANES : (i + 1) * GROUP_LANES] for i in range(n)]
+    return out
+
+
+def group_sums(tiles, right, p, slot):
+    sums = {}
+    for b, g, n in by_block(slot):
+        left = tiles[g] if n == 1 else jnp.concatenate(tiles[g : g + n], axis=1)
+        sums[b] = nt(left, right[p, :, g * GROUP_LANES : (g + n) * GROUP_LANES])
+    return sums
 
 
 def walk(t, y, cn):
@@ -1136,10 +1166,9 @@
 
             def run(masked):
                 seen = visible(p, j, y, w, cn, wn, rows) if masked else None
+                scores = group_scores(lambda b: key_block(kvg, zz, yy, late, rows, b), qpad, p, key_slot)
                 for g in groups:
-                    s = jnp.dot(
-                        key_block(kvg, zz, yy, late, rows, key_slot(g)[0]), qpad[g, p], preferred_element_type=f32
-                    )
+                    s = scores[g]
                     if masked:
                         s = jnp.where(seen, s, NEG)
                     m_old = m_s[g, p]
@@ -1216,7 +1245,7 @@
             pltpu.VMEM(block, b16),
             pltpu.VMEM(kv_shape, b16),
             pltpu.VMEM(block, b16),
-            pltpu.VMEM((HALF_GROUPS, 4, WIDE, PER * WIDE), b16),
+            pltpu.VMEM((4, WIDE, HALF_GROUPS * PER * WIDE), b16),
             pltpu.VMEM((2 * cn, HALF_GROUPS, HEAD_SIZE, wn * rows), b16),
             pltpu.VMEM(stat, f32),
             pltpu.VMEM(stat, f32),
@@ -1371,9 +1400,9 @@
     shares = []
     for a, s in zip(ins_all, split):
         shares += [pltpu.VMEM(half(a, s), b16), pltpu.VMEM(half(a, s), b16)]
-    outs_shape = [
-        (act_rows, width), (ra, ff), (ra, ff), (ra, width), (16, rest_w), (ra, qkv_w), (16, qkv_rest_w)
-    ]
+    rb = rests[0].shape[0] // (cn * wn)
+    own_rows = ra + rb
+    outs_shape = [(act_rows, width), (own_rows, ff), (own_rows, ff), (own_rows, width), (own_rows, qkv_w)]
     n_out = len(outs_shape)
     n_last = len(last)
 
@@ -1390,7 +1419,8 @@
         pairs, rest = rest[: len(shares)], rest[len(shares) :]
         (held, gq, gq_other, dkv_in, oh, gh, give, got) = rest[:8]
         kb = rest[8:12]
-        send, recv, ps, pr, pl_, xs, xr, ks, kr, gs, gr, loads = rest[12:]
+        rest_sum, qkv_rest_sum = rest[12:14]
+        send, recv, ps, pr, pl_, xs, xr, ks, kr, gs, gr, loads = rest[14:]
         dqh, dq_in = gh, oh
         greet(zn)
         z, y, x, k = place()
@@ -1496,8 +1526,15 @@
         makes += [product(OT, both(GB), 0, 0, (OT, GB)), rest_product]
         makes += [product(HN, gq_both, 0, 0, (HN,)), product(HN, gq_both, 2 * KV_LANES, 0, (HN,)), qkv_rest_product]
         targets = [outs[0].at[pl.ds(ra * i, ra), :] for i in range(n_down)]
-        targets += [outs[1 if g == GG else 2].at[:, pl.ds(lo, n)] for g, lo, n in ffn_parts]
-        targets += [outs[3], outs[4], outs[5].at[:, pl.ds(0, 2 * KV_LANES)], outs[5].at[:, pl.ds(2 * KV_LANES, q_rows)], outs[6]]
+        block_rows = pl.ds(0, ra)
+        targets += [outs[1 if g == GG else 2].at[block_rows, pl.ds(lo, n)] for g, lo, n in ffn_parts]
+        targets += [
+            outs[3].at[block_rows, :],
+            rest_sum,
+            outs[4].at[block_rows, pl.ds(0, 2 * KV_LANES)],
+            outs[4].at[block_rows, pl.ds(2 * KV_LANES, q_rows)],
+            qkv_rest_sum,
+        ]
         items = []
         for i, (nr, nc) in enumerate(sizes):
             slot = held.at[ORDER.index(i) % ring, :, :, :, pl.ds(0, nr), pl.ds(0, nc)]
@@ -1554,22 +1591,22 @@
                 def run(masked):
                     seen = visible(p, j, y, w, cn, wn, rows) if masked else None
                     blocks = [key_block(kvg, zz, yy, late, rows, b) for b in range(KV_LANES // WIDE)]
-                    sums = [None] * len(blocks)
-
-                    def put(b, v):
-                        sums[b] = v if sums[b] is None else sums[b] + v
-
+                    scores = group_scores(lambda b: blocks[b], qt, p, key_slot)
+                    dps = group_scores(lambda b: blocks[b], dot_, p, value_slot)
+                    es, dss = [], []
                     for g in groups:
-                        s = jnp.dot(blocks[key_slot(g)[0]], qt[g, p], preferred_element_type=f32)
+                        s = scores[g]
                         if masked:
                             s = jnp.where(seen, s, NEG)
                         e = jnp.exp(s - lse_ref[g, p])
-                        dp = jnp.dot(blocks[value_slot(g)[0]], dot_[g, p], preferred_element_type=f32)
-                        ds = (e * (dp - delta[g, p])).astype(b16)
-                        put(value_slot(g)[0], nt(e.astype(b16), dot_[g, p]))
-                        put(key_slot(g)[0], nt(ds, qt[g, p]))
+                        ds = (e * (dps[g] - delta[g, p])).astype(b16)
+                        es.append(e.astype(b16))
+                        dss.append(ds)
                         dq[g, p] += jnp.dot(kt[j, g], ds, preferred_element_type=f32)
-                    for b, v in enumerate(sums):
+                    sums = group_sums(es, dot_, p, value_slot)
+                    for b, v in group_sums(dss, qt, p, key_slot).items():
+                        sums[b] = sums[b] + v if b in sums else v
+                    for b, v in sums.items():
                         dkv[zz, yy, :, :, pl.ds(late, rows), WIDE * b : WIDE * b + WIDE] += v.reshape(
                             2, 2, rows, WIDE
                         )
@@ -1596,7 +1633,7 @@
             dx.start()
 
         stat = (HALF_GROUPS, 4, 1, PER * WIDE)
-        tile = (HALF_GROUPS, 4, WIDE, PER * WIDE)
+        tile = (4, WIDE, HALF_GROUPS * PER * WIDE)
         pl.run_scoped(
             attention_back,
             pltpu.VMEM(kvg_ref.shape, b16),
@@ -1721,6 +1758,17 @@
             pltpu.VMEM(gx1_ref.shape, f32),
             pltpu.VMEM(x_ref.shape, b16),
         )
+        width3 = 3 * WIDE
+        columns = []
+        for ref, n in ((outs[3], width), (outs[1], ff), (outs[2], ff)):
+            columns += [(ref, lo) for lo in range(0, n, width3)]
+        per = rest_w // width3
+        for i, (ref, lo) in enumerate(columns):
+            q, at = i // per * rb, i % per * width3
+            ref[ra:own_rows, lo : lo + width3] = rest_sum[q : q + rb, at : at + width3]
+        for q in range(16 // rb):
+            lo, hi = q * qkv_rest_w, min((q + 1) * qkv_rest_w, qkv_w)
+            outs[4][ra:own_rows, lo:hi] = qkv_rest_sum[rb * q : rb * (q + 1), : hi - lo]
         dx.sent()
         gx.sent()
         gq_share.sent()
@@ -1753,6 +1801,8 @@
         ]
         + Scatter.scratch(zn, tokens, KV_LANES)[:4]
         + [
+            pltpu.VMEM((16, rest_w), f32),
+            pltpu.VMEM((16, qkv_rest_w), f32),
             dma((n_items, Sum.SEMS)),
             dma((n_items, Sum.SEMS)),
             dma((n_in + 1,)),
@@ -1984,7 +2034,7 @@
     )
     gy_plain = cotangent.reshape(rows, width)
     left = lambda t: t.reshape(zn, 2, 2, 2, -1, rows)
-    r_down, r_gate, r_up, r_out, r_b2, r_qkv, r_b1, input_grad, gain_sums = scatter_attend(
+    d_down, d_gate, d_up, d_out, d_qkv, input_grad, gain_sums = scatter_attend(
         go_t,
         qh,
         kvg,
@@ -2004,12 +2054,6 @@
         first = lax.dynamic_slice(t, (device_at * ra,), (ra,))
         return jnp.concatenate([first, lax.dynamic_slice(t, (wa + device_at * rb,), (rb,))])
 
-    def own_rows(t):
-        return t.reshape(fold, rb, -1).transpose(1, 0, 2).reshape(rb, -1)
-
-    e1, e2 = own_rows(r_b1), own_rows(r_b2)
-    whole = lambda a, b: jnp.concatenate([a, b], axis=0)
-    d_qkv = whole(r_qkv, e1[:, :qkv_w])
     return (
         out.reshape(inputs.shape),
         input_grad.reshape(inputs.shape),
@@ -2017,11 +2061,11 @@
         d_qkv[:, 2 * hid :],
         jnp.concatenate([d_qkv[:, :half_hid], d_qkv[:, hid : hid + half_hid]], axis=1),
         jnp.concatenate([d_qkv[:, half_hid:hid], d_qkv[:, hid + half_hid : 2 * hid]], axis=1),
-        whole(r_out, e2[:, :width]),
+        d_out,
         own_gain(gain_sums[1]),
-        whole(r_gate, e2[:, width : width + ff]),
-        whole(r_up, e2[:, width + ff : width + 2 * ff]),
-        r_down,
+        d_gate,
+        d_up,
+        d_down,
     )
 
 

time: 382 us -> 377 us (0.987)
  other arithmetic: 10.4 us -> 4.51 us
  local copies, waits for them, and re-layouts: 7.07 us -> 12.1 us
  Pallas kernels: 359 us -> 354 us
    concatenate x5 -> x0, other arithmetic: 5.98 us -> none  [fast_device(): whole = lambda a, b: jnp.concatenate([a, b], axis=0)]
    unnamed x10 -> x13, local copies, waits for them, and re-layouts: 1.59 us -> 5.87 us
where the time goes in v7:
time: 377 us; the launch traced here: 372 us
  Pallas kernels  354 us (94%)
  local copies, waits for them, and re-layouts  12.1 us (3%)
  other arithmetic  4.51 us (1%)
    pallas_call x1, Pallas kernels, scatter_attend(): pl.pallas_call(kernel, out_shape=[jax.ShapeDtypeStruct(s, f32) for s in o...  169 us
    pallas_call x1, Pallas kernels, gather_attend(): pl.pallas_call(kernel, out_shape=[sds(x.shape, b16), sds(x.shape, b16), s...  156 us
    pallas_call x1, Pallas kernels, ffn(): pl.pallas_call(kernel, out_shape=[sds((rows, width), b16), sds((rows, wid...  29.7 us

profile of v7, /device:TPU:0, one launch (start us, length us, event | category | flops | bytes accessed | tf_op | source)
XLA Modules:
  0.0 371.7 jit_solution(13046016911962945913)
XLA Ops:
  0.7 0.7 fusion.5
  1.4 0.9 fusion.17
  2.3 1.0 concatenate.30.refs_3_
  3.3 0.0 copy-start
  3.3 0.6 reshape.99.refs_4_
  3.9 0.3 multiply_cosine_fusion
  4.3 0.2 maximum_bitcast_fusion.1
  4.5 0.7 pad_maximum_fusion.refs_2_.refs_5_
  5.2 0.0 copy-done
  5.2 155.7 %shard_map.194 = (bf16[256,1152]{1,0:T(8,128)(2,1)}, bf16[256,1152]{1,0:T(8,128)(2,1)}, bf16[1152,1152]{1,0:T(8,128)(2,1)}, bf16[2,1152,128]{2,1,0:T(8,128)(2,1)...) custom-call(bf16[256,1152]{1,0:T(8,128)(2,1)} %bitcast.43, ...), custom_call_target="tpu_custom_call" | custom-call | tf_op jit(solution)/shard_map/pallas_call | solution.py:1213
  160.9 29.7 %shard_map.195 = (bf16[256,1152]{1,0:T(8,128)(2,1)}, f32[256,1152]{1,0:T(8,128)}, bf16[256,1152]{1,0:T(8,128)(2,1)}, bf16[256,3072]{1,0:T(8,128)(2,1)}, bf16[256...) custom-call(bf16[2,1152,128]{2,1,0:T(8,128)(2,1)} %get-tuple-element, ...), custom_call_target="tpu_custom_call" | custom-call | tf_op jit(solution)/shard_map/pallas_call | solution.py:1922
  190.6 168.7 %shard_map.196 = (f32[96,1152]{1,0:T(8,128)}, f32[36,3072]{1,0:T(8,128)}, f32[36,3072]{1,0:T(8,128)}, f32[36,1152]{1,0:T(8,128)}, f32[36,1920]{1,0:T(8,128)}, /*...) custom-call(bf16[2,1152,128]{2,1,0:T(8,128)(2,1)} %get-tuple-element.60.refs_0_, ...), custom_call_target="tpu_custom_call" | custom-call | tf_op jit(solution)/shard_map/pallas_call | solution.py:1782
  359.2 0.0 copy-start.2
  359.2 0.0 copy-start.1
  359.2 0.0 copy-start.3
  359.2 0.9 fusion.16
  360.1 0.1 fusion.11
  360.2 0.1 fusion.10
  360.3 0.6 pad_maximum_fusion.5
  360.9 0.1 fusion.8
  361.0 0.1 fusion.9
  361.0 0.6 pad_maximum_fusion.4
  361.6 0.9 fusion.15
  362.6 1.6 slice.42
  364.2 0.7 pad_maximum_fusion.2
  364.9 0.7 pad_maximum_fusion.1
  365.6 1.9 copy.28
  367.5 1.6 copy.29
  369.1 0.0 copy-done.2
  369.1 0.8 copy.30
  369.9 0.0 copy-done.1
  369.9 0.8 copy.31
  370.7 0.0 copy-done.3
  370.7 0.8 copy.32
  (5 shorter events, 0.0 us)
Async XLA Ops:
  3.3 1.9 copy-start
  359.2 9.9 %copy-start.2 = (f32[36,3072]{1,0:T(8,128)S(1)}, f32[36,3072]{1,0:T(8,128)}, u32[]{:S(2)}) copy-start(f32[36,3072]{1,0:T(8,128)} %get-tuple-element.124) | copy-start | bytes 1327108
  359.2 10.7 %copy-start.1 = (f32[36,3072]{1,0:T(8,128)S(1)}, f32[36,3072]{1,0:T(8,128)}, u32[]{:S(2)}) copy-start(f32[36,3072]{1,0:T(8,128)} %get-tuple-element.125) | copy-start | bytes 1327108
  359.2 11.4 %copy-start.3 = (f32[96,1152]{1,0:T(8,128)S(1)}, f32[96,1152]{1,0:T(8,128)}, u32[]{:S(2)}) copy-start(f32[96,1152]{1,0:T(8,128)} %get-tuple-element.126) | copy-start | bytes 1327108

commit v8 on v7

--- a/solution.py
+++ b/solution.py
@@ -1841,9 +1841,11 @@
                 [(order_hbm, order_s), (rest_hbm, rest_s), (out_hbm, out_s), (gate_hbm, gate_s), (up_hbm, up_s), (down_hbm, down_s)]
             )
         ]
-        for c in loads:
+        for c in loads[:3]:
             c.start()
         loads[0].wait()
+        for c in loads[3:]:
+            c.start()
         for mb in range(mbs):
             at = slice(mb * tokens, (mb + 1) * tokens)
             t = jnp.dot(order_s[...], o_ref[mb], preferred_element_type=f32)

time: 377 us -> 377 us (level)
  no operation moved by 1% of the time
where the time goes in v8:
time: 377 us; the launch traced here: 372 us
  Pallas kernels  354 us (94%)
  local copies, waits for them, and re-layouts  12.1 us (3%)
  other arithmetic  4.51 us (1%)
    pallas_call x1, Pallas kernels, scatter_attend(): pl.pallas_call(kernel, out_shape=[jax.ShapeDtypeStruct(s, f32) for s in o...  169 us
    pallas_call x1, Pallas kernels, gather_attend(): pl.pallas_call(kernel, out_shape=[sds(x.shape, b16), sds(x.shape, b16), s...  156 us
    pallas_call x1, Pallas kernels, ffn(): pl.pallas_call(kernel, out_shape=[sds((rows, width), b16), sds((rows, wid...  29.9 us

profile of v8, /device:TPU:0, one launch (start us, length us, event | category | flops | bytes accessed | tf_op | source)
XLA Modules:
  0.0 371.9 jit_solution(1332356167822270352)
XLA Ops:
  0.7 0.7 fusion.5
  1.4 0.9 fusion.17
  2.3 1.0 concatenate.30.refs_3_
  3.3 0.0 copy-start
  3.3 0.6 reshape.99.refs_4_
  3.9 0.3 multiply_cosine_fusion
  4.3 0.2 maximum_bitcast_fusion.1
  4.5 0.7 pad_maximum_fusion.refs_2_.refs_5_
  5.2 0.0 copy-done
  5.2 155.7 %shard_map.194 = (bf16[256,1152]{1,0:T(8,128)(2,1)}, bf16[256,1152]{1,0:T(8,128)(2,1)}, bf16[1152,1152]{1,0:T(8,128)(2,1)}, bf16[2,1152,128]{2,1,0:T(8,128)(2,1)...) custom-call(bf16[256,1152]{1,0:T(8,128)(2,1)} %bitcast.43, ...), custom_call_target="tpu_custom_call" | custom-call | tf_op jit(solution)/shard_map/pallas_call | solution.py:1213
  160.9 29.9 %shard_map.195 = (bf16[256,1152]{1,0:T(8,128)(2,1)}, f32[256,1152]{1,0:T(8,128)}, bf16[256,1152]{1,0:T(8,128)(2,1)}, bf16[256,3072]{1,0:T(8,128)(2,1)}, bf16[256...) custom-call(bf16[2,1152,128]{2,1,0:T(8,128)(2,1)} %get-tuple-element, ...), custom_call_target="tpu_custom_call" | custom-call | tf_op jit(solution)/shard_map/pallas_call | solution.py:1924
  190.8 168.6 %shard_map.196 = (f32[96,1152]{1,0:T(8,128)}, f32[36,3072]{1,0:T(8,128)}, f32[36,3072]{1,0:T(8,128)}, f32[36,1152]{1,0:T(8,128)}, f32[36,1920]{1,0:T(8,128)}, /*...) custom-call(bf16[2,1152,128]{2,1,0:T(8,128)(2,1)} %get-tuple-element.60.refs_0_, ...), custom_call_target="tpu_custom_call" | custom-call | tf_op jit(solution)/shard_map/pallas_call | solution.py:1782
  359.4 0.0 copy-start.2
  359.4 0.0 copy-start.1
  359.4 0.0 copy-start.3
  359.5 0.9 fusion.16
  360.4 0.1 fusion.11
  360.4 0.1 fusion.10
  360.5 0.6 pad_maximum_fusion.5
  361.1 0.1 fusion.8
  361.2 0.1 fusion.9
  361.2 0.6 pad_maximum_fusion.4
  361.8 0.9 fusion.15
  362.8 1.6 slice.42
  364.4 0.7 pad_maximum_fusion.2
  365.1 0.7 pad_maximum_fusion.1
  365.8 1.9 copy.28
  367.7 1.6 copy.29
  369.3 0.0 copy-done.2
  369.3 0.8 copy.30
  370.1 0.0 copy-done.1
  370.1 0.8 copy.31
  370.9 0.0 copy-done.3
  370.9 0.8 copy.32
  (5 shorter events, 0.0 us)
Async XLA Ops:
  3.3 1.9 copy-start
  359.4 9.9 %copy-start.2 = (f32[36,3072]{1,0:T(8,128)S(1)}, f32[36,3072]{1,0:T(8,128)}, u32[]{:S(2)}) copy-start(f32[36,3072]{1,0:T(8,128)} %get-tuple-element.124) | copy-start | bytes 1327108
  359.4 10.7 %copy-start.1 = (f32[36,3072]{1,0:T(8,128)S(1)}, f32[36,3072]{1,0:T(8,128)}, u32[]{:S(2)}) copy-start(f32[36,3072]{1,0:T(8,128)} %get-tuple-element.125) | copy-start | bytes 1327108
  359.4 11.4 %copy-start.3 = (f32[96,1152]{1,0:T(8,128)S(1)}, f32[96,1152]{1,0:T(8,128)}, u32[]{:S(2)}) copy-start(f32[96,1152]{1,0:T(8,128)} %get-tuple-element.126) | copy-start | bytes 1327108
